TPU v7x, 128 devices: a whole 4x4x4 slice. The times are simulated.
128 devices in a mesh: cp: 32 (over z, y_hi, x), tp: 4 (over y_lo, core).
Axes of the slice: x: 4, y: 4 (y_hi: 2, y_lo: 2; y = y_hi * 2 + y_lo), z: 4, core: 2. Of those that a mesh axis runs over, the one named last changes fastest.
Arguments:
- queries: bfloat16 [256, 128, 128], P('cp', 'tp'), may hold values from -32 to 32
- keys: bfloat16 [65536, 8, 128], P('cp', 'tp'), may hold values from -24 to 24
- values: bfloat16 [65536, 8, 128], P('cp', 'tp'), may hold values from -12 to 12
- lengths: int32 [32], P('cp'), may hold values from 1024 to 2048
- start: int32 [1], replicated, may hold values from 32512 to 65280
- out_weight: bfloat16 [16384, 16384], P('tp', 'cp'), may hold values from -0.046875 to 0.046875
Outputs:
- projected: bfloat16 [256, 16384], P('tp', 'cp')
All inputs are finite; a program needn't handle non-finite values.
Results may differ from a plain program's by a relative error of at most 0.0065.
Values may be sent and summed in bfloat16 or wider, within the bound.
No kernel may reach another device: no remote copies, remote signals or barrier semaphores. Data moves between devices by JAX's collectives and lax.ppermute only.
A program may use at most 64 MiB of HBM per device.

v0:
```python
import functools
import itertools
import math

import jax
import jax.numpy as jnp
from jax import lax
from jax.experimental import pallas as pl
from jax.experimental.pallas import tpu as pltpu
from jax.sharding import PartitionSpec as P

NEG = -1e30
BIG = 2.0**100
RING = 4
MIB = 2**20


def coords(cp, tp):
    z, yh, x = cp // 8, (cp // 4) % 2, cp % 4
    yl, core = tp // 2, tp % 2
    return z, yh, x, yl, core


def moved(x, a=0, b=0, yh=0, yl=0, core=0):
    pairs = []
    for cp, tp in itertools.product(range(32), range(4)):
        zi, yhi, xi, yli, ci = coords(cp, tp)
        dz, dx = (a, b) if ci == 0 else (b, a)
        zo, xo = (zi + dz) % RING, (xi + dx) % RING
        yho, ylo, co = yhi ^ yh, yli ^ yl, ci ^ core
        pairs.append((cp * 4 + tp, ((zo * 2 + yho) * 4 + xo) * 4 + ylo * 2 + co))
    return lax.ppermute(x, ("cp", "tp"), pairs)


def together(*arrays):
    return lax.optimization_barrier(arrays)


def source(me, da, db, dy):
    z, yh, x, _, core = me
    dz = jnp.where(core == 0, da, db)
    dx = jnp.where(core == 0, db, da)
    return (z - dz) & (RING - 1), yh ^ dy, (x - dx) & (RING - 1)


def spread(row, eye):
    return jnp.sum(jnp.where(eye, row, 0.0), axis=1, keepdims=True)


def gathered_row(column, eye):
    return jnp.sum(jnp.where(eye, column, 0.0), axis=0, keepdims=True)


def diagonal():
    shape = (128, 128)
    return lax.broadcasted_iota(jnp.int32, shape, 0) == lax.broadcasted_iota(jnp.int32, shape, 1)


def stat_rows(m, l):
    high = l.astype(jnp.bfloat16).astype(jnp.float32)
    return jnp.concatenate([m, high, l - high, jnp.zeros((5, 128), jnp.float32)], axis=0)


def prepare_kernel(info, k_ref, v_ref, vx, *masked):
    nkv, span = k_ref.shape[:2]
    me = tuple(info[i] for i in range(5))
    length, start = info[5], info[6]
    shard = (me[0] * 2 + me[1]) * 4 + me[2]
    lane = lax.broadcasted_iota(jnp.int32, (1, 128), 1)
    slot = lax.broadcasted_iota(jnp.int32, (span, 128), 0)
    for db, kx in enumerate(masked):
        z, yh, x = source(me, lane >> 4, db, (lane >> 3) & 1)
        seen = start + z * 64 + yh * 32 + x * 8 + (lane & 7) + 1 - shard * span
        seen = jnp.minimum(seen, length)
        mask = jnp.where((slot >= seen) & (lane < 64), NEG, 0.0).astype(jnp.bfloat16)
        for kv in range(nkv):
            kx[kv, :, :128] = k_ref[kv]
            kx[kv, :, 128:] = mask
    for kv in range(nkv):
        vx[kv, :, :128] = v_ref[kv]
        vx[kv, :, 128:] = jnp.ones((span, 128), jnp.bfloat16)


def prepare(info, k, v):
    vmem = pl.BlockSpec(memory_space=pltpu.VMEM)
    count = 1 + RING
    return pl.pallas_call(
        prepare_kernel,
        in_specs=[pl.BlockSpec(memory_space=pltpu.SMEM), vmem, vmem],
        out_specs=[vmem] * count,
        out_shape=[jax.ShapeDtypeStruct((*k.shape[:2], 256), jnp.bfloat16)] * count,
        compiler_params=pltpu.CompilerParams(vmem_limit_bytes=4 * MIB),
        name="prepare",
    )(info, k, v)


def attend_kernel(q_ref, kx, vx, o_ref, *, kvs, first, nb, tile, scale):
    step = pl.program_id(0)
    span = vx.shape[1]
    eye = diagonal()

    def rows_of(b, count):
        row = lax.broadcasted_iota(jnp.int32, (count * 128, 128), 0)
        lane = lax.broadcasted_iota(jnp.int32, (count * 128, 128), 1)
        token = (first + step * nb + b + (row >> 7)) * 8 + ((row >> 4) & 7)
        hot = jnp.where(lane == token, 1.0, 0.0).astype(jnp.bfloat16)
        heads = [q_ref[pl.ds(b, count), :, kv * 16 : (kv + 1) * 16, :].reshape(count * 128, 128) for kv in kvs]
        return [jnp.concatenate([h, hot], axis=1) for h in heads]

    def scores(q, kv, t):
        return lax.dot_general(
            q, kx[kv, pl.ds(t, tile), :], (((1,), (1,)), ((), ())), preferred_element_type=jnp.float32
        )

    def point(m):
        return jnp.maximum(m * scale, 0.01 * NEG).astype(jnp.bfloat16).astype(jnp.float32)

    def put(b, r, results):
        stats = []
        for i, (m, acc) in enumerate(results):
            o_ref[b, i * 128 : (i + 1) * 128, :] = acc[r, :128].astype(jnp.bfloat16)
            stats.append(stat_rows(gathered_row(m[r], eye), gathered_row(acc[r, 128:], eye)))
        o_ref[b, len(results) * 128 :, :] = jnp.concatenate(stats, axis=0).astype(jnp.bfloat16)

    ok, results = [], []
    for q, kv in zip(rows_of(0, nb), kvs):
        s0 = scores(q, kv, 0)
        m = point(jnp.max(s0, axis=1, keepdims=True))
        p = []
        for t in range(0, span, tile):
            s = s0 if t == 0 else scores(q, kv, t)
            p.append(jnp.exp2(s * scale - m).astype(jnp.bfloat16))
        acc = jnp.dot(jnp.concatenate(p, axis=1), vx[kv], preferred_element_type=jnp.float32)
        ok.append(jnp.min(jnp.where(acc[:, 128:] < BIG, 1.0, 0.0)))
        results.append((m, acc))
    for b in range(nb):
        put(b, slice(b * 128, (b + 1) * 128), results)

    @pl.when(functools.reduce(jnp.minimum, ok) < 0.5)
    def _():
        def block(b, _):
            results = []
            for q, kv in zip(rows_of(b, 1), kvs):

                def top(n, m):
                    s = scores(q, kv, pl.multiple_of(n * tile, tile))
                    return jnp.maximum(m, jnp.max(s, axis=1, keepdims=True))

                m = point(lax.fori_loop(0, span // tile, top, jnp.full((128, 1), NEG, jnp.float32)))

                def add(n, acc):
                    t = pl.multiple_of(n * tile, tile)
                    p = jnp.exp2(scores(q, kv, t) * scale - m).astype(jnp.bfloat16)
                    return acc + jnp.dot(p, vx[kv, pl.ds(t, tile), :], preferred_element_type=jnp.float32)

                results.append((m, lax.fori_loop(0, span // tile, add, jnp.zeros((128, 256), jnp.float32))))
            put(b, slice(0, 128), results)
            return 0

        lax.fori_loop(0, nb, block, 0)


def attend(q, kx, vx, kvs, first=0, blocks=8):
    span = vx.shape[1]
    nb, tile = 8 // len(kvs), 256
    skip = first // nb
    vmem = pl.BlockSpec(memory_space=pltpu.VMEM)
    return pl.pallas_call(
        functools.partial(
            attend_kernel, kvs=kvs, first=first, nb=nb, tile=tile, scale=math.log2(math.e) / math.sqrt(128)
        ),
        grid=(blocks // nb,),
        in_specs=[pl.BlockSpec((nb, *q.shape[1:]), lambda i: (skip + i, 0, 0, 0)), vmem, vmem],
        out_specs=pl.BlockSpec((nb, len(kvs) * 136, 128), lambda i: (i, 0, 0)),
        out_shape=jax.ShapeDtypeStruct((blocks, len(kvs) * 136, 128), jnp.bfloat16),
        compiler_params=pltpu.CompilerParams(vmem_limit_bytes=20 * MIB, dimension_semantics=("arbitrary",)),
        cost_estimate=pl.CostEstimate(
            flops=8 * blocks * len(kvs) * 128 * span * 128,
            bytes_accessed=4 * MIB,
            transcendentals=blocks * len(kvs) * 128 * span,
        ),
        name="attend_plane",
    )(q, kx, vx)


def merged(parts, kv, nkv, eye):
    stats = [p[nkv * 128 :, :].astype(jnp.float32)[kv * 8 : kv * 8 + 8] for p in parts]
    m = functools.reduce(jnp.maximum, [s[0:1] for s in stats])
    total = jnp.zeros((1, 128), jnp.float32)
    out = jnp.zeros((128, 128), jnp.float32)
    for p, s in zip(parts, stats):
        factor = jnp.exp2(s[0:1] - m)
        total = total + factor * (s[1:2] + s[2:3])
        out = out + spread(factor, eye) * p[kv * 128 : (kv + 1) * 128, :].astype(jnp.float32)
    return out, m, total


def combine_kernel(*refs, pieces):
    o_ref = refs[-1]
    blocks, nkv = o_ref.shape[0], o_ref.shape[1] // 136
    eye = diagonal()
    for b in range(blocks):
        parts, at = [], 0
        for count in pieces:
            share = blocks // count
            parts.append(refs[at + b // share].at[b % share])
            at += count
        stats = []
        for kv in range(nkv):
            out, m, total = merged(parts, kv, nkv, eye)
            o_ref[b, kv * 128 : (kv + 1) * 128, :] = out.astype(jnp.bfloat16)
            stats.append(stat_rows(m, total))
        o_ref[b, nkv * 128 :, :] = jnp.concatenate(stats, axis=0).astype(jnp.bfloat16)


def combine(parts):
    vmem = pl.BlockSpec(memory_space=pltpu.VMEM)
    flat = [piece for part in parts for piece in part]
    blocks = sum(piece.shape[0] for piece in parts[0])
    return pl.pallas_call(
        functools.partial(combine_kernel, pieces=[len(part) for part in parts]),
        in_specs=[vmem] * len(flat),
        out_specs=vmem,
        out_shape=jax.ShapeDtypeStruct((blocks, *flat[0].shape[1:]), jnp.bfloat16),
        compiler_params=pltpu.CompilerParams(vmem_limit_bytes=8 * MIB),
        name="combine",
    )(*flat)


def finish_kernel(mine, theirs, o_ref, rows):
    eye = diagonal()
    nkv = mine.shape[1] // 136
    for kv in range(nkv):
        for dy in range(2):
            out, _, total = merged([mine.at[dy], theirs.at[1 - dy]], kv, nkv, eye)
            rows[kv, dy] = out * spread(1.0 / total, eye)
    for kv, h in itertools.product(range(nkv), range(16)):
        c = (kv * 16 + h) * 128
        both = [rows[kv, dy, pl.ds(h, 8, stride=16), :] for dy in range(2)]
        o_ref[:, c : c + 128] = jnp.concatenate(both, axis=0).astype(jnp.bfloat16)


def finish(mine, theirs):
    vmem = pl.BlockSpec(memory_space=pltpu.VMEM)
    nkv = mine.shape[1] // 136
    return pl.pallas_call(
        finish_kernel,
        in_specs=[vmem, vmem],
        out_specs=vmem,
        scratch_shapes=[pltpu.VMEM((nkv, 2, 128, 128), jnp.float32)],
        compiler_params=pltpu.CompilerParams(vmem_limit_bytes=4 * MIB),
        out_shape=jax.ShapeDtypeStruct((16, nkv * 2048), jnp.bfloat16),
        name="finish",
    )(mine, theirs)


def assemble_kernel(x0, x1, x2, x3, _, o_ref):
    for i, x in enumerate((x0, x1, x2, x3)):
        o_ref[i * x.shape[0] : (i + 1) * x.shape[0], :] = x[...]


def assemble(*pieces):
    vmem = pl.BlockSpec(memory_space=pltpu.VMEM)
    rows, width = pieces[0].shape
    return pl.pallas_call(
        assemble_kernel,
        in_specs=[vmem] * 4 + [pl.BlockSpec(memory_space=pl.ANY)],
        out_specs=vmem,
        out_shape=jax.ShapeDtypeStruct((RING * rows, width), pieces[0].dtype),
        compiler_params=pltpu.CompilerParams(vmem_limit_bytes=4 * MIB),
        name="assemble",
    )(*pieces)


def project_kernel(x_ref, w_ref, o_ref):
    o_ref[...] = jnp.dot(x_ref[...], w_ref[...], preferred_element_type=jnp.float32)


def project(x, w):
    vmem = pl.BlockSpec(memory_space=pltpu.VMEM)
    return pl.pallas_call(
        project_kernel,
        in_specs=[vmem, vmem],
        out_specs=vmem,
        out_shape=jax.ShapeDtypeStruct((x.shape[0], w.shape[1]), jnp.float32),
        compiler_params=pltpu.CompilerParams(vmem_limit_bytes=8 * MIB),
        cost_estimate=pl.CostEstimate(
            flops=8 * x.shape[0] * w.shape[0] * w.shape[1], bytes_accessed=4 * MIB, transcendentals=0
        ),
        name="project",
    )(x, w)


def place_kernel(info, y0, y1, y3, x_ref, w_ref, o_ref):
    me = tuple(info[i] for i in range(5))
    yl, core = me[3], me[4]
    y2 = jnp.dot(x_ref[...], w_ref[...], preferred_element_type=jnp.float32)
    for db, y in ((0, y0), (1, y1), (2, y2), (3, y3)):
        for da, dy in itertools.product(range(RING), range(2)):
            z, yh, xx = source(me, da, db, dy)
            row = (((z & 1) ^ core) * 2 + ((z >> 1) ^ yl)) * 64 + yh * 32 + xx * 8
            at = da * 16 + dy * 8
            o_ref[pl.ds(pl.multiple_of(row, 8), 8), :] = y[at : at + 8, :]


def place(info, y0, y1, y3, x, w):
    vmem = pl.BlockSpec(memory_space=pltpu.VMEM)
    return pl.pallas_call(
        place_kernel,
        in_specs=[pl.BlockSpec(memory_space=pltpu.SMEM)] + [vmem] * 5,
        out_specs=vmem,
        out_shape=jax.ShapeDtypeStruct((RING * y0.shape[0], w.shape[1]), jnp.float32),
        compiler_params=pltpu.CompilerParams(vmem_limit_bytes=8 * MIB),
        name="place",
    )(info, y0, y1, y3, x, w)


def on_device(queries, keys, values, lengths, start, out_weight):
    nkv = keys.shape[1]
    me = coords(lax.axis_index("cp"), lax.axis_index("tp"))
    info = jnp.concatenate([jnp.stack(me).astype(jnp.int32), lengths, start])
    k = keys.transpose(1, 0, 2)
    v = values.transpose(1, 0, 2)
    q = queries[None]
    q = jnp.concatenate([q, moved(q, yh=1)], axis=0)
    q, k, v, info = together(q, k, v, info)
    vx, kx0, kx1, kx2, kx3 = prepare(info, k, v)
    q2, q1, q3 = (moved(q, a=d) for d in (2, 1, 3))
    q = jnp.concatenate([q, q1, q2, q3], axis=0)
    q, vx, kx0, kx1, kx2, kx3 = together(q, vx, kx0, kx1, kx2, kx3)

    q1, q2, q3 = (moved(q, b=d) for d in (1, 2, 3))

    kvs = tuple(range(nkv))
    own0 = attend(q, kx0, vx, kvs, 0, 4)
    q1, own0 = together(q1, own0)
    p1 = attend(q1, kx1, vx, kvs)
    r1 = moved(p1, b=-1)
    q2, q3, p1 = together(q2, q3, p1)
    p2 = attend(q2, kx2, vx, kvs)
    r2 = moved(p2, b=-2)
    q3, p2, r1 = together(q3, p2, r1)
    p3a = attend(q3, kx3, vx, kvs, 0, 4)
    r3a = moved(p3a, b=-3)
    q3, p3a = together(q3, p3a)
    p3b = attend(q3, kx3, vx, kvs, 4, 4)
    r3b = moved(p3b, b=-3)
    q, p3b, r2, r3a = together(q, p3b, r2, r3a)
    own1 = attend(q, kx0, vx, kvs, 4, 4)
    c = combine([[own0, own1], [r1], [r2], [r3a, r3b]])
    c = combine([[c[:2]]] + [[moved(c[2 * d : 2 * d + 2], a=-d)] for d in (2, 1, 3)])
    attn = finish(c, moved(c, yh=1))
    x2, x1, x3 = (moved(attn, a=d) for d in (2, 1, 3))
    attn = assemble(attn, x1, x2, x3, moved(x2, core=1))
    x1, x3, x2 = (moved(attn, b=d) for d in (1, 3, 2))
    y = place(info, project(attn, out_weight), project(x1, out_weight), project(x3, out_weight), x2, out_weight)
    y = y[:128] + moved(y[128:], core=1)
    y = y[:64] + moved(y[64:].astype(jnp.bfloat16), yl=1).astype(jnp.float32)
    return y.astype(jnp.bfloat16)


def solution(mesh):
    in_specs = (
        P("cp", "tp", None),
        P("cp", "tp", None),
        P("cp", "tp", None),
        P("cp"),
        P(),
        P("tp", "cp"),
    )
    return jax.shard_map(on_device, mesh=mesh, in_specs=in_specs, out_specs=P("tp", "cp"), check_vma=False)
```

profile of v0, /device:TPU:0, one launch (start us, length us, event | category | flops | bytes accessed | tf_op | source)
XLA Modules:
  0.0 110.1 jit_solution(4272141776012754842)
XLA Ops:
  0.0 3.3 %collective-permute-start = (bf16[1,8,32,128]{3,2,1,0:T(8,128)(2,1)}, bf16[1,8,32,128]{3,2,1,0:T(8,128)(2,1)S(1)}, u32[]{:S(2)}, u32[]{:S(2)}) collective-permute-start(bf16[1,8,32,128]{3,2,1,0:T(8,128)(2,1)} %bitcast.10), channel_id=1, source_target_pairs={{0,16},{1,17},{2,18},{3,19},{4,20},{5,21},{6,22},{7,23},{8,24},{9,... | collective-permute-start | bytes 196616 | tf_op jit(solution)/shard_map/ppermute | solution.py:32
  3.3 1.8 %copy_bitcast_fusion = (bf16[2,2048,128]{2,1,0:T(8,128)(2,1)S(1)}, bf16[2,2048,128]{2,1,0:T(8,128)(2,1)S(1)}) fusion(bf16[2048,2,128]{2,1,0:T(2,128)(2,1)} %param.8, bf16[2048,2,128]{2,1,0:T(2,128)(2,1)} %param.7), kind=kLoop, calls=%fused_computation | loop fusion | bytes 4194304 | tf_op jit(solution)/shard_map/transpose | solution.py:323
  6.6 2.0 %collective-permute-start.1 = (bf16[2,8,32,128]{3,2,1,0:T(8,128)(2,1)S(1)}, bf16[2,8,32,128]{3,2,1,0:T(8,128)(2,1)S(1)}, u32[]{:S(2)}, u32[]{:S(2)}) collective-permute-start(bf16[2,8,32,128]{3,2,1,0:T(8,128)(2,1)S(1)} %pad_maximum_fusion.1), channel_id=1, source_target_pairs={{0,32},{1,5},{2,34},{3,7},{4,36},{5,9},{6,38},{7,11},{8,40},{9,13}... | collective-permute-start | bytes 393224 | tf_op jit(solution)/shard_map/ppermute | solution.py:32
  8.5 3.6 %collective-permute-start.2 = (bf16[2,8,32,128]{3,2,1,0:T(8,128)(2,1)S(1)}, bf16[2,8,32,128]{3,2,1,0:T(8,128)(2,1)S(1)}, u32[]{:S(2)}, u32[]{:S(2)}) collective-permute-start(bf16[2,8,32,128]{3,2,1,0:T(8,128)(2,1)S(1)} %pad_maximum_fusion.1), channel_id=1, source_target_pairs={{0,64},{1,9},{2,66},{3,11},{4,68},{5,13},{6,70},{7,15},{8,72},{9,1... | collective-permute-start | bytes 393224 | tf_op jit(solution)/shard_map/ppermute | solution.py:32
  13.1 2.2 %prepare.1 = (bf16[2,2048,256]{2,1,0:T(8,128)(2,1)S(1)}, bf16[2,2048,256]{2,1,0:T(8,128)(2,1)S(1)}, bf16[2,2048,256]{2,1,0:T(8,128)(2,1)S(1)}, bf16[2,2048,256]{...) custom-call(s32[7]{0:T(128)S(1)} %concatenate.10.info, bf16[2,2048,128]{2,1,0:T(8,128)(2,1)S(1)} %get-tuple-element.32.k_ref, ...), custom_call_target="tpu_custom_call" | custom-call | tf_op jit(solution)/shard_map/prepare/pallas_call | solution.py:87
  17.2 1.6 %collective-permute-start.4 = (bf16[8,8,32,128]{3,2,1,0:T(8,128)(2,1)S(1)}, bf16[8,8,32,128]{3,2,1,0:T(8,128)(2,1)S(1)}, u32[]{:S(2)}, u32[]{:S(2)}) collective-permute-start(bf16[8,8,32,128]{3,2,1,0:T(8,128)(2,1)S(1)} %pad_maximum_fusion.q_ref), channel_id=1, source_target_pairs={{0,4},{1,33},{2,6},{3,35},{4,8},{5,37},{6,10},{7,39},{8,12},{9,41}... | collective-permute-start | bytes 1572872 | tf_op jit(solution)/shard_map/ppermute | solution.py:32
  18.7 2.7 %collective-permute-start.5 = (bf16[8,8,32,128]{3,2,1,0:T(8,128)(2,1)S(1)}, bf16[8,8,32,128]{3,2,1,0:T(8,128)(2,1)S(1)}, u32[]{:S(2)}, u32[]{:S(2)}) collective-permute-start(bf16[8,8,32,128]{3,2,1,0:T(8,128)(2,1)S(1)} %pad_maximum_fusion.q_ref), channel_id=1, source_target_pairs={{0,8},{1,65},{2,10},{3,67},{4,12},{5,69},{6,14},{7,71},{8,0},{9,73... | collective-permute-start | bytes 1572872 | tf_op jit(solution)/shard_map/ppermute | solution.py:32
  21.5 1.4 %collective-permute-start.6 = (bf16[8,8,32,128]{3,2,1,0:T(8,128)(2,1)S(1)}, bf16[8,8,32,128]{3,2,1,0:T(8,128)(2,1)S(1)}, u32[]{:S(2)}, u32[]{:S(2)}) collective-permute-start(bf16[8,8,32,128]{3,2,1,0:T(8,128)(2,1)S(1)} %pad_maximum_fusion.q_ref), channel_id=1, source_target_pairs={{0,12},{1,97},{2,14},{3,99},{4,0},{5,101},{6,2},{7,103},{8,4},{9,1... | collective-permute-start | bytes 1572872 | tf_op jit(solution)/shard_map/ppermute | solution.py:32
  22.9 2.8 %attend_plane.6.refs_0_ = bf16[4,272,128]{2,1,0:T(8,128)(2,1)S(1)} custom-call(bf16[8,8,32,128]{3,2,1,0:T(8,128)(2,1)S(1)} %pad_maximum_fusion.q_ref, bf16[2,2048,256]{2,1,0:T(8,128)(2,1)S(1)} %get-tuple-element.40.kx, bf16[2,2048,256]{2,1,0:T(8,128)(2,1)S(1)} %get-tuple-element.41.vx), custom_call_target="tpu_custom_call" | custom-call | flops 2147483648 | bytes 4194304 | tf_op jit(solution)/shard_map/attend_plane/pallas_call | solution.py:168
  25.7 2.0 %collective-permute-done.4.q_ref = bf16[8,8,32,128]{3,2,1,0:T(8,128)(2,1)S(1)} collective-permute-done((bf16[8,8,32,128]{3,2,1,0:T(8,128)(2,1)S(1)}, bf16[8,8,32,128]{3,2,1,0:T(8,128)(2,1)S(1)}, u32[]{:S(2)}, u32[]{:S(2)}) %collective-permute-start.4) | collective-permute-done | bytes 524320 | tf_op jit(solution)/shard_map/ppermute | solution.py:32
  27.6 5.5 %attend_plane.7 = bf16[8,272,128]{2,1,0:T(8,128)(2,1)S(1)} custom-call(bf16[8,8,32,128]{3,2,1,0:T(8,128)(2,1)S(1)} %collective-permute-done.4.q_ref, bf16[2,2048,256]{2,1,0:T(8,128)(2,1)S(1)} %get-tuple-element.44.kx, bf16[2,2048,256]{2,1,0:T(8,128)(2,1)S(1)} %get-tuple-element.41.vx), custom_call_target="tpu_custom_call" | custom-call | flops 4294967296 | bytes 4194304 | tf_op jit(solution)/shard_map/attend_plane/pallas_call | solution.py:168
  33.2 1.8 %collective-permute-start.7 = (bf16[8,272,128]{2,1,0:T(8,128)(2,1)S(1)}, bf16[8,272,128]{2,1,0:T(8,128)(2,1)S(1)}, u32[]{:S(2)}, u32[]{:S(2)}) collective-permute-start(bf16[8,272,128]{2,1,0:T(8,128)(2,1)S(1)} %attend_plane.7), channel_id=1, source_target_pairs={{0,12},{1,97},{2,14},{3,99},{4,0},{5,101},{6,2},{7,103},{8,4},{9,1... | collective-permute-start | bytes 1671176 | tf_op jit(solution)/shard_map/ppermute | solution.py:32
  35.0 5.5 %attend_plane.8 = bf16[8,272,128]{2,1,0:T(8,128)(2,1)S(1)} custom-call(bf16[8,8,32,128]{3,2,1,0:T(8,128)(2,1)S(1)} %collective-permute-done.5.q_ref, bf16[2,2048,256]{2,1,0:T(8,128)(2,1)S(1)} %get-tuple-element.47.kx, bf16[2,2048,256]{2,1,0:T(8,128)(2,1)S(1)} %get-tuple-element.41.vx), custom_call_target="tpu_custom_call" | custom-call | flops 4294967296 | bytes 4194304 | tf_op jit(solution)/shard_map/attend_plane/pallas_call | solution.py:168
  40.5 2.3 %collective-permute-start.8 = (bf16[8,272,128]{2,1,0:T(8,128)(2,1)S(1)}, bf16[8,272,128]{2,1,0:T(8,128)(2,1)S(1)}, u32[]{:S(2)}, u32[]{:S(2)}) collective-permute-start(bf16[8,272,128]{2,1,0:T(8,128)(2,1)S(1)} %attend_plane.8), channel_id=1, source_target_pairs={{0,8},{1,65},{2,10},{3,67},{4,12},{5,69},{6,14},{7,71},{8,0},{9,73... | collective-permute-start | bytes 1671176 | tf_op jit(solution)/shard_map/ppermute | solution.py:32
  43.0 2.8 %attend_plane.9 = bf16[4,272,128]{2,1,0:T(8,128)(2,1)S(1)} custom-call(bf16[8,8,32,128]{3,2,1,0:T(8,128)(2,1)S(1)} %collective-permute-done.6.q_ref, bf16[2,2048,256]{2,1,0:T(8,128)(2,1)S(1)} %get-tuple-element.49.kx, bf16[2,2048,256]{2,1,0:T(8,128)(2,1)S(1)} %get-tuple-element.41.vx), custom_call_target="tpu_custom_call" | custom-call | flops 2147483648 | bytes 4194304 | tf_op jit(solution)/shard_map/attend_plane/pallas_call | solution.py:168
  46.1 2.8 %attend_plane.10 = bf16[4,272,128]{2,1,0:T(8,128)(2,1)S(1)} custom-call(bf16[8,8,32,128]{3,2,1,0:T(8,128)(2,1)S(1)} %collective-permute-done.6.q_ref, bf16[2,2048,256]{2,1,0:T(8,128)(2,1)S(1)} %get-tuple-element.49.kx, bf16[2,2048,256]{2,1,0:T(8,128)(2,1)S(1)} %get-tuple-element.41.vx), custom_call_target="tpu_custom_call" | custom-call | flops 2147483648 | bytes 4194304 | tf_op jit(solution)/shard_map/attend_plane/pallas_call | solution.py:168
  48.9 1.8 %collective-permute-start.10 = (bf16[4,272,128]{2,1,0:T(8,128)(2,1)S(1)}, bf16[4,272,128]{2,1,0:T(8,128)(2,1)S(1)}, u32[]{:S(2)}, u32[]{:S(2)}) collective-permute-start(bf16[4,272,128]{2,1,0:T(8,128)(2,1)S(1)} %attend_plane.10), channel_id=1, source_target_pairs={{0,4},{1,33},{2,6},{3,35},{4,8},{5,37},{6,10},{7,39},{8,12},{9,41}... | collective-permute-start | bytes 835592 | tf_op jit(solution)/shard_map/ppermute | solution.py:32
  51.8 2.9 %collective-permute-done.9.refs_4_ = bf16[4,272,128]{2,1,0:T(8,128)(2,1)S(1)} collective-permute-done((bf16[4,272,128]{2,1,0:T(8,128)(2,1)S(1)}, bf16[4,272,128]{2,1,0:T(8,128)(2,1)S(1)}, u32[]{:S(2)}, u32[]{:S(2)}) %collective-permute-start.9) | collective-permute-done | bytes 278560 | tf_op jit(solution)/shard_map/ppermute | solution.py:32
  54.6 2.8 %attend_plane.11.refs_1_ = bf16[4,272,128]{2,1,0:T(8,128)(2,1)S(1)} custom-call(bf16[8,8,32,128]{3,2,1,0:T(8,128)(2,1)S(1)} %pad_maximum_fusion.q_ref, bf16[2,2048,256]{2,1,0:T(8,128)(2,1)S(1)} %get-tuple-element.40.kx, bf16[2,2048,256]{2,1,0:T(8,128)(2,1)S(1)} %get-tuple-element.41.vx), custom_call_target="tpu_custom_call" | custom-call | flops 2147483648 | bytes 4194304 | tf_op jit(solution)/shard_map/attend_plane/pallas_call | solution.py:168
  58.9 2.0 %collective-permute-start.11 = (bf16[2,272,128]{2,1,0:T(8,128)(2,1)S(1)}, bf16[2,272,128]{2,1,0:T(8,128)(2,1)S(1)}, u32[]{:S(2)}, u32[]{:S(2)}) collective-permute-start(bf16[2,272,128]{2,1,0:T(8,128)(2,1)S(1)} %get-tuple-element.57), channel_id=1, source_target_pairs={{0,64},{1,9},{2,66},{3,11},{4,68},{5,13},{6,70},{7,15},{8,72},{9,1... | collective-permute-start | bytes 417800 | tf_op jit(solution)/shard_map/ppermute | solution.py:32
  60.9 1.7 %collective-permute-start.12 = (bf16[2,272,128]{2,1,0:T(8,128)(2,1)S(1)}, bf16[2,272,128]{2,1,0:T(8,128)(2,1)S(1)}, u32[]{:S(2)}, u32[]{:S(2)}) collective-permute-start(bf16[2,272,128]{2,1,0:T(8,128)(2,1)S(1)} %get-tuple-element.56), channel_id=1, source_target_pairs={{0,96},{1,13},{2,98},{3,15},{4,100},{5,1},{6,102},{7,3},{8,104},{9... | collective-permute-start | bytes 417800 | tf_op jit(solution)/shard_map/ppermute | solution.py:32
  62.9 2.6 %collective-permute-done.11.refs_1_ = bf16[2,272,128]{2,1,0:T(8,128)(2,1)S(1)} collective-permute-done((bf16[2,272,128]{2,1,0:T(8,128)(2,1)S(1)}, bf16[2,272,128]{2,1,0:T(8,128)(2,1)S(1)}, u32[]{:S(2)}, u32[]{:S(2)}) %collective-permute-start.11) | collective-permute-done | bytes 139296 | tf_op jit(solution)/shard_map/ppermute | solution.py:32
  66.6 2.2 %collective-permute-done.13.refs_3_ = bf16[2,272,128]{2,1,0:T(8,128)(2,1)S(1)} collective-permute-done((bf16[2,272,128]{2,1,0:T(8,128)(2,1)S(1)}, bf16[2,272,128]{2,1,0:T(8,128)(2,1)S(1)}, u32[]{:S(2)}, u32[]{:S(2)}) %collective-permute-start.13) | collective-permute-done | bytes 139296 | tf_op jit(solution)/shard_map/ppermute | solution.py:32
  69.2 2.8 %collective-permute-start.14 = (bf16[2,272,128]{2,1,0:T(8,128)(2,1)S(1)}, bf16[2,272,128]{2,1,0:T(8,128)(2,1)S(1)}, u32[]{:S(2)}, u32[]{:S(2)}) collective-permute-start(bf16[2,272,128]{2,1,0:T(8,128)(2,1)S(1)} %combine.3.mine), channel_id=1, source_target_pairs={{0,16},{1,17},{2,18},{3,19},{4,20},{5,21},{6,22},{7,23},{8,24},{9,... | collective-permute-start | bytes 417800 | tf_op jit(solution)/shard_map/ppermute | solution.py:32
  72.0 3.8 %collective-permute-done.14.theirs = bf16[2,272,128]{2,1,0:T(8,128)(2,1)S(1)} collective-permute-done((bf16[2,272,128]{2,1,0:T(8,128)(2,1)S(1)}, bf16[2,272,128]{2,1,0:T(8,128)(2,1)S(1)}, u32[]{:S(2)}, u32[]{:S(2)}) %collective-permute-start.14) | collective-permute-done | bytes 139296 | tf_op jit(solution)/shard_map/ppermute | solution.py:32
  77.6 2.9 %collective-permute-start.17 = (bf16[16,4096]{1,0:T(8,128)(2,1)S(1)}, bf16[16,4096]{1,0:T(8,128)(2,1)S(1)}, u32[]{:S(2)}, u32[]{:S(2)}) collective-permute-start(bf16[16,4096]{1,0:T(8,128)(2,1)S(1)} %finish.1.x0), channel_id=1, source_target_pairs={{0,96},{1,13},{2,98},{3,15},{4,100},{5,1},{6,102},{7,3},{8,104},{9... | collective-permute-start | bytes 393224 | tf_op jit(solution)/shard_map/ppermute | solution.py:32
  80.5 2.4 %collective-permute-done.16.x2 = bf16[16,4096]{1,0:T(8,128)(2,1)S(1)} collective-permute-done((bf16[16,4096]{1,0:T(8,128)(2,1)S(1)}, bf16[16,4096]{1,0:T(8,128)(2,1)S(1)}, u32[]{:S(2)}, u32[]{:S(2)}) %collective-permute-start.16) | collective-permute-done | bytes 131104 | tf_op jit(solution)/shard_map/ppermute | solution.py:32
  85.0 2.5 %collective-permute-start.20 = (bf16[64,4096]{1,0:T(8,128)(2,1)S(1)}, bf16[64,4096]{1,0:T(8,128)(2,1)S(1)}, u32[]{:S(2)}, u32[]{:S(2)}) collective-permute-start(bf16[64,4096]{1,0:T(8,128)(2,1)S(1)} %assemble.1.x_ref), channel_id=1, source_target_pairs={{0,12},{1,97},{2,14},{3,99},{4,0},{5,101},{6,2},{7,103},{8,4},{9,1... | collective-permute-start | bytes 1572872 | tf_op jit(solution)/shard_map/ppermute | solution.py:32
  89.4 10.9 %collective-permute-done.19.x_ref = bf16[64,4096]{1,0:T(8,128)(2,1)S(1)} collective-permute-done((bf16[64,4096]{1,0:T(8,128)(2,1)S(1)}, bf16[64,4096]{1,0:T(8,128)(2,1)S(1)}, u32[]{:S(2)}, u32[]{:S(2)}) %collective-permute-start.19) | collective-permute-done | bytes 524320 | tf_op jit(solution)/shard_map/ppermute | solution.py:32
  102.0 1.4 %place.1 = f32[256,512]{1,0:T(8,128)S(1)} custom-call(s32[7]{0:T(128)S(1)} %concatenate.10.info, f32[64,512]{1,0:T(8,128)S(1)} %project.3.y0, f32[64,512]{1,0:T(8,128)S(1)} %project.4.y1, f32[64,512]{1,0:T(8,128)S(1)} %project.5.y3, bf16[64,4096]{1,0:T(8,128)(2,1)S(1)} %collective-permute-done.21.x_ref, bf16[4096,512]{1,0:T(8,128)(2,1)S(1)} %copy-done), custom_call_target="tpu_custom_call" | custom-call | tf_op jit(solution)/shard_map/place/pallas_call | solution.py:308
  103.5 1.5 %collective-permute-done.22 = f32[128,512]{1,0:T(8,128)S(1)} collective-permute-done((f32[128,512]{1,0:T(8,128)S(1)}, f32[128,512]{1,0:T(8,128)S(1)}, u32[]{:S(2)}, u32[]{:S(2)}) %collective-permute-start.22) | collective-permute-done | bytes 262176 | tf_op jit(solution)/shard_map/ppermute | solution.py:32
  106.3 3.1 %collective-permute-done.23 = bf16[64,512]{1,0:T(8,128)(2,1)S(1)} collective-permute-done((bf16[64,512]{1,0:T(8,128)(2,1)S(1)}, bf16[64,512]{1,0:T(8,128)(2,1)S(1)}, u32[]{:S(2)}, u32[]{:S(2)}) %collective-permute-start.23) | collective-permute-done | bytes 65568 | tf_op jit(solution)/shard_map/ppermute | solution.py:32
  (44 shorter events, 17.3 us)
Async XLA Ops:
  0.0 6.5 %copy-start.1 = (bf16[8,32,128]{2,1,0:T(8,128)(2,1)S(1)}, bf16[8,32,128]{2,1,0:T(8,128)(2,1)}, u32[]{:S(2)}) copy-start(bf16[8,32,128]{2,1,0:T(8,128)(2,1)} %param.6) | copy-start | bytes 196612
  0.0 6.5 %collective-permute-start = (bf16[1,8,32,128]{3,2,1,0:T(8,128)(2,1)}, bf16[1,8,32,128]{3,2,1,0:T(8,128)(2,1)S(1)}, u32[]{:S(2)}, u32[]{:S(2)}) collective-permute-start(bf16[1,8,32,128]{3,2,1,0:T(8,128)(2,1)} %bitcast.10), channel_id=1, source_target_pairs={{0,16},{1,17},{2,18},{3,19},{4,20},{5,21},{6,22},{7,23},{8,24},{9,... | collective-permute-start | bytes 196616 | tf_op jit(solution)/shard_map/ppermute | solution.py:32
  6.6 8.7 %collective-permute-start.1 = (bf16[2,8,32,128]{3,2,1,0:T(8,128)(2,1)S(1)}, bf16[2,8,32,128]{3,2,1,0:T(8,128)(2,1)S(1)}, u32[]{:S(2)}, u32[]{:S(2)}) collective-permute-start(bf16[2,8,32,128]{3,2,1,0:T(8,128)(2,1)S(1)} %pad_maximum_fusion.1), channel_id=1, source_target_pairs={{0,32},{1,5},{2,34},{3,7},{4,36},{5,9},{6,38},{7,11},{8,40},{9,13}... | collective-permute-start | bytes 393224 | tf_op jit(solution)/shard_map/ppermute | solution.py:32
  8.5 7.9 %collective-permute-start.2 = (bf16[2,8,32,128]{3,2,1,0:T(8,128)(2,1)S(1)}, bf16[2,8,32,128]{3,2,1,0:T(8,128)(2,1)S(1)}, u32[]{:S(2)}, u32[]{:S(2)}) collective-permute-start(bf16[2,8,32,128]{3,2,1,0:T(8,128)(2,1)S(1)} %pad_maximum_fusion.1), channel_id=1, source_target_pairs={{0,64},{1,9},{2,66},{3,11},{4,68},{5,13},{6,70},{7,15},{8,72},{9,1... | collective-permute-start | bytes 393224 | tf_op jit(solution)/shard_map/ppermute | solution.py:32
  12.1 5.0 %collective-permute-start.3 = (bf16[2,8,32,128]{3,2,1,0:T(8,128)(2,1)S(1)}, bf16[2,8,32,128]{3,2,1,0:T(8,128)(2,1)S(1)}, u32[]{:S(2)}, u32[]{:S(2)}) collective-permute-start(bf16[2,8,32,128]{3,2,1,0:T(8,128)(2,1)S(1)} %pad_maximum_fusion.1), channel_id=1, source_target_pairs={{0,96},{1,13},{2,98},{3,15},{4,100},{5,1},{6,102},{7,3},{8,104},{9... | collective-permute-start | bytes 393224 | tf_op jit(solution)/shard_map/ppermute | solution.py:32
  17.2 10.5 %collective-permute-start.4 = (bf16[8,8,32,128]{3,2,1,0:T(8,128)(2,1)S(1)}, bf16[8,8,32,128]{3,2,1,0:T(8,128)(2,1)S(1)}, u32[]{:S(2)}, u32[]{:S(2)}) collective-permute-start(bf16[8,8,32,128]{3,2,1,0:T(8,128)(2,1)S(1)} %pad_maximum_fusion.q_ref), channel_id=1, source_target_pairs={{0,4},{1,33},{2,6},{3,35},{4,8},{5,37},{6,10},{7,39},{8,12},{9,41}... | collective-permute-start | bytes 1572872 | tf_op jit(solution)/shard_map/ppermute | solution.py:32
  18.7 16.2 %collective-permute-start.5 = (bf16[8,8,32,128]{3,2,1,0:T(8,128)(2,1)S(1)}, bf16[8,8,32,128]{3,2,1,0:T(8,128)(2,1)S(1)}, u32[]{:S(2)}, u32[]{:S(2)}) collective-permute-start(bf16[8,8,32,128]{3,2,1,0:T(8,128)(2,1)S(1)} %pad_maximum_fusion.q_ref), channel_id=1, source_target_pairs={{0,8},{1,65},{2,10},{3,67},{4,12},{5,69},{6,14},{7,71},{8,0},{9,73... | collective-permute-start | bytes 1572872 | tf_op jit(solution)/shard_map/ppermute | solution.py:32
  21.5 13.5 %collective-permute-start.6 = (bf16[8,8,32,128]{3,2,1,0:T(8,128)(2,1)S(1)}, bf16[8,8,32,128]{3,2,1,0:T(8,128)(2,1)S(1)}, u32[]{:S(2)}, u32[]{:S(2)}) collective-permute-start(bf16[8,8,32,128]{3,2,1,0:T(8,128)(2,1)S(1)} %pad_maximum_fusion.q_ref), channel_id=1, source_target_pairs={{0,12},{1,97},{2,14},{3,99},{4,0},{5,101},{6,2},{7,103},{8,4},{9,1... | collective-permute-start | bytes 1572872 | tf_op jit(solution)/shard_map/ppermute | solution.py:32
  33.2 9.8 %collective-permute-start.7 = (bf16[8,272,128]{2,1,0:T(8,128)(2,1)S(1)}, bf16[8,272,128]{2,1,0:T(8,128)(2,1)S(1)}, u32[]{:S(2)}, u32[]{:S(2)}) collective-permute-start(bf16[8,272,128]{2,1,0:T(8,128)(2,1)S(1)} %attend_plane.7), channel_id=1, source_target_pairs={{0,12},{1,97},{2,14},{3,99},{4,0},{5,101},{6,2},{7,103},{8,4},{9,1... | collective-permute-start | bytes 1671176 | tf_op jit(solution)/shard_map/ppermute | solution.py:32
  40.5 11.2 %collective-permute-start.8 = (bf16[8,272,128]{2,1,0:T(8,128)(2,1)S(1)}, bf16[8,272,128]{2,1,0:T(8,128)(2,1)S(1)}, u32[]{:S(2)}, u32[]{:S(2)}) collective-permute-start(bf16[8,272,128]{2,1,0:T(8,128)(2,1)S(1)} %attend_plane.8), channel_id=1, source_target_pairs={{0,8},{1,65},{2,10},{3,67},{4,12},{5,69},{6,14},{7,71},{8,0},{9,73... | collective-permute-start | bytes 1671176 | tf_op jit(solution)/shard_map/ppermute | solution.py:32
  45.7 8.9 %collective-permute-start.9 = (bf16[4,272,128]{2,1,0:T(8,128)(2,1)S(1)}, bf16[4,272,128]{2,1,0:T(8,128)(2,1)S(1)}, u32[]{:S(2)}, u32[]{:S(2)}) collective-permute-start(bf16[4,272,128]{2,1,0:T(8,128)(2,1)S(1)} %attend_plane.9), channel_id=1, source_target_pairs={{0,4},{1,33},{2,6},{3,35},{4,8},{5,37},{6,10},{7,39},{8,12},{9,41}... | collective-permute-start | bytes 835592 | tf_op jit(solution)/shard_map/ppermute | solution.py:32
  48.9 8.7 %collective-permute-start.10 = (bf16[4,272,128]{2,1,0:T(8,128)(2,1)S(1)}, bf16[4,272,128]{2,1,0:T(8,128)(2,1)S(1)}, u32[]{:S(2)}, u32[]{:S(2)}) collective-permute-start(bf16[4,272,128]{2,1,0:T(8,128)(2,1)S(1)} %attend_plane.10), channel_id=1, source_target_pairs={{0,4},{1,33},{2,6},{3,35},{4,8},{5,37},{6,10},{7,39},{8,12},{9,41}... | collective-permute-start | bytes 835592 | tf_op jit(solution)/shard_map/ppermute | solution.py:32
  57.6 30.9 %copy-start = (bf16[4096,512]{1,0:T(8,128)(2,1)S(1)}, bf16[4096,512]{1,0:T(8,128)(2,1)}, u32[]{:S(2)}) copy-start(bf16[4096,512]{1,0:T(8,128)(2,1)} %w_ref.7) | copy-start | bytes 12582916
  58.9 6.6 %collective-permute-start.11 = (bf16[2,272,128]{2,1,0:T(8,128)(2,1)S(1)}, bf16[2,272,128]{2,1,0:T(8,128)(2,1)S(1)}, u32[]{:S(2)}, u32[]{:S(2)}) collective-permute-start(bf16[2,272,128]{2,1,0:T(8,128)(2,1)S(1)} %get-tuple-element.57), channel_id=1, source_target_pairs={{0,64},{1,9},{2,66},{3,11},{4,68},{5,13},{6,70},{7,15},{8,72},{9,1... | collective-permute-start | bytes 417800 | tf_op jit(solution)/shard_map/ppermute | solution.py:32
  60.9 5.7 %collective-permute-start.12 = (bf16[2,272,128]{2,1,0:T(8,128)(2,1)S(1)}, bf16[2,272,128]{2,1,0:T(8,128)(2,1)S(1)}, u32[]{:S(2)}, u32[]{:S(2)}) collective-permute-start(bf16[2,272,128]{2,1,0:T(8,128)(2,1)S(1)} %get-tuple-element.56), channel_id=1, source_target_pairs={{0,96},{1,13},{2,98},{3,15},{4,100},{5,1},{6,102},{7,3},{8,104},{9... | collective-permute-start | bytes 417800 | tf_op jit(solution)/shard_map/ppermute | solution.py:32
  62.6 6.3 %collective-permute-start.13 = (bf16[2,272,128]{2,1,0:T(8,128)(2,1)S(1)}, bf16[2,272,128]{2,1,0:T(8,128)(2,1)S(1)}, u32[]{:S(2)}, u32[]{:S(2)}) collective-permute-start(bf16[2,272,128]{2,1,0:T(8,128)(2,1)S(1)} %get-tuple-element.55), channel_id=1, source_target_pairs={{0,32},{1,5},{2,34},{3,7},{4,36},{5,9},{6,38},{7,11},{8,40},{9,13}... | collective-permute-start | bytes 417800 | tf_op jit(solution)/shard_map/ppermute | solution.py:32
  69.2 6.6 %collective-permute-start.14 = (bf16[2,272,128]{2,1,0:T(8,128)(2,1)S(1)}, bf16[2,272,128]{2,1,0:T(8,128)(2,1)S(1)}, u32[]{:S(2)}, u32[]{:S(2)}) collective-permute-start(bf16[2,272,128]{2,1,0:T(8,128)(2,1)S(1)} %combine.3.mine), channel_id=1, source_target_pairs={{0,16},{1,17},{2,18},{3,19},{4,20},{5,21},{6,22},{7,23},{8,24},{9,... | collective-permute-start | bytes 417800 | tf_op jit(solution)/shard_map/ppermute | solution.py:32
  76.2 6.6 %collective-permute-start.16 = (bf16[16,4096]{1,0:T(8,128)(2,1)S(1)}, bf16[16,4096]{1,0:T(8,128)(2,1)S(1)}, u32[]{:S(2)}, u32[]{:S(2)}) collective-permute-start(bf16[16,4096]{1,0:T(8,128)(2,1)S(1)} %finish.1.x0), channel_id=1, source_target_pairs={{0,64},{1,9},{2,66},{3,11},{4,68},{5,13},{6,70},{7,15},{8,72},{9,1... | collective-permute-start | bytes 393224 | tf_op jit(solution)/shard_map/ppermute | solution.py:32
  77.2 6.9 %collective-permute-start.15 = (bf16[16,4096]{1,0:T(8,128)(2,1)S(1)}, bf16[16,4096]{1,0:T(8,128)(2,1)S(1)}, u32[]{:S(2)}, u32[]{:S(2)}) collective-permute-start(bf16[16,4096]{1,0:T(8,128)(2,1)S(1)} %finish.1.x0), channel_id=1, source_target_pairs={{0,32},{1,5},{2,34},{3,7},{4,36},{5,9},{6,38},{7,11},{8,40},{9,13}... | collective-permute-start | bytes 393224 | tf_op jit(solution)/shard_map/ppermute | solution.py:32
  77.6 6.6 %collective-permute-start.17 = (bf16[16,4096]{1,0:T(8,128)(2,1)S(1)}, bf16[16,4096]{1,0:T(8,128)(2,1)S(1)}, u32[]{:S(2)}, u32[]{:S(2)}) collective-permute-start(bf16[16,4096]{1,0:T(8,128)(2,1)S(1)} %finish.1.x0), channel_id=1, source_target_pairs={{0,96},{1,13},{2,98},{3,15},{4,100},{5,1},{6,102},{7,3},{8,104},{9... | collective-permute-start | bytes 393224 | tf_op jit(solution)/shard_map/ppermute | solution.py:32
  82.8 1.3 %collective-permute-start.18 = (bf16[16,4096]{1,0:T(8,128)(2,1)S(1)}, bf16[16,4096]{1,0:T(8,128)(2,1)S(1)}, u32[]{:S(2)}, u32[]{:S(2)}) collective-permute-start(bf16[16,4096]{1,0:T(8,128)(2,1)S(1)} %collective-permute-done.16.x2), channel_id=1, source_target_pairs={{0,1},{1,0},{2,3},{3,2},{4,5},{5,4},{6,7},{7,6},{8,9},{9,8},{10,11... | collective-permute-start | bytes 393224 | tf_op jit(solution)/shard_map/ppermute | solution.py:32
  84.2 16.1 %collective-permute-start.19 = (bf16[64,4096]{1,0:T(8,128)(2,1)S(1)}, bf16[64,4096]{1,0:T(8,128)(2,1)S(1)}, u32[]{:S(2)}, u32[]{:S(2)}) collective-permute-start(bf16[64,4096]{1,0:T(8,128)(2,1)S(1)} %assemble.1.x_ref), channel_id=1, source_target_pairs={{0,4},{1,33},{2,6},{3,35},{4,8},{5,37},{6,10},{7,39},{8,12},{9,41}... | collective-permute-start | bytes 1572872 | tf_op jit(solution)/shard_map/ppermute | solution.py:32
  85.0 16.1 %collective-permute-start.20 = (bf16[64,4096]{1,0:T(8,128)(2,1)S(1)}, bf16[64,4096]{1,0:T(8,128)(2,1)S(1)}, u32[]{:S(2)}, u32[]{:S(2)}) collective-permute-start(bf16[64,4096]{1,0:T(8,128)(2,1)S(1)} %assemble.1.x_ref), channel_id=1, source_target_pairs={{0,12},{1,97},{2,14},{3,99},{4,0},{5,101},{6,2},{7,103},{8,4},{9,1... | collective-permute-start | bytes 1572872 | tf_op jit(solution)/shard_map/ppermute | solution.py:32
  87.5 14.5 %collective-permute-start.21 = (bf16[64,4096]{1,0:T(8,128)(2,1)S(1)}, bf16[64,4096]{1,0:T(8,128)(2,1)S(1)}, u32[]{:S(2)}, u32[]{:S(2)}) collective-permute-start(bf16[64,4096]{1,0:T(8,128)(2,1)S(1)} %assemble.1.x_ref), channel_id=1, source_target_pairs={{0,8},{1,65},{2,10},{3,67},{4,12},{5,69},{6,14},{7,71},{8,0},{9,73... | collective-permute-start | bytes 1572872 | tf_op jit(solution)/shard_map/ppermute | solution.py:32
  103.4 1.6 %collective-permute-start.22 = (f32[128,512]{1,0:T(8,128)S(1)}, f32[128,512]{1,0:T(8,128)S(1)}, u32[]{:S(2)}, u32[]{:S(2)}) collective-permute-start(f32[128,512]{1,0:T(8,128)S(1)} %slice.38), channel_id=1, source_target_pairs={{0,1},{1,0},{2,3},{3,2},{4,5},{5,4},{6,7},{7,6},{8,9},{9,8},{10,11... | collective-permute-start | bytes 786440 | tf_op jit(solution)/shard_map/ppermute | solution.py:32
  105.1 4.3 %collective-permute-start.23 = (bf16[64,512]{1,0:T(8,128)(2,1)S(1)}, bf16[64,512]{1,0:T(8,128)(2,1)S(1)}, u32[]{:S(2)}, u32[]{:S(2)}) collective-permute-start(bf16[64,512]{1,0:T(8,128)(2,1)S(1)} %slice.46), channel_id=1, source_target_pairs={{0,2},{1,3},{2,0},{3,1},{4,6},{5,7},{6,4},{7,5},{8,10},{9,11},{10,... | collective-permute-start | bytes 196616 | tf_op jit(solution)/shard_map/ppermute | solution.py:32
where the time goes:
time: 110 us
  starting transfers between devices  38.4 us (35%)
  waiting for transfers between devices  37.2 us (34%)
  Pallas kernels  30.2 us (27%)
  local copies, waits for them, and re-layouts  1.97 us (2%)
  between operations  1.56 us (1%)
    ppermute x24, starting transfers between devices, moved(): return lax.ppermute(x, ('cp', 'tp'), pairs)  38.4 us
    ppermute x24, waiting for transfers between devices, moved(): return lax.ppermute(x, ('cp', 'tp'), pairs)  37.2 us
    pallas_call x6, Pallas kernels, attend(): pl.pallas_call(functools.partial(attend_kernel, kvs=kvs, first=first, nb=...  22.1 us
    pallas_call x3, Pallas kernels, project(): pl.pallas_call(project_kernel, in_specs=[vmem, vmem], out_specs=vmem, out...  2.5 us
  transfers between devices with their start and end apart: 24, of which 16 were waited for; matrix products, arithmetic and copies ran while one was open for 2% of the time, Pallas kernels for 24%

commit v1 on v0

--- a/solution.py
+++ b/solution.py
@@ -195,36 +195,31 @@
     return out, m, total
 
 
-def combine_kernel(*refs, pieces):
-    o_ref = refs[-1]
-    blocks, nkv = o_ref.shape[0], o_ref.shape[1] // 136
+def combine_kernel(*refs, starts):
+    parts, o_ref = refs[:-1], refs[-1]
+    nkv = o_ref.shape[1] // 136
     eye = diagonal()
-    for b in range(blocks):
-        parts, at = [], 0
-        for count in pieces:
-            share = blocks // count
-            parts.append(refs[at + b // share].at[b % share])
-            at += count
+    for b in range(o_ref.shape[0]):
+        here = [part.at[at + b] for part, at in zip(parts, starts)]
         stats = []
         for kv in range(nkv):
-            out, m, total = merged(parts, kv, nkv, eye)
+            out, m, total = merged(here, kv, nkv, eye)
             o_ref[b, kv * 128 : (kv + 1) * 128, :] = out.astype(jnp.bfloat16)
             stats.append(stat_rows(m, total))
         o_ref[b, nkv * 128 :, :] = jnp.concatenate(stats, axis=0).astype(jnp.bfloat16)
 
 
-def combine(parts):
-    vmem = pl.BlockSpec(memory_space=pltpu.VMEM)
-    flat = [piece for part in parts for piece in part]
-    blocks = sum(piece.shape[0] for piece in parts[0])
-    return pl.pallas_call(
-        functools.partial(combine_kernel, pieces=[len(part) for part in parts]),
-        in_specs=[vmem] * len(flat),
-        out_specs=vmem,
-        out_shape=jax.ShapeDtypeStruct((blocks, *flat[0].shape[1:]), jnp.bfloat16),
+def combine(blocks, *parts):
+    vmem = pl.BlockSpec(memory_space=pltpu.VMEM)
+    arrays, starts = zip(*parts)
+    return pl.pallas_call(
+        functools.partial(combine_kernel, starts=starts),
+        in_specs=[vmem] * len(arrays),
+        out_specs=vmem,
+        out_shape=jax.ShapeDtypeStruct((blocks, *arrays[0].shape[1:]), jnp.bfloat16),
         compiler_params=pltpu.CompilerParams(vmem_limit_bytes=8 * MIB),
         name="combine",
-    )(*flat)
+    )(*arrays)
 
 
 def finish_kernel(mine, theirs, o_ref, rows):
@@ -329,26 +324,29 @@
     q = jnp.concatenate([q, q1, q2, q3], axis=0)
     q, vx, kx0, kx1, kx2, kx3 = together(q, vx, kx0, kx1, kx2, kx3)
 
-    q1, q2, q3 = (moved(q, b=d) for d in (1, 2, 3))
-
+    q2, q1, q3 = (moved(q, b=d) for d in (2, 1, 3))
     kvs = tuple(range(nkv))
     own0 = attend(q, kx0, vx, kvs, 0, 4)
-    q1, own0 = together(q1, own0)
+    q2, own0 = together(q2, own0)
+    p2 = attend(q2, kx2, vx, kvs)
+    r2 = moved(p2, b=-2)
+    q1, q3, p2 = together(q1, q3, p2)
     p1 = attend(q1, kx1, vx, kvs)
     r1 = moved(p1, b=-1)
-    q2, q3, p1 = together(q2, q3, p1)
-    p2 = attend(q2, kx2, vx, kvs)
-    r2 = moved(p2, b=-2)
-    q3, p2, r1 = together(q3, p2, r1)
+    q3, p1 = together(q3, p1)
     p3a = attend(q3, kx3, vx, kvs, 0, 4)
     r3a = moved(p3a, b=-3)
-    q3, p3a = together(q3, p3a)
+    q3, p3a, r2 = together(q3, p3a, r2)
     p3b = attend(q3, kx3, vx, kvs, 4, 4)
     r3b = moved(p3b, b=-3)
-    q, p3b, r2, r3a = together(q, p3b, r2, r3a)
+    q, p3b, r1, r3a = together(q, p3b, r1, r3a)
+    low = combine(4, (own0, 0), (r1, 0), (r2, 0), (r3a, 0))
+    q, low = together(q, low)
     own1 = attend(q, kx0, vx, kvs, 4, 4)
-    c = combine([[own0, own1], [r1], [r2], [r3a, r3b]])
-    c = combine([[c[:2]]] + [[moved(c[2 * d : 2 * d + 2], a=-d)] for d in (2, 1, 3)])
+    s1 = moved(low[2:], a=-1)
+    high = combine(4, (own1, 0), (r1, 4), (r2, 4), (r3b, 0))
+    s2, s3 = moved(high[:2], a=-2), moved(high[2:], a=-3)
+    c = combine(2, (low, 0), (s1, 0), (s2, 0), (s3, 0))
     attn = finish(c, moved(c, yh=1))
     x2, x1, x3 = (moved(attn, a=d) for d in (2, 1, 3))
     attn = assemble(attn, x1, x2, x3, moved(x2, core=1))

time: 110 us -> 110 us (level)
    ppermute x24, waiting for transfers between devices: 37.2 us -> 38.3 us  [moved(): return lax.ppermute(x, ('cp', 'tp'), pairs)]
  transfers between devices with their start and end apart: 24 -> 24, of which waited for: 16 -> 12; matrix products, arithmetic and copies ran while one was open for 2% -> 2% of each run, Pallas kernels for 24% -> 26%
where the time goes in v1:
time: 110 us
  waiting for transfers between devices  38.3 us (35%)
  starting transfers between devices  37.4 us (34%)
  Pallas kernels  30.2 us (27%)
  local copies, waits for them, and re-layouts  1.97 us (2%)
  between operations  1.59 us (1%)
    ppermute x24, waiting for transfers between devices, moved(): return lax.ppermute(x, ('cp', 'tp'), pairs)  38.3 us
    ppermute x24, starting transfers between devices, moved(): return lax.ppermute(x, ('cp', 'tp'), pairs)  37.4 us
    pallas_call x6, Pallas kernels, attend(): pl.pallas_call(functools.partial(attend_kernel, kvs=kvs, first=first, nb=...  22.1 us
    pallas_call x3, Pallas kernels, project(): pl.pallas_call(project_kernel, in_specs=[vmem, vmem], out_specs=vmem, out...  2.5 us
  transfers between devices with their start and end apart: 24, of which 12 were waited for; matrix products, arithmetic and copies ran while one was open for 2% of the time, Pallas kernels for 26%

profile of v1, /device:TPU:0, one launch (start us, length us, event | category | flops | bytes accessed | tf_op | source)
XLA Modules:
  0.0 110.3 jit_solution(9877165309897506871)
XLA Ops:
  0.0 3.3 %collective-permute-start = (bf16[1,8,32,128]{3,2,1,0:T(8,128)(2,1)}, bf16[1,8,32,128]{3,2,1,0:T(8,128)(2,1)S(1)}, u32[]{:S(2)}, u32[]{:S(2)}) collective-permute-start(bf16[1,8,32,128]{3,2,1,0:T(8,128)(2,1)} %bitcast.10), channel_id=1, source_target_pairs={{0,16},{1,17},{2,18},{3,19},{4,20},{5,21},{6,22},{7,23},{8,24},{9,... | collective-permute-start | bytes 196616 | tf_op jit(solution)/shard_map/ppermute | solution.py:32
  3.3 1.8 %copy_bitcast_fusion = (bf16[2,2048,128]{2,1,0:T(8,128)(2,1)S(1)}, bf16[2,2048,128]{2,1,0:T(8,128)(2,1)S(1)}) fusion(bf16[2048,2,128]{2,1,0:T(2,128)(2,1)} %param.8, bf16[2048,2,128]{2,1,0:T(2,128)(2,1)} %param.7), kind=kLoop, calls=%fused_computation | loop fusion | bytes 4194304 | tf_op jit(solution)/shard_map/transpose | solution.py:318
  6.6 2.0 %collective-permute-start.1 = (bf16[2,8,32,128]{3,2,1,0:T(8,128)(2,1)S(1)}, bf16[2,8,32,128]{3,2,1,0:T(8,128)(2,1)S(1)}, u32[]{:S(2)}, u32[]{:S(2)}) collective-permute-start(bf16[2,8,32,128]{3,2,1,0:T(8,128)(2,1)S(1)} %pad_maximum_fusion.1), channel_id=1, source_target_pairs={{0,32},{1,5},{2,34},{3,7},{4,36},{5,9},{6,38},{7,11},{8,40},{9,13}... | collective-permute-start | bytes 393224 | tf_op jit(solution)/shard_map/ppermute | solution.py:32
  8.5 3.6 %collective-permute-start.2 = (bf16[2,8,32,128]{3,2,1,0:T(8,128)(2,1)S(1)}, bf16[2,8,32,128]{3,2,1,0:T(8,128)(2,1)S(1)}, u32[]{:S(2)}, u32[]{:S(2)}) collective-permute-start(bf16[2,8,32,128]{3,2,1,0:T(8,128)(2,1)S(1)} %pad_maximum_fusion.1), channel_id=1, source_target_pairs={{0,64},{1,9},{2,66},{3,11},{4,68},{5,13},{6,70},{7,15},{8,72},{9,1... | collective-permute-start | bytes 393224 | tf_op jit(solution)/shard_map/ppermute | solution.py:32
  13.1 2.2 %prepare.1 = (bf16[2,2048,256]{2,1,0:T(8,128)(2,1)S(1)}, bf16[2,2048,256]{2,1,0:T(8,128)(2,1)S(1)}, bf16[2,2048,256]{2,1,0:T(8,128)(2,1)S(1)}, bf16[2,2048,256]{...) custom-call(s32[7]{0:T(128)S(1)} %concatenate.10.info, bf16[2,2048,128]{2,1,0:T(8,128)(2,1)S(1)} %get-tuple-element.34.k_ref, ...), custom_call_target="tpu_custom_call" | custom-call | tf_op jit(solution)/shard_map/prepare/pallas_call | solution.py:87
  15.3 1.2 %collective-permute-done.2 = bf16[2,8,32,128]{3,2,1,0:T(8,128)(2,1)S(1)} collective-permute-done((bf16[2,8,32,128]{3,2,1,0:T(8,128)(2,1)S(1)}, bf16[2,8,32,128]{3,2,1,0:T(8,128)(2,1)S(1)}, u32[]{:S(2)}, u32[]{:S(2)}) %collective-permute-start.2) | collective-permute-done | bytes 131104 | tf_op jit(solution)/shard_map/ppermute | solution.py:32
  17.2 3.1 %collective-permute-start.6 = (bf16[8,8,32,128]{3,2,1,0:T(8,128)(2,1)S(1)}, bf16[8,8,32,128]{3,2,1,0:T(8,128)(2,1)S(1)}, u32[]{:S(2)}, u32[]{:S(2)}) collective-permute-start(bf16[8,8,32,128]{3,2,1,0:T(8,128)(2,1)S(1)} %pad_maximum_fusion.q_ref), channel_id=1, source_target_pairs={{0,8},{1,65},{2,10},{3,67},{4,12},{5,69},{6,14},{7,71},{8,0},{9,73... | collective-permute-start | bytes 1572872 | tf_op jit(solution)/shard_map/ppermute | solution.py:32
  20.9 2.6 %collective-permute-start.5 = (bf16[8,8,32,128]{3,2,1,0:T(8,128)(2,1)S(1)}, bf16[8,8,32,128]{3,2,1,0:T(8,128)(2,1)S(1)}, u32[]{:S(2)}, u32[]{:S(2)}) collective-permute-start(bf16[8,8,32,128]{3,2,1,0:T(8,128)(2,1)S(1)} %pad_maximum_fusion.q_ref), channel_id=1, source_target_pairs={{0,12},{1,97},{2,14},{3,99},{4,0},{5,101},{6,2},{7,103},{8,4},{9,1... | collective-permute-start | bytes 1572872 | tf_op jit(solution)/shard_map/ppermute | solution.py:32
  23.5 2.8 %attend_plane.6.refs_0_ = bf16[4,272,128]{2,1,0:T(8,128)(2,1)S(1)} custom-call(bf16[8,8,32,128]{3,2,1,0:T(8,128)(2,1)S(1)} %pad_maximum_fusion.q_ref, bf16[2,2048,256]{2,1,0:T(8,128)(2,1)S(1)} %get-tuple-element.42.kx, bf16[2,2048,256]{2,1,0:T(8,128)(2,1)S(1)} %get-tuple-element.43.vx), custom_call_target="tpu_custom_call" | custom-call | flops 2147483648 | bytes 4194304 | tf_op jit(solution)/shard_map/attend_plane/pallas_call | solution.py:168
  26.3 1.8 %collective-permute-done.6.q_ref = bf16[8,8,32,128]{3,2,1,0:T(8,128)(2,1)S(1)} collective-permute-done((bf16[8,8,32,128]{3,2,1,0:T(8,128)(2,1)S(1)}, bf16[8,8,32,128]{3,2,1,0:T(8,128)(2,1)S(1)}, u32[]{:S(2)}, u32[]{:S(2)}) %collective-permute-start.6) | collective-permute-done | bytes 524320 | tf_op jit(solution)/shard_map/ppermute | solution.py:32
  28.0 5.5 %attend_plane.7 = bf16[8,272,128]{2,1,0:T(8,128)(2,1)S(1)} custom-call(bf16[8,8,32,128]{3,2,1,0:T(8,128)(2,1)S(1)} %collective-permute-done.6.q_ref, bf16[2,2048,256]{2,1,0:T(8,128)(2,1)S(1)} %get-tuple-element.45.kx, bf16[2,2048,256]{2,1,0:T(8,128)(2,1)S(1)} %get-tuple-element.43.vx), custom_call_target="tpu_custom_call" | custom-call | flops 4294967296 | bytes 4194304 | tf_op jit(solution)/shard_map/attend_plane/pallas_call | solution.py:168
  33.6 3.3 %collective-permute-start.7 = (bf16[8,272,128]{2,1,0:T(8,128)(2,1)S(1)}, bf16[8,272,128]{2,1,0:T(8,128)(2,1)S(1)}, u32[]{:S(2)}, u32[]{:S(2)}) collective-permute-start(bf16[8,272,128]{2,1,0:T(8,128)(2,1)S(1)} %attend_plane.7), channel_id=1, source_target_pairs={{0,8},{1,65},{2,10},{3,67},{4,12},{5,69},{6,14},{7,71},{8,0},{9,73... | collective-permute-start | bytes 1671176 | tf_op jit(solution)/shard_map/ppermute | solution.py:32
  36.9 5.5 %attend_plane.8 = bf16[8,272,128]{2,1,0:T(8,128)(2,1)S(1)} custom-call(bf16[8,8,32,128]{3,2,1,0:T(8,128)(2,1)S(1)} %collective-permute-done.4.q_ref, bf16[2,2048,256]{2,1,0:T(8,128)(2,1)S(1)} %get-tuple-element.48.kx, bf16[2,2048,256]{2,1,0:T(8,128)(2,1)S(1)} %get-tuple-element.43.vx), custom_call_target="tpu_custom_call" | custom-call | flops 4294967296 | bytes 4194304 | tf_op jit(solution)/shard_map/attend_plane/pallas_call | solution.py:168
  42.4 1.2 %collective-permute-start.8 = (bf16[8,272,128]{2,1,0:T(8,128)(2,1)S(1)}, bf16[8,272,128]{2,1,0:T(8,128)(2,1)S(1)}, u32[]{:S(2)}, u32[]{:S(2)}) collective-permute-start(bf16[8,272,128]{2,1,0:T(8,128)(2,1)S(1)} %attend_plane.8), channel_id=1, source_target_pairs={{0,12},{1,97},{2,14},{3,99},{4,0},{5,101},{6,2},{7,103},{8,4},{9,1... | collective-permute-start | bytes 1671176 | tf_op jit(solution)/shard_map/ppermute | solution.py:32
  43.6 2.8 %attend_plane.9 = bf16[4,272,128]{2,1,0:T(8,128)(2,1)S(1)} custom-call(bf16[8,8,32,128]{3,2,1,0:T(8,128)(2,1)S(1)} %collective-permute-done.5.q_ref, bf16[2,2048,256]{2,1,0:T(8,128)(2,1)S(1)} %get-tuple-element.50.kx, bf16[2,2048,256]{2,1,0:T(8,128)(2,1)S(1)} %get-tuple-element.43.vx), custom_call_target="tpu_custom_call" | custom-call | flops 2147483648 | bytes 4194304 | tf_op jit(solution)/shard_map/attend_plane/pallas_call | solution.py:168
  47.4 2.8 %attend_plane.10 = bf16[4,272,128]{2,1,0:T(8,128)(2,1)S(1)} custom-call(bf16[8,8,32,128]{3,2,1,0:T(8,128)(2,1)S(1)} %collective-permute-done.5.q_ref, bf16[2,2048,256]{2,1,0:T(8,128)(2,1)S(1)} %get-tuple-element.50.kx, bf16[2,2048,256]{2,1,0:T(8,128)(2,1)S(1)} %get-tuple-element.43.vx), custom_call_target="tpu_custom_call" | custom-call | flops 2147483648 | bytes 4194304 | tf_op jit(solution)/shard_map/attend_plane/pallas_call | solution.py:168
  50.8 3.4 %collective-permute-done.9.refs_3_ = bf16[4,272,128]{2,1,0:T(8,128)(2,1)S(1)} collective-permute-done((bf16[4,272,128]{2,1,0:T(8,128)(2,1)S(1)}, bf16[4,272,128]{2,1,0:T(8,128)(2,1)S(1)}, u32[]{:S(2)}, u32[]{:S(2)}) %collective-permute-start.9) | collective-permute-done | bytes 278560 | tf_op jit(solution)/shard_map/ppermute | solution.py:32
  54.9 2.5 %collective-permute-start.10 = (bf16[2,272,128]{2,1,0:T(8,128)(2,1)S(1)}, bf16[2,272,128]{2,1,0:T(8,128)(2,1)S(1)}, u32[]{:S(2)}, u32[]{:S(2)}) collective-permute-start(bf16[2,272,128]{2,1,0:T(8,128)(2,1)S(1)} %slice.22), channel_id=1, source_target_pairs={{0,96},{1,13},{2,98},{3,15},{4,100},{5,1},{6,102},{7,3},{8,104},{9... | collective-permute-start | bytes 417800 | tf_op jit(solution)/shard_map/ppermute | solution.py:32
  57.4 2.8 %attend_plane.11.refs_0_ = bf16[4,272,128]{2,1,0:T(8,128)(2,1)S(1)} custom-call(bf16[8,8,32,128]{3,2,1,0:T(8,128)(2,1)S(1)} %pad_maximum_fusion.q_ref, bf16[2,2048,256]{2,1,0:T(8,128)(2,1)S(1)} %get-tuple-element.42.kx, bf16[2,2048,256]{2,1,0:T(8,128)(2,1)S(1)} %get-tuple-element.43.vx), custom_call_target="tpu_custom_call" | custom-call | flops 2147483648 | bytes 4194304 | tf_op jit(solution)/shard_map/attend_plane/pallas_call | solution.py:168
  62.1 5.6 %collective-permute-done.12.refs_2_ = bf16[2,272,128]{2,1,0:T(8,128)(2,1)S(1)} collective-permute-done((bf16[2,272,128]{2,1,0:T(8,128)(2,1)S(1)}, bf16[2,272,128]{2,1,0:T(8,128)(2,1)S(1)}, u32[]{:S(2)}, u32[]{:S(2)}) %collective-permute-start.12) | collective-permute-done | bytes 139296 | tf_op jit(solution)/shard_map/ppermute | solution.py:32
  67.7 1.4 %collective-permute-done.13.refs_3_ = bf16[2,272,128]{2,1,0:T(8,128)(2,1)S(1)} collective-permute-done((bf16[2,272,128]{2,1,0:T(8,128)(2,1)S(1)}, bf16[2,272,128]{2,1,0:T(8,128)(2,1)S(1)}, u32[]{:S(2)}, u32[]{:S(2)}) %collective-permute-start.13) | collective-permute-done | bytes 139296 | tf_op jit(solution)/shard_map/ppermute | solution.py:32
  69.5 2.8 %collective-permute-start.14 = (bf16[2,272,128]{2,1,0:T(8,128)(2,1)S(1)}, bf16[2,272,128]{2,1,0:T(8,128)(2,1)S(1)}, u32[]{:S(2)}, u32[]{:S(2)}) collective-permute-start(bf16[2,272,128]{2,1,0:T(8,128)(2,1)S(1)} %combine.5.mine), channel_id=1, source_target_pairs={{0,16},{1,17},{2,18},{3,19},{4,20},{5,21},{6,22},{7,23},{8,24},{9,... | collective-permute-start | bytes 417800 | tf_op jit(solution)/shard_map/ppermute | solution.py:32
  72.3 3.8 %collective-permute-done.14.theirs = bf16[2,272,128]{2,1,0:T(8,128)(2,1)S(1)} collective-permute-done((bf16[2,272,128]{2,1,0:T(8,128)(2,1)S(1)}, bf16[2,272,128]{2,1,0:T(8,128)(2,1)S(1)}, u32[]{:S(2)}, u32[]{:S(2)}) %collective-permute-start.14) | collective-permute-done | bytes 139296 | tf_op jit(solution)/shard_map/ppermute | solution.py:32
  77.9 2.6 %collective-permute-start.17 = (bf16[16,4096]{1,0:T(8,128)(2,1)S(1)}, bf16[16,4096]{1,0:T(8,128)(2,1)S(1)}, u32[]{:S(2)}, u32[]{:S(2)}) collective-permute-start(bf16[16,4096]{1,0:T(8,128)(2,1)S(1)} %finish.1.x0), channel_id=1, source_target_pairs={{0,96},{1,13},{2,98},{3,15},{4,100},{5,1},{6,102},{7,3},{8,104},{9... | collective-permute-start | bytes 393224 | tf_op jit(solution)/shard_map/ppermute | solution.py:32
  80.5 2.6 %collective-permute-done.16.x2 = bf16[16,4096]{1,0:T(8,128)(2,1)S(1)} collective-permute-done((bf16[16,4096]{1,0:T(8,128)(2,1)S(1)}, bf16[16,4096]{1,0:T(8,128)(2,1)S(1)}, u32[]{:S(2)}, u32[]{:S(2)}) %collective-permute-start.16) | collective-permute-done | bytes 131104 | tf_op jit(solution)/shard_map/ppermute | solution.py:32
  83.1 1.3 %collective-permute-done.15.x1 = bf16[16,4096]{1,0:T(8,128)(2,1)S(1)} collective-permute-done((bf16[16,4096]{1,0:T(8,128)(2,1)S(1)}, bf16[16,4096]{1,0:T(8,128)(2,1)S(1)}, u32[]{:S(2)}, u32[]{:S(2)}) %collective-permute-start.15) | collective-permute-done | bytes 131104 | tf_op jit(solution)/shard_map/ppermute | solution.py:32
  84.5 3.2 %collective-permute-start.20 = (bf16[64,4096]{1,0:T(8,128)(2,1)S(1)}, bf16[64,4096]{1,0:T(8,128)(2,1)S(1)}, u32[]{:S(2)}, u32[]{:S(2)}) collective-permute-start(bf16[64,4096]{1,0:T(8,128)(2,1)S(1)} %assemble.1.x_ref), channel_id=1, source_target_pairs={{0,12},{1,97},{2,14},{3,99},{4,0},{5,101},{6,2},{7,103},{8,4},{9,1... | collective-permute-start | bytes 1572872 | tf_op jit(solution)/shard_map/ppermute | solution.py:32
  88.6 11.9 %collective-permute-done.19.x_ref = bf16[64,4096]{1,0:T(8,128)(2,1)S(1)} collective-permute-done((bf16[64,4096]{1,0:T(8,128)(2,1)S(1)}, bf16[64,4096]{1,0:T(8,128)(2,1)S(1)}, u32[]{:S(2)}, u32[]{:S(2)}) %collective-permute-start.19) | collective-permute-done | bytes 524320 | tf_op jit(solution)/shard_map/ppermute | solution.py:32
  102.2 1.4 %place.1 = f32[256,512]{1,0:T(8,128)S(1)} custom-call(s32[7]{0:T(128)S(1)} %concatenate.10.info, f32[64,512]{1,0:T(8,128)S(1)} %project.3.y0, f32[64,512]{1,0:T(8,128)S(1)} %project.4.y1, f32[64,512]{1,0:T(8,128)S(1)} %project.5.y3, bf16[64,4096]{1,0:T(8,128)(2,1)S(1)} %collective-permute-done.21.x_ref, bf16[4096,512]{1,0:T(8,128)(2,1)S(1)} %copy-done), custom_call_target="tpu_custom_call" | custom-call | tf_op jit(solution)/shard_map/place/pallas_call | solution.py:303
  103.7 1.5 %collective-permute-done.22 = f32[128,512]{1,0:T(8,128)S(1)} collective-permute-done((f32[128,512]{1,0:T(8,128)S(1)}, f32[128,512]{1,0:T(8,128)S(1)}, u32[]{:S(2)}, u32[]{:S(2)}) %collective-permute-start.22) | collective-permute-done | bytes 262176 | tf_op jit(solution)/shard_map/ppermute | solution.py:32
  105.3 1.2 %collective-permute-start.23 = (bf16[64,512]{1,0:T(8,128)(2,1)S(1)}, bf16[64,512]{1,0:T(8,128)(2,1)S(1)}, u32[]{:S(2)}, u32[]{:S(2)}) collective-permute-start(bf16[64,512]{1,0:T(8,128)(2,1)S(1)} %slice.40), channel_id=1, source_target_pairs={{0,2},{1,3},{2,0},{3,1},{4,6},{5,7},{6,4},{7,5},{8,10},{9,11},{10,... | collective-permute-start | bytes 196616 | tf_op jit(solution)/shard_map/ppermute | solution.py:32
  106.5 3.2 %collective-permute-done.23 = bf16[64,512]{1,0:T(8,128)(2,1)S(1)} collective-permute-done((bf16[64,512]{1,0:T(8,128)(2,1)S(1)}, bf16[64,512]{1,0:T(8,128)(2,1)S(1)}, u32[]{:S(2)}, u32[]{:S(2)}) %collective-permute-start.23) | collective-permute-done | bytes 65568 | tf_op jit(solution)/shard_map/ppermute | solution.py:32
  (46 shorter events, 12.2 us)
Async XLA Ops:
  0.0 6.5 %copy-start.1 = (bf16[8,32,128]{2,1,0:T(8,128)(2,1)S(1)}, bf16[8,32,128]{2,1,0:T(8,128)(2,1)}, u32[]{:S(2)}) copy-start(bf16[8,32,128]{2,1,0:T(8,128)(2,1)} %param.6) | copy-start | bytes 196612
  0.0 6.5 %collective-permute-start = (bf16[1,8,32,128]{3,2,1,0:T(8,128)(2,1)}, bf16[1,8,32,128]{3,2,1,0:T(8,128)(2,1)S(1)}, u32[]{:S(2)}, u32[]{:S(2)}) collective-permute-start(bf16[1,8,32,128]{3,2,1,0:T(8,128)(2,1)} %bitcast.10), channel_id=1, source_target_pairs={{0,16},{1,17},{2,18},{3,19},{4,20},{5,21},{6,22},{7,23},{8,24},{9,... | collective-permute-start | bytes 196616 | tf_op jit(solution)/shard_map/ppermute | solution.py:32
  6.6 8.7 %collective-permute-start.1 = (bf16[2,8,32,128]{3,2,1,0:T(8,128)(2,1)S(1)}, bf16[2,8,32,128]{3,2,1,0:T(8,128)(2,1)S(1)}, u32[]{:S(2)}, u32[]{:S(2)}) collective-permute-start(bf16[2,8,32,128]{3,2,1,0:T(8,128)(2,1)S(1)} %pad_maximum_fusion.1), channel_id=1, source_target_pairs={{0,32},{1,5},{2,34},{3,7},{4,36},{5,9},{6,38},{7,11},{8,40},{9,13}... | collective-permute-start | bytes 393224 | tf_op jit(solution)/shard_map/ppermute | solution.py:32
  8.5 7.9 %collective-permute-start.2 = (bf16[2,8,32,128]{3,2,1,0:T(8,128)(2,1)S(1)}, bf16[2,8,32,128]{3,2,1,0:T(8,128)(2,1)S(1)}, u32[]{:S(2)}, u32[]{:S(2)}) collective-permute-start(bf16[2,8,32,128]{3,2,1,0:T(8,128)(2,1)S(1)} %pad_maximum_fusion.1), channel_id=1, source_target_pairs={{0,64},{1,9},{2,66},{3,11},{4,68},{5,13},{6,70},{7,15},{8,72},{9,1... | collective-permute-start | bytes 393224 | tf_op jit(solution)/shard_map/ppermute | solution.py:32
  12.1 5.0 %collective-permute-start.3 = (bf16[2,8,32,128]{3,2,1,0:T(8,128)(2,1)S(1)}, bf16[2,8,32,128]{3,2,1,0:T(8,128)(2,1)S(1)}, u32[]{:S(2)}, u32[]{:S(2)}) collective-permute-start(bf16[2,8,32,128]{3,2,1,0:T(8,128)(2,1)S(1)} %pad_maximum_fusion.1), channel_id=1, source_target_pairs={{0,96},{1,13},{2,98},{3,15},{4,100},{5,1},{6,102},{7,3},{8,104},{9... | collective-permute-start | bytes 393224 | tf_op jit(solution)/shard_map/ppermute | solution.py:32
  17.2 10.9 %collective-permute-start.6 = (bf16[8,8,32,128]{3,2,1,0:T(8,128)(2,1)S(1)}, bf16[8,8,32,128]{3,2,1,0:T(8,128)(2,1)S(1)}, u32[]{:S(2)}, u32[]{:S(2)}) collective-permute-start(bf16[8,8,32,128]{3,2,1,0:T(8,128)(2,1)S(1)} %pad_maximum_fusion.q_ref), channel_id=1, source_target_pairs={{0,8},{1,65},{2,10},{3,67},{4,12},{5,69},{6,14},{7,71},{8,0},{9,73... | collective-permute-start | bytes 1572872 | tf_op jit(solution)/shard_map/ppermute | solution.py:32
  20.3 16.6 %collective-permute-start.4 = (bf16[8,8,32,128]{3,2,1,0:T(8,128)(2,1)S(1)}, bf16[8,8,32,128]{3,2,1,0:T(8,128)(2,1)S(1)}, u32[]{:S(2)}, u32[]{:S(2)}) collective-permute-start(bf16[8,8,32,128]{3,2,1,0:T(8,128)(2,1)S(1)} %pad_maximum_fusion.q_ref), channel_id=1, source_target_pairs={{0,4},{1,33},{2,6},{3,35},{4,8},{5,37},{6,10},{7,39},{8,12},{9,41}... | collective-permute-start | bytes 1572872 | tf_op jit(solution)/shard_map/ppermute | solution.py:32
  20.9 16.0 %collective-permute-start.5 = (bf16[8,8,32,128]{3,2,1,0:T(8,128)(2,1)S(1)}, bf16[8,8,32,128]{3,2,1,0:T(8,128)(2,1)S(1)}, u32[]{:S(2)}, u32[]{:S(2)}) collective-permute-start(bf16[8,8,32,128]{3,2,1,0:T(8,128)(2,1)S(1)} %pad_maximum_fusion.q_ref), channel_id=1, source_target_pairs={{0,12},{1,97},{2,14},{3,99},{4,0},{5,101},{6,2},{7,103},{8,4},{9,1... | collective-permute-start | bytes 1572872 | tf_op jit(solution)/shard_map/ppermute | solution.py:32
  33.6 13.8 %collective-permute-start.7 = (bf16[8,272,128]{2,1,0:T(8,128)(2,1)S(1)}, bf16[8,272,128]{2,1,0:T(8,128)(2,1)S(1)}, u32[]{:S(2)}, u32[]{:S(2)}) collective-permute-start(bf16[8,272,128]{2,1,0:T(8,128)(2,1)S(1)} %attend_plane.7), channel_id=1, source_target_pairs={{0,8},{1,65},{2,10},{3,67},{4,12},{5,69},{6,14},{7,71},{8,0},{9,73... | collective-permute-start | bytes 1671176 | tf_op jit(solution)/shard_map/ppermute | solution.py:32
  42.4 11.8 %collective-permute-start.8 = (bf16[8,272,128]{2,1,0:T(8,128)(2,1)S(1)}, bf16[8,272,128]{2,1,0:T(8,128)(2,1)S(1)}, u32[]{:S(2)}, u32[]{:S(2)}) collective-permute-start(bf16[8,272,128]{2,1,0:T(8,128)(2,1)S(1)} %attend_plane.8), channel_id=1, source_target_pairs={{0,12},{1,97},{2,14},{3,99},{4,0},{5,101},{6,2},{7,103},{8,4},{9,1... | collective-permute-start | bytes 1671176 | tf_op jit(solution)/shard_map/ppermute | solution.py:32
  46.4 7.8 %collective-permute-start.9 = (bf16[4,272,128]{2,1,0:T(8,128)(2,1)S(1)}, bf16[4,272,128]{2,1,0:T(8,128)(2,1)S(1)}, u32[]{:S(2)}, u32[]{:S(2)}) collective-permute-start(bf16[4,272,128]{2,1,0:T(8,128)(2,1)S(1)} %attend_plane.9), channel_id=1, source_target_pairs={{0,4},{1,33},{2,6},{3,35},{4,8},{5,37},{6,10},{7,39},{8,12},{9,41}... | collective-permute-start | bytes 835592 | tf_op jit(solution)/shard_map/ppermute | solution.py:32
  50.1 10.1 %collective-permute-start.11 = (bf16[4,272,128]{2,1,0:T(8,128)(2,1)S(1)}, bf16[4,272,128]{2,1,0:T(8,128)(2,1)S(1)}, u32[]{:S(2)}, u32[]{:S(2)}) collective-permute-start(bf16[4,272,128]{2,1,0:T(8,128)(2,1)S(1)} %attend_plane.10), channel_id=1, source_target_pairs={{0,4},{1,33},{2,6},{3,35},{4,8},{5,37},{6,10},{7,39},{8,12},{9,41}... | collective-permute-start | bytes 835592 | tf_op jit(solution)/shard_map/ppermute | solution.py:32
  54.9 7.2 %collective-permute-start.10 = (bf16[2,272,128]{2,1,0:T(8,128)(2,1)S(1)}, bf16[2,272,128]{2,1,0:T(8,128)(2,1)S(1)}, u32[]{:S(2)}, u32[]{:S(2)}) collective-permute-start(bf16[2,272,128]{2,1,0:T(8,128)(2,1)S(1)} %slice.22), channel_id=1, source_target_pairs={{0,96},{1,13},{2,98},{3,15},{4,100},{5,1},{6,102},{7,3},{8,104},{9... | collective-permute-start | bytes 417800 | tf_op jit(solution)/shard_map/ppermute | solution.py:32
  60.2 27.6 %copy-start = (bf16[4096,512]{1,0:T(8,128)(2,1)S(1)}, bf16[4096,512]{1,0:T(8,128)(2,1)}, u32[]{:S(2)}) copy-start(bf16[4096,512]{1,0:T(8,128)(2,1)} %w_ref.7) | copy-start | bytes 12582916
  60.9 6.7 %collective-permute-start.12 = (bf16[2,272,128]{2,1,0:T(8,128)(2,1)S(1)}, bf16[2,272,128]{2,1,0:T(8,128)(2,1)S(1)}, u32[]{:S(2)}, u32[]{:S(2)}) collective-permute-start(bf16[2,272,128]{2,1,0:T(8,128)(2,1)S(1)} %get-tuple-element.60), channel_id=1, source_target_pairs={{0,64},{1,9},{2,66},{3,11},{4,68},{5,13},{6,70},{7,15},{8,72},{9,1... | collective-permute-start | bytes 417800 | tf_op jit(solution)/shard_map/ppermute | solution.py:32
  61.8 7.3 %collective-permute-start.13 = (bf16[2,272,128]{2,1,0:T(8,128)(2,1)S(1)}, bf16[2,272,128]{2,1,0:T(8,128)(2,1)S(1)}, u32[]{:S(2)}, u32[]{:S(2)}) collective-permute-start(bf16[2,272,128]{2,1,0:T(8,128)(2,1)S(1)} %get-tuple-element.59), channel_id=1, source_target_pairs={{0,32},{1,5},{2,34},{3,7},{4,36},{5,9},{6,38},{7,11},{8,40},{9,13}... | collective-permute-start | bytes 417800 | tf_op jit(solution)/shard_map/ppermute | solution.py:32
  69.5 6.6 %collective-permute-start.14 = (bf16[2,272,128]{2,1,0:T(8,128)(2,1)S(1)}, bf16[2,272,128]{2,1,0:T(8,128)(2,1)S(1)}, u32[]{:S(2)}, u32[]{:S(2)}) collective-permute-start(bf16[2,272,128]{2,1,0:T(8,128)(2,1)S(1)} %combine.5.mine), channel_id=1, source_target_pairs={{0,16},{1,17},{2,18},{3,19},{4,20},{5,21},{6,22},{7,23},{8,24},{9,... | collective-permute-start | bytes 417800 | tf_op jit(solution)/shard_map/ppermute | solution.py:32
  76.4 6.7 %collective-permute-start.16 = (bf16[16,4096]{1,0:T(8,128)(2,1)S(1)}, bf16[16,4096]{1,0:T(8,128)(2,1)S(1)}, u32[]{:S(2)}, u32[]{:S(2)}) collective-permute-start(bf16[16,4096]{1,0:T(8,128)(2,1)S(1)} %finish.1.x0), channel_id=1, source_target_pairs={{0,64},{1,9},{2,66},{3,11},{4,68},{5,13},{6,70},{7,15},{8,72},{9,1... | collective-permute-start | bytes 393224 | tf_op jit(solution)/shard_map/ppermute | solution.py:32
  77.2 7.1 %collective-permute-start.15 = (bf16[16,4096]{1,0:T(8,128)(2,1)S(1)}, bf16[16,4096]{1,0:T(8,128)(2,1)S(1)}, u32[]{:S(2)}, u32[]{:S(2)}) collective-permute-start(bf16[16,4096]{1,0:T(8,128)(2,1)S(1)} %finish.1.x0), channel_id=1, source_target_pairs={{0,32},{1,5},{2,34},{3,7},{4,36},{5,9},{6,38},{7,11},{8,40},{9,13}... | collective-permute-start | bytes 393224 | tf_op jit(solution)/shard_map/ppermute | solution.py:32
  77.9 6.5 %collective-permute-start.17 = (bf16[16,4096]{1,0:T(8,128)(2,1)S(1)}, bf16[16,4096]{1,0:T(8,128)(2,1)S(1)}, u32[]{:S(2)}, u32[]{:S(2)}) collective-permute-start(bf16[16,4096]{1,0:T(8,128)(2,1)S(1)} %finish.1.x0), channel_id=1, source_target_pairs={{0,96},{1,13},{2,98},{3,15},{4,100},{5,1},{6,102},{7,3},{8,104},{9... | collective-permute-start | bytes 393224 | tf_op jit(solution)/shard_map/ppermute | solution.py:32
  83.1 1.3 %collective-permute-start.18 = (bf16[16,4096]{1,0:T(8,128)(2,1)S(1)}, bf16[16,4096]{1,0:T(8,128)(2,1)S(1)}, u32[]{:S(2)}, u32[]{:S(2)}) collective-permute-start(bf16[16,4096]{1,0:T(8,128)(2,1)S(1)} %collective-permute-done.16.x2), channel_id=1, source_target_pairs={{0,1},{1,0},{2,3},{3,2},{4,5},{5,4},{6,7},{7,6},{8,9},{9,8},{10,11... | collective-permute-start | bytes 393224 | tf_op jit(solution)/shard_map/ppermute | solution.py:32
  84.5 16.1 %collective-permute-start.19 = (bf16[64,4096]{1,0:T(8,128)(2,1)S(1)}, bf16[64,4096]{1,0:T(8,128)(2,1)S(1)}, u32[]{:S(2)}, u32[]{:S(2)}) collective-permute-start(bf16[64,4096]{1,0:T(8,128)(2,1)S(1)} %assemble.1.x_ref), channel_id=1, source_target_pairs={{0,4},{1,33},{2,6},{3,35},{4,8},{5,37},{6,10},{7,39},{8,12},{9,41}... | collective-permute-start | bytes 1572872 | tf_op jit(solution)/shard_map/ppermute | solution.py:32
  84.5 16.8 %collective-permute-start.20 = (bf16[64,4096]{1,0:T(8,128)(2,1)S(1)}, bf16[64,4096]{1,0:T(8,128)(2,1)S(1)}, u32[]{:S(2)}, u32[]{:S(2)}) collective-permute-start(bf16[64,4096]{1,0:T(8,128)(2,1)S(1)} %assemble.1.x_ref), channel_id=1, source_target_pairs={{0,12},{1,97},{2,14},{3,99},{4,0},{5,101},{6,2},{7,103},{8,4},{9,1... | collective-permute-start | bytes 1572872 | tf_op jit(solution)/shard_map/ppermute | solution.py:32
  87.8 14.5 %collective-permute-start.21 = (bf16[64,4096]{1,0:T(8,128)(2,1)S(1)}, bf16[64,4096]{1,0:T(8,128)(2,1)S(1)}, u32[]{:S(2)}, u32[]{:S(2)}) collective-permute-start(bf16[64,4096]{1,0:T(8,128)(2,1)S(1)} %assemble.1.x_ref), channel_id=1, source_target_pairs={{0,8},{1,65},{2,10},{3,67},{4,12},{5,69},{6,14},{7,71},{8,0},{9,73... | collective-permute-start | bytes 1572872 | tf_op jit(solution)/shard_map/ppermute | solution.py:32
  103.6 1.6 %collective-permute-start.22 = (f32[128,512]{1,0:T(8,128)S(1)}, f32[128,512]{1,0:T(8,128)S(1)}, u32[]{:S(2)}, u32[]{:S(2)}) collective-permute-start(f32[128,512]{1,0:T(8,128)S(1)} %slice.32), channel_id=1, source_target_pairs={{0,1},{1,0},{2,3},{3,2},{4,5},{5,4},{6,7},{7,6},{8,9},{9,8},{10,11... | collective-permute-start | bytes 786440 | tf_op jit(solution)/shard_map/ppermute | solution.py:32
  105.3 4.3 %collective-permute-start.23 = (bf16[64,512]{1,0:T(8,128)(2,1)S(1)}, bf16[64,512]{1,0:T(8,128)(2,1)S(1)}, u32[]{:S(2)}, u32[]{:S(2)}) collective-permute-start(bf16[64,512]{1,0:T(8,128)(2,1)S(1)} %slice.40), channel_id=1, source_target_pairs={{0,2},{1,3},{2,0},{3,1},{4,6},{5,7},{6,4},{7,5},{8,10},{9,11},{10,... | collective-permute-start | bytes 196616 | tf_op jit(solution)/shard_map/ppermute | solution.py:32

commit v2 on v1

--- a/solution.py
+++ b/solution.py
@@ -249,47 +249,53 @@
     )(mine, theirs)
 
 
-def assemble_kernel(x0, x1, x2, x3, _, o_ref):
-    for i, x in enumerate((x0, x1, x2, x3)):
-        o_ref[i * x.shape[0] : (i + 1) * x.shape[0], :] = x[...]
-
-
-def assemble(*pieces):
-    vmem = pl.BlockSpec(memory_space=pltpu.VMEM)
-    rows, width = pieces[0].shape
-    return pl.pallas_call(
-        assemble_kernel,
-        in_specs=[vmem] * 4 + [pl.BlockSpec(memory_space=pl.ANY)],
-        out_specs=vmem,
-        out_shape=jax.ShapeDtypeStruct((RING * rows, width), pieces[0].dtype),
+def assemble_kernel(*refs, count):
+    at = 0
+    for x in refs[:count]:
+        refs[-1][at : at + x.shape[0], :] = x[...]
+        at += x.shape[0]
+
+
+def assemble(pieces, *others):
+    vmem = pl.BlockSpec(memory_space=pltpu.VMEM)
+    rows, width = sum(p.shape[0] for p in pieces), pieces[0].shape[1]
+    return pl.pallas_call(
+        functools.partial(assemble_kernel, count=len(pieces)),
+        in_specs=[vmem] * len(pieces) + [pl.BlockSpec(memory_space=pl.ANY)] * len(others),
+        out_specs=vmem,
+        out_shape=jax.ShapeDtypeStruct((rows, width), pieces[0].dtype),
         compiler_params=pltpu.CompilerParams(vmem_limit_bytes=4 * MIB),
         name="assemble",
-    )(*pieces)
-
-
-def project_kernel(x_ref, w_ref, o_ref):
-    o_ref[...] = jnp.dot(x_ref[...], w_ref[...], preferred_element_type=jnp.float32)
-
-
-def project(x, w):
-    vmem = pl.BlockSpec(memory_space=pltpu.VMEM)
+    )(*pieces, *others)
+
+
+def times_weight(halves, w_ref):
+    x = jnp.concatenate([h[...] for h in halves], axis=0)
+    return jnp.dot(x, w_ref[...], preferred_element_type=jnp.float32)
+
+
+def project_kernel(xa, xb, w_ref, o_ref):
+    o_ref[...] = times_weight((xa, xb), w_ref)
+
+
+def project(xa, xb, w):
+    vmem = pl.BlockSpec(memory_space=pltpu.VMEM)
+    rows = xa.shape[0] + xb.shape[0]
     return pl.pallas_call(
         project_kernel,
-        in_specs=[vmem, vmem],
-        out_specs=vmem,
-        out_shape=jax.ShapeDtypeStruct((x.shape[0], w.shape[1]), jnp.float32),
+        in_specs=[vmem] * 3,
+        out_specs=vmem,
+        out_shape=jax.ShapeDtypeStruct((rows, w.shape[1]), jnp.float32),
         compiler_params=pltpu.CompilerParams(vmem_limit_bytes=8 * MIB),
-        cost_estimate=pl.CostEstimate(
-            flops=8 * x.shape[0] * w.shape[0] * w.shape[1], bytes_accessed=4 * MIB, transcendentals=0
-        ),
+        cost_estimate=pl.CostEstimate(flops=2 * rows * w.shape[0] * w.shape[1], bytes_accessed=MIB, transcendentals=0),
         name="project",
-    )(x, w)
-
-
-def place_kernel(info, y0, y1, y3, x_ref, w_ref, o_ref):
+    )(xa, xb, w)
+
+
+def place_kernel(info, y0, y1, y3, xa, xb, w_ref, o_ref):
     me = tuple(info[i] for i in range(5))
     yl, core = me[3], me[4]
-    y2 = jnp.dot(x_ref[...], w_ref[...], preferred_element_type=jnp.float32)
+    y2 = times_weight((xa, xb), w_ref)
     for db, y in ((0, y0), (1, y1), (2, y2), (3, y3)):
         for da, dy in itertools.product(range(RING), range(2)):
             z, yh, xx = source(me, da, db, dy)
@@ -298,16 +304,16 @@
             o_ref[pl.ds(pl.multiple_of(row, 8), 8), :] = y[at : at + 8, :]
 
 
-def place(info, y0, y1, y3, x, w):
+def place(info, y0, y1, y3, xa, xb, w):
     vmem = pl.BlockSpec(memory_space=pltpu.VMEM)
     return pl.pallas_call(
         place_kernel,
-        in_specs=[pl.BlockSpec(memory_space=pltpu.SMEM)] + [vmem] * 5,
+        in_specs=[pl.BlockSpec(memory_space=pltpu.SMEM)] + [vmem] * 6,
         out_specs=vmem,
         out_shape=jax.ShapeDtypeStruct((RING * y0.shape[0], w.shape[1]), jnp.float32),
         compiler_params=pltpu.CompilerParams(vmem_limit_bytes=8 * MIB),
         name="place",
-    )(info, y0, y1, y3, x, w)
+    )(info, y0, y1, y3, xa, xb, w)
 
 
 def on_device(queries, keys, values, lengths, start, out_weight):
@@ -349,9 +355,13 @@
     c = combine(2, (low, 0), (s1, 0), (s2, 0), (s3, 0))
     attn = finish(c, moved(c, yh=1))
     x2, x1, x3 = (moved(attn, a=d) for d in (2, 1, 3))
-    attn = assemble(attn, x1, x2, x3, moved(x2, core=1))
-    x1, x3, x2 = (moved(attn, b=d) for d in (1, 3, 2))
-    y = place(info, project(attn, out_weight), project(x1, out_weight), project(x3, out_weight), x2, out_weight)
+    low = assemble([attn, x1], moved(x2, core=1))
+    high = assemble([x2, x3])
+    x1a, x3b = moved(low, b=1), moved(high, b=3)
+    x1b, x3a = moved(high, b=1), moved(low, b=3)
+    x2a, x2b = moved(x1a, b=1), moved(x3b, b=3)
+    ys = [project(xa, xb, out_weight) for xa, xb in ((low, high), (x1a, x1b), (x3a, x3b))]
+    y = place(info, *ys, x2a, x2b, out_weight)
     y = y[:128] + moved(y[128:], core=1)
     y = y[:64] + moved(y[64:].astype(jnp.bfloat16), yl=1).astype(jnp.float32)
     return y.astype(jnp.bfloat16)

time: 110 us -> 108 us (0.982)
  waiting for transfers between devices: 38.3 us -> 35.2 us
    ppermute x24 -> x27, waiting for transfers between devices: 38.3 us -> 35.2 us  [moved(): return lax.ppermute(x, ('cp', 'tp'), pairs)]
    ppermute x24 -> x27, starting transfers between devices: 37.4 us -> 38.1 us  [moved(): return lax.ppermute(x, ('cp', 'tp'), pairs)]
    pallas_call x4 -> x5, Pallas kernels: 2.53 us -> 2.56 us  [the longest x3 2.53 us: project(): pl.pallas_call(project_kernel, in_specs=[vmem] * 3, out_specs=vmem, out_s...]
  transfers between devices with their start and end apart: 24 -> 27, of which waited for: 12 -> 15; matrix products, arithmetic and copies ran while one was open for 2% -> 2% of each run, Pallas kernels for 26% -> 26%
where the time goes in v2:
time: 108 us
  starting transfers between devices  38.1 us (35%)
  waiting for transfers between devices  35.2 us (33%)
  Pallas kernels  30.3 us (28%)
  local copies, waits for them, and re-layouts  1.97 us (2%)
  between operations  1.6 us (1%)
    ppermute x27, starting transfers between devices, moved(): return lax.ppermute(x, ('cp', 'tp'), pairs)  38.1 us
    ppermute x27, waiting for transfers between devices, moved(): return lax.ppermute(x, ('cp', 'tp'), pairs)  35.2 us
    pallas_call x6, Pallas kernels, attend(): pl.pallas_call(functools.partial(attend_kernel, kvs=kvs, first=first, nb=...  22.1 us
    pallas_call x3, Pallas kernels, project(): pl.pallas_call(project_kernel, in_specs=[vmem] * 3, out_specs=vmem, out_s...  2.53 us
    pallas_call x1, Pallas kernels, prepare(): pl.pallas_call(prepare_kernel, in_specs=[pl.BlockSpec(memory_space=pltpu....  2.16 us
  transfers between devices with their start and end apart: 27, of which 15 were waited for; matrix products, arithmetic and copies ran while one was open for 2% of the time, Pallas kernels for 26%

profile of v2, /device:TPU:0, one launch (start us, length us, event | category | flops | bytes accessed | tf_op | source)
XLA Modules:
  0.0 107.9 jit_solution(6447430559412505524)
XLA Ops:
  0.0 3.3 %collective-permute-start = (bf16[1,8,32,128]{3,2,1,0:T(8,128)(2,1)}, bf16[1,8,32,128]{3,2,1,0:T(8,128)(2,1)S(1)}, u32[]{:S(2)}, u32[]{:S(2)}) collective-permute-start(bf16[1,8,32,128]{3,2,1,0:T(8,128)(2,1)} %bitcast.10), channel_id=1, source_target_pairs={{0,16},{1,17},{2,18},{3,19},{4,20},{5,21},{6,22},{7,23},{8,24},{9,... | collective-permute-start | bytes 196616 | tf_op jit(solution)/shard_map/ppermute | solution.py:32
  3.3 1.8 %copy_bitcast_fusion = (bf16[2,2048,128]{2,1,0:T(8,128)(2,1)S(1)}, bf16[2,2048,128]{2,1,0:T(8,128)(2,1)S(1)}) fusion(bf16[2048,2,128]{2,1,0:T(2,128)(2,1)} %param.8, bf16[2048,2,128]{2,1,0:T(2,128)(2,1)} %param.7), kind=kLoop, calls=%fused_computation | loop fusion | bytes 4194304 | tf_op jit(solution)/shard_map/transpose | solution.py:324
  6.6 2.0 %collective-permute-start.1 = (bf16[2,8,32,128]{3,2,1,0:T(8,128)(2,1)S(1)}, bf16[2,8,32,128]{3,2,1,0:T(8,128)(2,1)S(1)}, u32[]{:S(2)}, u32[]{:S(2)}) collective-permute-start(bf16[2,8,32,128]{3,2,1,0:T(8,128)(2,1)S(1)} %pad_maximum_fusion.1), channel_id=1, source_target_pairs={{0,32},{1,5},{2,34},{3,7},{4,36},{5,9},{6,38},{7,11},{8,40},{9,13}... | collective-permute-start | bytes 393224 | tf_op jit(solution)/shard_map/ppermute | solution.py:32
  8.5 3.6 %collective-permute-start.2 = (bf16[2,8,32,128]{3,2,1,0:T(8,128)(2,1)S(1)}, bf16[2,8,32,128]{3,2,1,0:T(8,128)(2,1)S(1)}, u32[]{:S(2)}, u32[]{:S(2)}) collective-permute-start(bf16[2,8,32,128]{3,2,1,0:T(8,128)(2,1)S(1)} %pad_maximum_fusion.1), channel_id=1, source_target_pairs={{0,64},{1,9},{2,66},{3,11},{4,68},{5,13},{6,70},{7,15},{8,72},{9,1... | collective-permute-start | bytes 393224 | tf_op jit(solution)/shard_map/ppermute | solution.py:32
  13.1 2.2 %prepare.1 = (bf16[2,2048,256]{2,1,0:T(8,128)(2,1)S(1)}, bf16[2,2048,256]{2,1,0:T(8,128)(2,1)S(1)}, bf16[2,2048,256]{2,1,0:T(8,128)(2,1)S(1)}, bf16[2,2048,256]{...) custom-call(s32[7]{0:T(128)S(1)} %concatenate.10.info, bf16[2,2048,128]{2,1,0:T(8,128)(2,1)S(1)} %get-tuple-element.34.k_ref, ...), custom_call_target="tpu_custom_call" | custom-call | tf_op jit(solution)/shard_map/prepare/pallas_call | solution.py:87
  17.2 3.1 %collective-permute-start.6 = (bf16[8,8,32,128]{3,2,1,0:T(8,128)(2,1)S(1)}, bf16[8,8,32,128]{3,2,1,0:T(8,128)(2,1)S(1)}, u32[]{:S(2)}, u32[]{:S(2)}) collective-permute-start(bf16[8,8,32,128]{3,2,1,0:T(8,128)(2,1)S(1)} %pad_maximum_fusion.q_ref), channel_id=1, source_target_pairs={{0,8},{1,65},{2,10},{3,67},{4,12},{5,69},{6,14},{7,71},{8,0},{9,73... | collective-permute-start | bytes 1572872 | tf_op jit(solution)/shard_map/ppermute | solution.py:32
  20.9 2.6 %collective-permute-start.5 = (bf16[8,8,32,128]{3,2,1,0:T(8,128)(2,1)S(1)}, bf16[8,8,32,128]{3,2,1,0:T(8,128)(2,1)S(1)}, u32[]{:S(2)}, u32[]{:S(2)}) collective-permute-start(bf16[8,8,32,128]{3,2,1,0:T(8,128)(2,1)S(1)} %pad_maximum_fusion.q_ref), channel_id=1, source_target_pairs={{0,12},{1,97},{2,14},{3,99},{4,0},{5,101},{6,2},{7,103},{8,4},{9,1... | collective-permute-start | bytes 1572872 | tf_op jit(solution)/shard_map/ppermute | solution.py:32
  23.5 2.8 %attend_plane.6.refs_0_ = bf16[4,272,128]{2,1,0:T(8,128)(2,1)S(1)} custom-call(bf16[8,8,32,128]{3,2,1,0:T(8,128)(2,1)S(1)} %pad_maximum_fusion.q_ref, bf16[2,2048,256]{2,1,0:T(8,128)(2,1)S(1)} %get-tuple-element.42.kx, bf16[2,2048,256]{2,1,0:T(8,128)(2,1)S(1)} %get-tuple-element.43.vx), custom_call_target="tpu_custom_call" | custom-call | flops 2147483648 | bytes 4194304 | tf_op jit(solution)/shard_map/attend_plane/pallas_call | solution.py:168
  26.3 1.8 %collective-permute-done.6.q_ref = bf16[8,8,32,128]{3,2,1,0:T(8,128)(2,1)S(1)} collective-permute-done((bf16[8,8,32,128]{3,2,1,0:T(8,128)(2,1)S(1)}, bf16[8,8,32,128]{3,2,1,0:T(8,128)(2,1)S(1)}, u32[]{:S(2)}, u32[]{:S(2)}) %collective-permute-start.6) | collective-permute-done | bytes 524320 | tf_op jit(solution)/shard_map/ppermute | solution.py:32
  28.0 5.5 %attend_plane.7 = bf16[8,272,128]{2,1,0:T(8,128)(2,1)S(1)} custom-call(bf16[8,8,32,128]{3,2,1,0:T(8,128)(2,1)S(1)} %collective-permute-done.6.q_ref, bf16[2,2048,256]{2,1,0:T(8,128)(2,1)S(1)} %get-tuple-element.45.kx, bf16[2,2048,256]{2,1,0:T(8,128)(2,1)S(1)} %get-tuple-element.43.vx), custom_call_target="tpu_custom_call" | custom-call | flops 4294967296 | bytes 4194304 | tf_op jit(solution)/shard_map/attend_plane/pallas_call | solution.py:168
  33.6 3.3 %collective-permute-start.7 = (bf16[8,272,128]{2,1,0:T(8,128)(2,1)S(1)}, bf16[8,272,128]{2,1,0:T(8,128)(2,1)S(1)}, u32[]{:S(2)}, u32[]{:S(2)}) collective-permute-start(bf16[8,272,128]{2,1,0:T(8,128)(2,1)S(1)} %attend_plane.7), channel_id=1, source_target_pairs={{0,8},{1,65},{2,10},{3,67},{4,12},{5,69},{6,14},{7,71},{8,0},{9,73... | collective-permute-start | bytes 1671176 | tf_op jit(solution)/shard_map/ppermute | solution.py:32
  36.9 5.5 %attend_plane.8 = bf16[8,272,128]{2,1,0:T(8,128)(2,1)S(1)} custom-call(bf16[8,8,32,128]{3,2,1,0:T(8,128)(2,1)S(1)} %collective-permute-done.4.q_ref, bf16[2,2048,256]{2,1,0:T(8,128)(2,1)S(1)} %get-tuple-element.48.kx, bf16[2,2048,256]{2,1,0:T(8,128)(2,1)S(1)} %get-tuple-element.43.vx), custom_call_target="tpu_custom_call" | custom-call | flops 4294967296 | bytes 4194304 | tf_op jit(solution)/shard_map/attend_plane/pallas_call | solution.py:168
  42.4 1.2 %collective-permute-start.8 = (bf16[8,272,128]{2,1,0:T(8,128)(2,1)S(1)}, bf16[8,272,128]{2,1,0:T(8,128)(2,1)S(1)}, u32[]{:S(2)}, u32[]{:S(2)}) collective-permute-start(bf16[8,272,128]{2,1,0:T(8,128)(2,1)S(1)} %attend_plane.8), channel_id=1, source_target_pairs={{0,12},{1,97},{2,14},{3,99},{4,0},{5,101},{6,2},{7,103},{8,4},{9,1... | collective-permute-start | bytes 1671176 | tf_op jit(solution)/shard_map/ppermute | solution.py:32
  43.6 2.8 %attend_plane.9 = bf16[4,272,128]{2,1,0:T(8,128)(2,1)S(1)} custom-call(bf16[8,8,32,128]{3,2,1,0:T(8,128)(2,1)S(1)} %collective-permute-done.5.q_ref, bf16[2,2048,256]{2,1,0:T(8,128)(2,1)S(1)} %get-tuple-element.50.kx, bf16[2,2048,256]{2,1,0:T(8,128)(2,1)S(1)} %get-tuple-element.43.vx), custom_call_target="tpu_custom_call" | custom-call | flops 2147483648 | bytes 4194304 | tf_op jit(solution)/shard_map/attend_plane/pallas_call | solution.py:168
  47.4 2.8 %attend_plane.10 = bf16[4,272,128]{2,1,0:T(8,128)(2,1)S(1)} custom-call(bf16[8,8,32,128]{3,2,1,0:T(8,128)(2,1)S(1)} %collective-permute-done.5.q_ref, bf16[2,2048,256]{2,1,0:T(8,128)(2,1)S(1)} %get-tuple-element.50.kx, bf16[2,2048,256]{2,1,0:T(8,128)(2,1)S(1)} %get-tuple-element.43.vx), custom_call_target="tpu_custom_call" | custom-call | flops 2147483648 | bytes 4194304 | tf_op jit(solution)/shard_map/attend_plane/pallas_call | solution.py:168
  50.8 3.4 %collective-permute-done.9.refs_3_ = bf16[4,272,128]{2,1,0:T(8,128)(2,1)S(1)} collective-permute-done((bf16[4,272,128]{2,1,0:T(8,128)(2,1)S(1)}, bf16[4,272,128]{2,1,0:T(8,128)(2,1)S(1)}, u32[]{:S(2)}, u32[]{:S(2)}) %collective-permute-start.9) | collective-permute-done | bytes 278560 | tf_op jit(solution)/shard_map/ppermute | solution.py:32
  54.9 2.5 %collective-permute-start.10 = (bf16[2,272,128]{2,1,0:T(8,128)(2,1)S(1)}, bf16[2,272,128]{2,1,0:T(8,128)(2,1)S(1)}, u32[]{:S(2)}, u32[]{:S(2)}) collective-permute-start(bf16[2,272,128]{2,1,0:T(8,128)(2,1)S(1)} %slice.22), channel_id=1, source_target_pairs={{0,96},{1,13},{2,98},{3,15},{4,100},{5,1},{6,102},{7,3},{8,104},{9... | collective-permute-start | bytes 417800 | tf_op jit(solution)/shard_map/ppermute | solution.py:32
  57.4 2.8 %attend_plane.11.refs_0_ = bf16[4,272,128]{2,1,0:T(8,128)(2,1)S(1)} custom-call(bf16[8,8,32,128]{3,2,1,0:T(8,128)(2,1)S(1)} %pad_maximum_fusion.q_ref, bf16[2,2048,256]{2,1,0:T(8,128)(2,1)S(1)} %get-tuple-element.42.kx, bf16[2,2048,256]{2,1,0:T(8,128)(2,1)S(1)} %get-tuple-element.43.vx), custom_call_target="tpu_custom_call" | custom-call | flops 2147483648 | bytes 4194304 | tf_op jit(solution)/shard_map/attend_plane/pallas_call | solution.py:168
  62.1 5.6 %collective-permute-done.12.refs_2_ = bf16[2,272,128]{2,1,0:T(8,128)(2,1)S(1)} collective-permute-done((bf16[2,272,128]{2,1,0:T(8,128)(2,1)S(1)}, bf16[2,272,128]{2,1,0:T(8,128)(2,1)S(1)}, u32[]{:S(2)}, u32[]{:S(2)}) %collective-permute-start.12) | collective-permute-done | bytes 139296 | tf_op jit(solution)/shard_map/ppermute | solution.py:32
  67.7 1.4 %collective-permute-done.13.refs_3_ = bf16[2,272,128]{2,1,0:T(8,128)(2,1)S(1)} collective-permute-done((bf16[2,272,128]{2,1,0:T(8,128)(2,1)S(1)}, bf16[2,272,128]{2,1,0:T(8,128)(2,1)S(1)}, u32[]{:S(2)}, u32[]{:S(2)}) %collective-permute-start.13) | collective-permute-done | bytes 139296 | tf_op jit(solution)/shard_map/ppermute | solution.py:32
  69.5 2.8 %collective-permute-start.14 = (bf16[2,272,128]{2,1,0:T(8,128)(2,1)S(1)}, bf16[2,272,128]{2,1,0:T(8,128)(2,1)S(1)}, u32[]{:S(2)}, u32[]{:S(2)}) collective-permute-start(bf16[2,272,128]{2,1,0:T(8,128)(2,1)S(1)} %combine.5.mine), channel_id=1, source_target_pairs={{0,16},{1,17},{2,18},{3,19},{4,20},{5,21},{6,22},{7,23},{8,24},{9,... | collective-permute-start | bytes 417800 | tf_op jit(solution)/shard_map/ppermute | solution.py:32
  72.3 3.8 %collective-permute-done.14.theirs = bf16[2,272,128]{2,1,0:T(8,128)(2,1)S(1)} collective-permute-done((bf16[2,272,128]{2,1,0:T(8,128)(2,1)S(1)}, bf16[2,272,128]{2,1,0:T(8,128)(2,1)S(1)}, u32[]{:S(2)}, u32[]{:S(2)}) %collective-permute-start.14) | collective-permute-done | bytes 139296 | tf_op jit(solution)/shard_map/ppermute | solution.py:32
  79.3 3.7 %collective-permute-done.16.refs_0_ = bf16[16,4096]{1,0:T(8,128)(2,1)S(1)} collective-permute-done((bf16[16,4096]{1,0:T(8,128)(2,1)S(1)}, bf16[16,4096]{1,0:T(8,128)(2,1)S(1)}, u32[]{:S(2)}, u32[]{:S(2)}) %collective-permute-start.16) | collective-permute-done | bytes 131104 | tf_op jit(solution)/shard_map/ppermute | solution.py:32
  83.2 1.4 %collective-permute-done.15.refs_1_ = bf16[16,4096]{1,0:T(8,128)(2,1)S(1)} collective-permute-done((bf16[16,4096]{1,0:T(8,128)(2,1)S(1)}, bf16[16,4096]{1,0:T(8,128)(2,1)S(1)}, u32[]{:S(2)}, u32[]{:S(2)}) %collective-permute-start.15) | collective-permute-done | bytes 131104 | tf_op jit(solution)/shard_map/ppermute | solution.py:32
  85.2 2.7 %collective-permute-start.21 = (bf16[32,4096]{1,0:T(8,128)(2,1)S(1)}, bf16[32,4096]{1,0:T(8,128)(2,1)S(1)}, u32[]{:S(2)}, u32[]{:S(2)}) collective-permute-start(bf16[32,4096]{1,0:T(8,128)(2,1)S(1)} %assemble.2.xa), channel_id=1, source_target_pairs={{0,12},{1,97},{2,14},{3,99},{4,0},{5,101},{6,2},{7,103},{8,4},{9,1... | collective-permute-start | bytes 786440 | tf_op jit(solution)/shard_map/ppermute | solution.py:32
  87.9 1.5 %collective-permute-done.22.xb = bf16[32,4096]{1,0:T(8,128)(2,1)S(1)} collective-permute-done((bf16[32,4096]{1,0:T(8,128)(2,1)S(1)}, bf16[32,4096]{1,0:T(8,128)(2,1)S(1)}, u32[]{:S(2)}, u32[]{:S(2)}) %collective-permute-start.22) | collective-permute-done | bytes 262176 | tf_op jit(solution)/shard_map/ppermute | solution.py:32
  89.4 1.7 %collective-permute-start.24 = (bf16[32,4096]{1,0:T(8,128)(2,1)S(1)}, bf16[32,4096]{1,0:T(8,128)(2,1)S(1)}, u32[]{:S(2)}, u32[]{:S(2)}) collective-permute-start(bf16[32,4096]{1,0:T(8,128)(2,1)S(1)} %collective-permute-done.22.xb), channel_id=1, source_target_pairs={{0,12},{1,97},{2,14},{3,99},{4,0},{5,101},{6,2},{7,103},{8,4},{9,1... | collective-permute-start | bytes 786440 | tf_op jit(solution)/shard_map/ppermute | solution.py:32
  94.0 1.5 %collective-permute-done.20.xb = bf16[32,4096]{1,0:T(8,128)(2,1)S(1)} collective-permute-done((bf16[32,4096]{1,0:T(8,128)(2,1)S(1)}, bf16[32,4096]{1,0:T(8,128)(2,1)S(1)}, u32[]{:S(2)}, u32[]{:S(2)}) %collective-permute-start.20) | collective-permute-done | bytes 262176 | tf_op jit(solution)/shard_map/ppermute | solution.py:32
  96.4 3.5 %collective-permute-done.23.xa = bf16[32,4096]{1,0:T(8,128)(2,1)S(1)} collective-permute-done((bf16[32,4096]{1,0:T(8,128)(2,1)S(1)}, bf16[32,4096]{1,0:T(8,128)(2,1)S(1)}, u32[]{:S(2)}, u32[]{:S(2)}) %collective-permute-start.23) | collective-permute-done | bytes 262176 | tf_op jit(solution)/shard_map/ppermute | solution.py:32
  99.9 1.4 %place.1 = f32[256,512]{1,0:T(8,128)S(1)} custom-call(s32[7]{0:T(128)S(1)} %concatenate.10.info, f32[64,512]{1,0:T(8,128)S(1)} %project.3.y0, f32[64,512]{1,0:T(8,128)S(1)} %project.4.y1, f32[64,512]{1,0:T(8,128)S(1)} %project.5.y3, bf16[32,4096]{1,0:T(8,128)(2,1)S(1)} %collective-permute-done.23.xa, bf16[32,4096]{1,0:T(8,128)(2,1)S(1)} %collective-permute-done.24.xb, ...), custom_call_target="tpu_custom_call" | custom-call | tf_op jit(solution)/shard_map/place/pallas_call | solution.py:309
  101.4 1.5 %collective-permute-done.25 = f32[128,512]{1,0:T(8,128)S(1)} collective-permute-done((f32[128,512]{1,0:T(8,128)S(1)}, f32[128,512]{1,0:T(8,128)S(1)}, u32[]{:S(2)}, u32[]{:S(2)}) %collective-permute-start.25) | collective-permute-done | bytes 262176 | tf_op jit(solution)/shard_map/ppermute | solution.py:32
  104.1 3.2 %collective-permute-done.26 = bf16[64,512]{1,0:T(8,128)(2,1)S(1)} collective-permute-done((bf16[64,512]{1,0:T(8,128)(2,1)S(1)}, bf16[64,512]{1,0:T(8,128)(2,1)S(1)}, u32[]{:S(2)}, u32[]{:S(2)}) %collective-permute-start.26) | collective-permute-done | bytes 65568 | tf_op jit(solution)/shard_map/ppermute | solution.py:32
  (53 shorter events, 17.7 us)
Async XLA Ops:
  0.0 6.5 %copy-start.1 = (bf16[8,32,128]{2,1,0:T(8,128)(2,1)S(1)}, bf16[8,32,128]{2,1,0:T(8,128)(2,1)}, u32[]{:S(2)}) copy-start(bf16[8,32,128]{2,1,0:T(8,128)(2,1)} %param.6) | copy-start | bytes 196612
  0.0 6.5 %collective-permute-start = (bf16[1,8,32,128]{3,2,1,0:T(8,128)(2,1)}, bf16[1,8,32,128]{3,2,1,0:T(8,128)(2,1)S(1)}, u32[]{:S(2)}, u32[]{:S(2)}) collective-permute-start(bf16[1,8,32,128]{3,2,1,0:T(8,128)(2,1)} %bitcast.10), channel_id=1, source_target_pairs={{0,16},{1,17},{2,18},{3,19},{4,20},{5,21},{6,22},{7,23},{8,24},{9,... | collective-permute-start | bytes 196616 | tf_op jit(solution)/shard_map/ppermute | solution.py:32
  6.6 8.7 %collective-permute-start.1 = (bf16[2,8,32,128]{3,2,1,0:T(8,128)(2,1)S(1)}, bf16[2,8,32,128]{3,2,1,0:T(8,128)(2,1)S(1)}, u32[]{:S(2)}, u32[]{:S(2)}) collective-permute-start(bf16[2,8,32,128]{3,2,1,0:T(8,128)(2,1)S(1)} %pad_maximum_fusion.1), channel_id=1, source_target_pairs={{0,32},{1,5},{2,34},{3,7},{4,36},{5,9},{6,38},{7,11},{8,40},{9,13}... | collective-permute-start | bytes 393224 | tf_op jit(solution)/shard_map/ppermute | solution.py:32
  8.5 7.9 %collective-permute-start.2 = (bf16[2,8,32,128]{3,2,1,0:T(8,128)(2,1)S(1)}, bf16[2,8,32,128]{3,2,1,0:T(8,128)(2,1)S(1)}, u32[]{:S(2)}, u32[]{:S(2)}) collective-permute-start(bf16[2,8,32,128]{3,2,1,0:T(8,128)(2,1)S(1)} %pad_maximum_fusion.1), channel_id=1, source_target_pairs={{0,64},{1,9},{2,66},{3,11},{4,68},{5,13},{6,70},{7,15},{8,72},{9,1... | collective-permute-start | bytes 393224 | tf_op jit(solution)/shard_map/ppermute | solution.py:32
  12.1 5.0 %collective-permute-start.3 = (bf16[2,8,32,128]{3,2,1,0:T(8,128)(2,1)S(1)}, bf16[2,8,32,128]{3,2,1,0:T(8,128)(2,1)S(1)}, u32[]{:S(2)}, u32[]{:S(2)}) collective-permute-start(bf16[2,8,32,128]{3,2,1,0:T(8,128)(2,1)S(1)} %pad_maximum_fusion.1), channel_id=1, source_target_pairs={{0,96},{1,13},{2,98},{3,15},{4,100},{5,1},{6,102},{7,3},{8,104},{9... | collective-permute-start | bytes 393224 | tf_op jit(solution)/shard_map/ppermute | solution.py:32
  17.2 10.9 %collective-permute-start.6 = (bf16[8,8,32,128]{3,2,1,0:T(8,128)(2,1)S(1)}, bf16[8,8,32,128]{3,2,1,0:T(8,128)(2,1)S(1)}, u32[]{:S(2)}, u32[]{:S(2)}) collective-permute-start(bf16[8,8,32,128]{3,2,1,0:T(8,128)(2,1)S(1)} %pad_maximum_fusion.q_ref), channel_id=1, source_target_pairs={{0,8},{1,65},{2,10},{3,67},{4,12},{5,69},{6,14},{7,71},{8,0},{9,73... | collective-permute-start | bytes 1572872 | tf_op jit(solution)/shard_map/ppermute | solution.py:32
  20.3 16.6 %collective-permute-start.4 = (bf16[8,8,32,128]{3,2,1,0:T(8,128)(2,1)S(1)}, bf16[8,8,32,128]{3,2,1,0:T(8,128)(2,1)S(1)}, u32[]{:S(2)}, u32[]{:S(2)}) collective-permute-start(bf16[8,8,32,128]{3,2,1,0:T(8,128)(2,1)S(1)} %pad_maximum_fusion.q_ref), channel_id=1, source_target_pairs={{0,4},{1,33},{2,6},{3,35},{4,8},{5,37},{6,10},{7,39},{8,12},{9,41}... | collective-permute-start | bytes 1572872 | tf_op jit(solution)/shard_map/ppermute | solution.py:32
  20.9 16.0 %collective-permute-start.5 = (bf16[8,8,32,128]{3,2,1,0:T(8,128)(2,1)S(1)}, bf16[8,8,32,128]{3,2,1,0:T(8,128)(2,1)S(1)}, u32[]{:S(2)}, u32[]{:S(2)}) collective-permute-start(bf16[8,8,32,128]{3,2,1,0:T(8,128)(2,1)S(1)} %pad_maximum_fusion.q_ref), channel_id=1, source_target_pairs={{0,12},{1,97},{2,14},{3,99},{4,0},{5,101},{6,2},{7,103},{8,4},{9,1... | collective-permute-start | bytes 1572872 | tf_op jit(solution)/shard_map/ppermute | solution.py:32
  33.6 13.8 %collective-permute-start.7 = (bf16[8,272,128]{2,1,0:T(8,128)(2,1)S(1)}, bf16[8,272,128]{2,1,0:T(8,128)(2,1)S(1)}, u32[]{:S(2)}, u32[]{:S(2)}) collective-permute-start(bf16[8,272,128]{2,1,0:T(8,128)(2,1)S(1)} %attend_plane.7), channel_id=1, source_target_pairs={{0,8},{1,65},{2,10},{3,67},{4,12},{5,69},{6,14},{7,71},{8,0},{9,73... | collective-permute-start | bytes 1671176 | tf_op jit(solution)/shard_map/ppermute | solution.py:32
  42.4 11.8 %collective-permute-start.8 = (bf16[8,272,128]{2,1,0:T(8,128)(2,1)S(1)}, bf16[8,272,128]{2,1,0:T(8,128)(2,1)S(1)}, u32[]{:S(2)}, u32[]{:S(2)}) collective-permute-start(bf16[8,272,128]{2,1,0:T(8,128)(2,1)S(1)} %attend_plane.8), channel_id=1, source_target_pairs={{0,12},{1,97},{2,14},{3,99},{4,0},{5,101},{6,2},{7,103},{8,4},{9,1... | collective-permute-start | bytes 1671176 | tf_op jit(solution)/shard_map/ppermute | solution.py:32
  46.4 7.8 %collective-permute-start.9 = (bf16[4,272,128]{2,1,0:T(8,128)(2,1)S(1)}, bf16[4,272,128]{2,1,0:T(8,128)(2,1)S(1)}, u32[]{:S(2)}, u32[]{:S(2)}) collective-permute-start(bf16[4,272,128]{2,1,0:T(8,128)(2,1)S(1)} %attend_plane.9), channel_id=1, source_target_pairs={{0,4},{1,33},{2,6},{3,35},{4,8},{5,37},{6,10},{7,39},{8,12},{9,41}... | collective-permute-start | bytes 835592 | tf_op jit(solution)/shard_map/ppermute | solution.py:32
  50.1 10.1 %collective-permute-start.11 = (bf16[4,272,128]{2,1,0:T(8,128)(2,1)S(1)}, bf16[4,272,128]{2,1,0:T(8,128)(2,1)S(1)}, u32[]{:S(2)}, u32[]{:S(2)}) collective-permute-start(bf16[4,272,128]{2,1,0:T(8,128)(2,1)S(1)} %attend_plane.10), channel_id=1, source_target_pairs={{0,4},{1,33},{2,6},{3,35},{4,8},{5,37},{6,10},{7,39},{8,12},{9,41}... | collective-permute-start | bytes 835592 | tf_op jit(solution)/shard_map/ppermute | solution.py:32
  54.9 7.2 %collective-permute-start.10 = (bf16[2,272,128]{2,1,0:T(8,128)(2,1)S(1)}, bf16[2,272,128]{2,1,0:T(8,128)(2,1)S(1)}, u32[]{:S(2)}, u32[]{:S(2)}) collective-permute-start(bf16[2,272,128]{2,1,0:T(8,128)(2,1)S(1)} %slice.22), channel_id=1, source_target_pairs={{0,96},{1,13},{2,98},{3,15},{4,100},{5,1},{6,102},{7,3},{8,104},{9... | collective-permute-start | bytes 417800 | tf_op jit(solution)/shard_map/ppermute | solution.py:32
  60.2 32.1 %copy-start = (bf16[4096,512]{1,0:T(8,128)(2,1)S(1)}, bf16[4096,512]{1,0:T(8,128)(2,1)}, u32[]{:S(2)}) copy-start(bf16[4096,512]{1,0:T(8,128)(2,1)} %w_ref.7) | copy-start | bytes 12582916
  60.9 6.7 %collective-permute-start.12 = (bf16[2,272,128]{2,1,0:T(8,128)(2,1)S(1)}, bf16[2,272,128]{2,1,0:T(8,128)(2,1)S(1)}, u32[]{:S(2)}, u32[]{:S(2)}) collective-permute-start(bf16[2,272,128]{2,1,0:T(8,128)(2,1)S(1)} %get-tuple-element.60), channel_id=1, source_target_pairs={{0,64},{1,9},{2,66},{3,11},{4,68},{5,13},{6,70},{7,15},{8,72},{9,1... | collective-permute-start | bytes 417800 | tf_op jit(solution)/shard_map/ppermute | solution.py:32
  61.8 7.3 %collective-permute-start.13 = (bf16[2,272,128]{2,1,0:T(8,128)(2,1)S(1)}, bf16[2,272,128]{2,1,0:T(8,128)(2,1)S(1)}, u32[]{:S(2)}, u32[]{:S(2)}) collective-permute-start(bf16[2,272,128]{2,1,0:T(8,128)(2,1)S(1)} %get-tuple-element.59), channel_id=1, source_target_pairs={{0,32},{1,5},{2,34},{3,7},{4,36},{5,9},{6,38},{7,11},{8,40},{9,13}... | collective-permute-start | bytes 417800 | tf_op jit(solution)/shard_map/ppermute | solution.py:32
  69.5 6.6 %collective-permute-start.14 = (bf16[2,272,128]{2,1,0:T(8,128)(2,1)S(1)}, bf16[2,272,128]{2,1,0:T(8,128)(2,1)S(1)}, u32[]{:S(2)}, u32[]{:S(2)}) collective-permute-start(bf16[2,272,128]{2,1,0:T(8,128)(2,1)S(1)} %combine.5.mine), channel_id=1, source_target_pairs={{0,16},{1,17},{2,18},{3,19},{4,20},{5,21},{6,22},{7,23},{8,24},{9,... | collective-permute-start | bytes 417800 | tf_op jit(solution)/shard_map/ppermute | solution.py:32
  76.4 6.6 %collective-permute-start.16 = (bf16[16,4096]{1,0:T(8,128)(2,1)S(1)}, bf16[16,4096]{1,0:T(8,128)(2,1)S(1)}, u32[]{:S(2)}, u32[]{:S(2)}) collective-permute-start(bf16[16,4096]{1,0:T(8,128)(2,1)S(1)} %finish.1.refs_0_), channel_id=1, source_target_pairs={{0,64},{1,9},{2,66},{3,11},{4,68},{5,13},{6,70},{7,15},{8,72},{9,1... | collective-permute-start | bytes 393224 | tf_op jit(solution)/shard_map/ppermute | solution.py:32
  77.2 5.7 %collective-permute-start.18 = (bf16[16,4096]{1,0:T(8,128)(2,1)S(1)}, bf16[16,4096]{1,0:T(8,128)(2,1)S(1)}, u32[]{:S(2)}, u32[]{:S(2)}) collective-permute-start(bf16[16,4096]{1,0:T(8,128)(2,1)S(1)} %finish.1.refs_0_), channel_id=1, source_target_pairs={{0,96},{1,13},{2,98},{3,15},{4,100},{5,1},{6,102},{7,3},{8,104},{9... | collective-permute-start | bytes 393224 | tf_op jit(solution)/shard_map/ppermute | solution.py:32
  78.4 6.2 %collective-permute-start.15 = (bf16[16,4096]{1,0:T(8,128)(2,1)S(1)}, bf16[16,4096]{1,0:T(8,128)(2,1)S(1)}, u32[]{:S(2)}, u32[]{:S(2)}) collective-permute-start(bf16[16,4096]{1,0:T(8,128)(2,1)S(1)} %finish.1.refs_0_), channel_id=1, source_target_pairs={{0,32},{1,5},{2,34},{3,7},{4,36},{5,9},{6,38},{7,11},{8,40},{9,13}... | collective-permute-start | bytes 393224 | tf_op jit(solution)/shard_map/ppermute | solution.py:32
  83.0 1.6 %collective-permute-start.17 = (bf16[16,4096]{1,0:T(8,128)(2,1)S(1)}, bf16[16,4096]{1,0:T(8,128)(2,1)S(1)}, u32[]{:S(2)}, u32[]{:S(2)}) collective-permute-start(bf16[16,4096]{1,0:T(8,128)(2,1)S(1)} %collective-permute-done.16.refs_0_), channel_id=1, source_target_pairs={{0,1},{1,0},{2,3},{3,2},{4,5},{5,4},{6,7},{7,6},{8,9},{9,8},{10,11... | collective-permute-start | bytes 393224 | tf_op jit(solution)/shard_map/ppermute | solution.py:32
  83.0 6.4 %collective-permute-start.22 = (bf16[32,4096]{1,0:T(8,128)(2,1)S(1)}, bf16[32,4096]{1,0:T(8,128)(2,1)S(1)}, u32[]{:S(2)}, u32[]{:S(2)}) collective-permute-start(bf16[32,4096]{1,0:T(8,128)(2,1)S(1)} %assemble.3.xb), channel_id=1, source_target_pairs={{0,12},{1,97},{2,14},{3,99},{4,0},{5,101},{6,2},{7,103},{8,4},{9,1... | collective-permute-start | bytes 786440 | tf_op jit(solution)/shard_map/ppermute | solution.py:32
  84.6 7.7 %collective-permute-start.19 = (bf16[32,4096]{1,0:T(8,128)(2,1)S(1)}, bf16[32,4096]{1,0:T(8,128)(2,1)S(1)}, u32[]{:S(2)}, u32[]{:S(2)}) collective-permute-start(bf16[32,4096]{1,0:T(8,128)(2,1)S(1)} %assemble.2.xa), channel_id=1, source_target_pairs={{0,4},{1,33},{2,6},{3,35},{4,8},{5,37},{6,10},{7,39},{8,12},{9,41}... | collective-permute-start | bytes 786440 | tf_op jit(solution)/shard_map/ppermute | solution.py:32
  85.2 7.9 %collective-permute-start.21 = (bf16[32,4096]{1,0:T(8,128)(2,1)S(1)}, bf16[32,4096]{1,0:T(8,128)(2,1)S(1)}, u32[]{:S(2)}, u32[]{:S(2)}) collective-permute-start(bf16[32,4096]{1,0:T(8,128)(2,1)S(1)} %assemble.2.xa), channel_id=1, source_target_pairs={{0,12},{1,97},{2,14},{3,99},{4,0},{5,101},{6,2},{7,103},{8,4},{9,1... | collective-permute-start | bytes 786440 | tf_op jit(solution)/shard_map/ppermute | solution.py:32
  87.9 7.6 %collective-permute-start.20 = (bf16[32,4096]{1,0:T(8,128)(2,1)S(1)}, bf16[32,4096]{1,0:T(8,128)(2,1)S(1)}, u32[]{:S(2)}, u32[]{:S(2)}) collective-permute-start(bf16[32,4096]{1,0:T(8,128)(2,1)S(1)} %assemble.3.xb), channel_id=1, source_target_pairs={{0,4},{1,33},{2,6},{3,35},{4,8},{5,37},{6,10},{7,39},{8,12},{9,41}... | collective-permute-start | bytes 786440 | tf_op jit(solution)/shard_map/ppermute | solution.py:32
  89.4 6.9 %collective-permute-start.24 = (bf16[32,4096]{1,0:T(8,128)(2,1)S(1)}, bf16[32,4096]{1,0:T(8,128)(2,1)S(1)}, u32[]{:S(2)}, u32[]{:S(2)}) collective-permute-start(bf16[32,4096]{1,0:T(8,128)(2,1)S(1)} %collective-permute-done.22.xb), channel_id=1, source_target_pairs={{0,12},{1,97},{2,14},{3,99},{4,0},{5,101},{6,2},{7,103},{8,4},{9,1... | collective-permute-start | bytes 786440 | tf_op jit(solution)/shard_map/ppermute | solution.py:32
  92.3 7.6 %collective-permute-start.23 = (bf16[32,4096]{1,0:T(8,128)(2,1)S(1)}, bf16[32,4096]{1,0:T(8,128)(2,1)S(1)}, u32[]{:S(2)}, u32[]{:S(2)}) collective-permute-start(bf16[32,4096]{1,0:T(8,128)(2,1)S(1)} %collective-permute-done.19.xa), channel_id=1, source_target_pairs={{0,4},{1,33},{2,6},{3,35},{4,8},{5,37},{6,10},{7,39},{8,12},{9,41}... | collective-permute-start | bytes 786440 | tf_op jit(solution)/shard_map/ppermute | solution.py:32
  101.3 1.6 %collective-permute-start.25 = (f32[128,512]{1,0:T(8,128)S(1)}, f32[128,512]{1,0:T(8,128)S(1)}, u32[]{:S(2)}, u32[]{:S(2)}) collective-permute-start(f32[128,512]{1,0:T(8,128)S(1)} %slice.32), channel_id=1, source_target_pairs={{0,1},{1,0},{2,3},{3,2},{4,5},{5,4},{6,7},{7,6},{8,9},{9,8},{10,11... | collective-permute-start | bytes 786440 | tf_op jit(solution)/shard_map/ppermute | solution.py:32
  102.9 4.3 %collective-permute-start.26 = (bf16[64,512]{1,0:T(8,128)(2,1)S(1)}, bf16[64,512]{1,0:T(8,128)(2,1)S(1)}, u32[]{:S(2)}, u32[]{:S(2)}) collective-permute-start(bf16[64,512]{1,0:T(8,128)(2,1)S(1)} %slice.40), channel_id=1, source_target_pairs={{0,2},{1,3},{2,0},{3,1},{4,6},{5,7},{6,4},{7,5},{8,10},{9,11},{10,... | collective-permute-start | bytes 196616 | tf_op jit(solution)/shard_map/ppermute | solution.py:32

commit v3 on v2

--- a/solution.py
+++ b/solution.py
@@ -69,7 +69,8 @@
     lane = lax.broadcasted_iota(jnp.int32, (1, 128), 1)
     slot = lax.broadcasted_iota(jnp.int32, (span, 128), 0)
     for db, kx in enumerate(masked):
-        z, yh, x = source(me, lane >> 4, db, (lane >> 3) & 1)
+        da = ((lane >> 5) & 1) | ((lane >> 3) & 2)
+        z, yh, x = source(me, da, db, (lane >> 3) & 1)
         seen = start + z * 64 + yh * 32 + x * 8 + (lane & 7) + 1 - shard * span
         seen = jnp.minimum(seen, length)
         mask = jnp.where((slot >= seen) & (lane < 64), NEG, 0.0).astype(jnp.bfloat16)
@@ -326,8 +327,8 @@
     q = jnp.concatenate([q, moved(q, yh=1)], axis=0)
     q, k, v, info = together(q, k, v, info)
     vx, kx0, kx1, kx2, kx3 = prepare(info, k, v)
-    q2, q1, q3 = (moved(q, a=d) for d in (2, 1, 3))
-    q = jnp.concatenate([q, q1, q2, q3], axis=0)
+    q1, q3 = moved(q, a=1), moved(q, a=3)
+    q = jnp.concatenate([q, moved(q1, a=1), q1, q3], axis=0)
     q, vx, kx0, kx1, kx2, kx3 = together(q, vx, kx0, kx1, kx2, kx3)
 
     q2, q1, q3 = (moved(q, b=d) for d in (2, 1, 3))
@@ -349,14 +350,14 @@
     low = combine(4, (own0, 0), (r1, 0), (r2, 0), (r3a, 0))
     q, low = together(q, low)
     own1 = attend(q, kx0, vx, kvs, 4, 4)
-    s1 = moved(low[2:], a=-1)
+    s2 = moved(low[2:], a=-2)
     high = combine(4, (own1, 0), (r1, 4), (r2, 4), (r3b, 0))
-    s2, s3 = moved(high[:2], a=-2), moved(high[2:], a=-3)
+    s1, s3 = moved(high[:2], a=-1), moved(high[2:], a=-3)
     c = combine(2, (low, 0), (s1, 0), (s2, 0), (s3, 0))
     attn = finish(c, moved(c, yh=1))
-    x2, x1, x3 = (moved(attn, a=d) for d in (2, 1, 3))
-    low = assemble([attn, x1], moved(x2, core=1))
-    high = assemble([x2, x3])
+    x1, x3 = moved(attn, a=1), moved(attn, a=3)
+    low = assemble([attn, x1], moved(x1, core=1))
+    high = assemble([moved(x1, a=1), x3])
     x1a, x3b = moved(low, b=1), moved(high, b=3)
     x1b, x3a = moved(high, b=1), moved(low, b=3)
     x2a, x2b = moved(x1a, b=1), moved(x3b, b=3)

time: 108 us -> 120 us (1.11)
  waiting for transfers between devices: 35.2 us -> 41.9 us
  starting transfers between devices: 38.1 us -> 43.3 us
    ppermute x27, waiting for transfers between devices: 35.2 us -> 41.9 us  [moved(): return lax.ppermute(x, ('cp', 'tp'), pairs)]
    ppermute x27, starting transfers between devices: 38.1 us -> 43.3 us  [moved(): return lax.ppermute(x, ('cp', 'tp'), pairs)]
  transfers between devices with their start and end apart: 27 -> 27, of which waited for: 15 -> 17; matrix products, arithmetic and copies ran while one was open for 2% -> 2% of each run, Pallas kernels for 26% -> 24%
where the time goes in v3:
time: 120 us
  starting transfers between devices  43.3 us (36%)
  waiting for transfers between devices  41.9 us (35%)
  Pallas kernels  30.3 us (25%)
  local copies, waits for them, and re-layouts  1.97 us (2%)
  between operations  1.6 us (1%)
    ppermute x27, starting transfers between devices, moved(): return lax.ppermute(x, ('cp', 'tp'), pairs)  43.3 us
    ppermute x27, waiting for transfers between devices, moved(): return lax.ppermute(x, ('cp', 'tp'), pairs)  41.9 us
    pallas_call x6, Pallas kernels, attend(): pl.pallas_call(functools.partial(attend_kernel, kvs=kvs, first=first, nb=...  22.1 us
    pallas_call x3, Pallas kernels, project(): pl.pallas_call(project_kernel, in_specs=[vmem] * 3, out_specs=vmem, out_s...  2.53 us
  transfers between devices with their start and end apart: 27, of which 17 were waited for; matrix products, arithmetic and copies ran while one was open for 2% of the time, Pallas kernels for 24%

profile of v3, /device:TPU:0, one launch (start us, length us, event | category | flops | bytes accessed | tf_op | source)
XLA Modules:
  0.0 119.8 jit_solution(10502162644272616161)
XLA Ops:
  0.0 3.3 %collective-permute-start = (bf16[1,8,32,128]{3,2,1,0:T(8,128)(2,1)}, bf16[1,8,32,128]{3,2,1,0:T(8,128)(2,1)S(1)}, u32[]{:S(2)}, u32[]{:S(2)}) collective-permute-start(bf16[1,8,32,128]{3,2,1,0:T(8,128)(2,1)} %bitcast.10), channel_id=1, source_target_pairs={{0,16},{1,17},{2,18},{3,19},{4,20},{5,21},{6,22},{7,23},{8,24},{9,... | collective-permute-start | bytes 196616 | tf_op jit(solution)/shard_map/ppermute | solution.py:32
  3.3 1.8 %copy_bitcast_fusion = (bf16[2,2048,128]{2,1,0:T(8,128)(2,1)S(1)}, bf16[2,2048,128]{2,1,0:T(8,128)(2,1)S(1)}) fusion(bf16[2048,2,128]{2,1,0:T(2,128)(2,1)} %param.8, bf16[2048,2,128]{2,1,0:T(2,128)(2,1)} %param.7), kind=kLoop, calls=%fused_computation | loop fusion | bytes 4194304 | tf_op jit(solution)/shard_map/transpose | solution.py:325
  6.6 2.0 %collective-permute-start.1 = (bf16[2,8,32,128]{3,2,1,0:T(8,128)(2,1)S(1)}, bf16[2,8,32,128]{3,2,1,0:T(8,128)(2,1)S(1)}, u32[]{:S(2)}, u32[]{:S(2)}) collective-permute-start(bf16[2,8,32,128]{3,2,1,0:T(8,128)(2,1)S(1)} %pad_maximum_fusion.1), channel_id=1, source_target_pairs={{0,32},{1,5},{2,34},{3,7},{4,36},{5,9},{6,38},{7,11},{8,40},{9,13}... | collective-permute-start | bytes 393224 | tf_op jit(solution)/shard_map/ppermute | solution.py:32
  8.5 2.2 %collective-permute-start.3 = (bf16[2,8,32,128]{3,2,1,0:T(8,128)(2,1)S(1)}, bf16[2,8,32,128]{3,2,1,0:T(8,128)(2,1)S(1)}, u32[]{:S(2)}, u32[]{:S(2)}) collective-permute-start(bf16[2,8,32,128]{3,2,1,0:T(8,128)(2,1)S(1)} %pad_maximum_fusion.1), channel_id=1, source_target_pairs={{0,96},{1,13},{2,98},{3,15},{4,100},{5,1},{6,102},{7,3},{8,104},{9... | collective-permute-start | bytes 393224 | tf_op jit(solution)/shard_map/ppermute | solution.py:32
  10.8 2.9 %collective-permute-done.1 = bf16[2,8,32,128]{3,2,1,0:T(8,128)(2,1)S(1)} collective-permute-done((bf16[2,8,32,128]{3,2,1,0:T(8,128)(2,1)S(1)}, bf16[2,8,32,128]{3,2,1,0:T(8,128)(2,1)S(1)}, u32[]{:S(2)}, u32[]{:S(2)}) %collective-permute-start.1) | collective-permute-done | bytes 131104 | tf_op jit(solution)/shard_map/ppermute | solution.py:32
  13.6 2.2 %prepare.1 = (bf16[2,2048,256]{2,1,0:T(8,128)(2,1)S(1)}, bf16[2,2048,256]{2,1,0:T(8,128)(2,1)S(1)}, bf16[2,2048,256]{2,1,0:T(8,128)(2,1)S(1)}, bf16[2,2048,256]{...) custom-call(s32[7]{0:T(128)S(1)} %concatenate.10.info, bf16[2,2048,128]{2,1,0:T(8,128)(2,1)S(1)} %get-tuple-element.34.k_ref, ...), custom_call_target="tpu_custom_call" | custom-call | tf_op jit(solution)/shard_map/prepare/pallas_call | solution.py:88
  15.8 4.0 %collective-permute-done.2 = bf16[2,8,32,128]{3,2,1,0:T(8,128)(2,1)S(1)} collective-permute-done((bf16[2,8,32,128]{3,2,1,0:T(8,128)(2,1)S(1)}, bf16[2,8,32,128]{3,2,1,0:T(8,128)(2,1)S(1)}, u32[]{:S(2)}, u32[]{:S(2)}) %collective-permute-start.2) | collective-permute-done | bytes 131104 | tf_op jit(solution)/shard_map/ppermute | solution.py:32
  19.9 4.2 %collective-permute-start.6 = (bf16[8,8,32,128]{3,2,1,0:T(8,128)(2,1)S(1)}, bf16[8,8,32,128]{3,2,1,0:T(8,128)(2,1)S(1)}, u32[]{:S(2)}, u32[]{:S(2)}) collective-permute-start(bf16[8,8,32,128]{3,2,1,0:T(8,128)(2,1)S(1)} %pad_maximum_fusion.q_ref), channel_id=1, source_target_pairs={{0,8},{1,65},{2,10},{3,67},{4,12},{5,69},{6,14},{7,71},{8,0},{9,73... | collective-permute-start | bytes 1572872 | tf_op jit(solution)/shard_map/ppermute | solution.py:32
  24.6 2.6 %collective-permute-start.5 = (bf16[8,8,32,128]{3,2,1,0:T(8,128)(2,1)S(1)}, bf16[8,8,32,128]{3,2,1,0:T(8,128)(2,1)S(1)}, u32[]{:S(2)}, u32[]{:S(2)}) collective-permute-start(bf16[8,8,32,128]{3,2,1,0:T(8,128)(2,1)S(1)} %pad_maximum_fusion.q_ref), channel_id=1, source_target_pairs={{0,12},{1,97},{2,14},{3,99},{4,0},{5,101},{6,2},{7,103},{8,4},{9,1... | collective-permute-start | bytes 1572872 | tf_op jit(solution)/shard_map/ppermute | solution.py:32
  27.3 2.8 %attend_plane.6.refs_0_ = bf16[4,272,128]{2,1,0:T(8,128)(2,1)S(1)} custom-call(bf16[8,8,32,128]{3,2,1,0:T(8,128)(2,1)S(1)} %pad_maximum_fusion.q_ref, bf16[2,2048,256]{2,1,0:T(8,128)(2,1)S(1)} %get-tuple-element.42.kx, bf16[2,2048,256]{2,1,0:T(8,128)(2,1)S(1)} %get-tuple-element.43.vx), custom_call_target="tpu_custom_call" | custom-call | flops 2147483648 | bytes 4194304 | tf_op jit(solution)/shard_map/attend_plane/pallas_call | solution.py:169
  31.3 5.5 %attend_plane.7 = bf16[8,272,128]{2,1,0:T(8,128)(2,1)S(1)} custom-call(bf16[8,8,32,128]{3,2,1,0:T(8,128)(2,1)S(1)} %collective-permute-done.6.q_ref, bf16[2,2048,256]{2,1,0:T(8,128)(2,1)S(1)} %get-tuple-element.45.kx, bf16[2,2048,256]{2,1,0:T(8,128)(2,1)S(1)} %get-tuple-element.43.vx), custom_call_target="tpu_custom_call" | custom-call | flops 4294967296 | bytes 4194304 | tf_op jit(solution)/shard_map/attend_plane/pallas_call | solution.py:169
  36.9 3.8 %collective-permute-start.7 = (bf16[8,272,128]{2,1,0:T(8,128)(2,1)S(1)}, bf16[8,272,128]{2,1,0:T(8,128)(2,1)S(1)}, u32[]{:S(2)}, u32[]{:S(2)}) collective-permute-start(bf16[8,272,128]{2,1,0:T(8,128)(2,1)S(1)} %attend_plane.7), channel_id=1, source_target_pairs={{0,8},{1,65},{2,10},{3,67},{4,12},{5,69},{6,14},{7,71},{8,0},{9,73... | collective-permute-start | bytes 1671176 | tf_op jit(solution)/shard_map/ppermute | solution.py:32
  40.7 5.5 %attend_plane.8 = bf16[8,272,128]{2,1,0:T(8,128)(2,1)S(1)} custom-call(bf16[8,8,32,128]{3,2,1,0:T(8,128)(2,1)S(1)} %collective-permute-done.4.q_ref, bf16[2,2048,256]{2,1,0:T(8,128)(2,1)S(1)} %get-tuple-element.48.kx, bf16[2,2048,256]{2,1,0:T(8,128)(2,1)S(1)} %get-tuple-element.43.vx), custom_call_target="tpu_custom_call" | custom-call | flops 4294967296 | bytes 4194304 | tf_op jit(solution)/shard_map/attend_plane/pallas_call | solution.py:169
  47.4 2.8 %attend_plane.9 = bf16[4,272,128]{2,1,0:T(8,128)(2,1)S(1)} custom-call(bf16[8,8,32,128]{3,2,1,0:T(8,128)(2,1)S(1)} %collective-permute-done.5.q_ref, bf16[2,2048,256]{2,1,0:T(8,128)(2,1)S(1)} %get-tuple-element.50.kx, bf16[2,2048,256]{2,1,0:T(8,128)(2,1)S(1)} %get-tuple-element.43.vx), custom_call_target="tpu_custom_call" | custom-call | flops 2147483648 | bytes 4194304 | tf_op jit(solution)/shard_map/attend_plane/pallas_call | solution.py:169
  51.2 2.8 %attend_plane.10 = bf16[4,272,128]{2,1,0:T(8,128)(2,1)S(1)} custom-call(bf16[8,8,32,128]{3,2,1,0:T(8,128)(2,1)S(1)} %collective-permute-done.5.q_ref, bf16[2,2048,256]{2,1,0:T(8,128)(2,1)S(1)} %get-tuple-element.50.kx, bf16[2,2048,256]{2,1,0:T(8,128)(2,1)S(1)} %get-tuple-element.43.vx), custom_call_target="tpu_custom_call" | custom-call | flops 2147483648 | bytes 4194304 | tf_op jit(solution)/shard_map/attend_plane/pallas_call | solution.py:169
  54.6 4.9 %collective-permute-done.9.refs_3_ = bf16[4,272,128]{2,1,0:T(8,128)(2,1)S(1)} collective-permute-done((bf16[4,272,128]{2,1,0:T(8,128)(2,1)S(1)}, bf16[4,272,128]{2,1,0:T(8,128)(2,1)S(1)}, u32[]{:S(2)}, u32[]{:S(2)}) %collective-permute-start.9) | collective-permute-done | bytes 278560 | tf_op jit(solution)/shard_map/ppermute | solution.py:32
  60.5 2.8 %attend_plane.11.refs_0_ = bf16[4,272,128]{2,1,0:T(8,128)(2,1)S(1)} custom-call(bf16[8,8,32,128]{3,2,1,0:T(8,128)(2,1)S(1)} %pad_maximum_fusion.q_ref, bf16[2,2048,256]{2,1,0:T(8,128)(2,1)S(1)} %get-tuple-element.42.kx, bf16[2,2048,256]{2,1,0:T(8,128)(2,1)S(1)} %get-tuple-element.43.vx), custom_call_target="tpu_custom_call" | custom-call | flops 2147483648 | bytes 4194304 | tf_op jit(solution)/shard_map/attend_plane/pallas_call | solution.py:169
  67.1 2.7 %collective-permute-done.11.refs_1_ = bf16[2,272,128]{2,1,0:T(8,128)(2,1)S(1)} collective-permute-done((bf16[2,272,128]{2,1,0:T(8,128)(2,1)S(1)}, bf16[2,272,128]{2,1,0:T(8,128)(2,1)S(1)}, u32[]{:S(2)}, u32[]{:S(2)}) %collective-permute-start.11) | collective-permute-done | bytes 139296 | tf_op jit(solution)/shard_map/ppermute | solution.py:32
  69.8 2.3 %collective-permute-done.13.refs_3_ = bf16[2,272,128]{2,1,0:T(8,128)(2,1)S(1)} collective-permute-done((bf16[2,272,128]{2,1,0:T(8,128)(2,1)S(1)}, bf16[2,272,128]{2,1,0:T(8,128)(2,1)S(1)}, u32[]{:S(2)}, u32[]{:S(2)}) %collective-permute-start.13) | collective-permute-done | bytes 139296 | tf_op jit(solution)/shard_map/ppermute | solution.py:32
  72.5 6.4 %collective-permute-start.14 = (bf16[2,272,128]{2,1,0:T(8,128)(2,1)S(1)}, bf16[2,272,128]{2,1,0:T(8,128)(2,1)S(1)}, u32[]{:S(2)}, u32[]{:S(2)}) collective-permute-start(bf16[2,272,128]{2,1,0:T(8,128)(2,1)S(1)} %combine.5.mine), channel_id=1, source_target_pairs={{0,16},{1,17},{2,18},{3,19},{4,20},{5,21},{6,22},{7,23},{8,24},{9,... | collective-permute-start | bytes 417800 | tf_op jit(solution)/shard_map/ppermute | solution.py:32
  78.9 3.0 %collective-permute-done.14.theirs = bf16[2,272,128]{2,1,0:T(8,128)(2,1)S(1)} collective-permute-done((bf16[2,272,128]{2,1,0:T(8,128)(2,1)S(1)}, bf16[2,272,128]{2,1,0:T(8,128)(2,1)S(1)}, u32[]{:S(2)}, u32[]{:S(2)}) %collective-permute-start.14) | collective-permute-done | bytes 139296 | tf_op jit(solution)/shard_map/ppermute | solution.py:32
  82.3 3.2 %collective-permute-start.18 = (bf16[16,4096]{1,0:T(8,128)(2,1)S(1)}, bf16[16,4096]{1,0:T(8,128)(2,1)S(1)}, u32[]{:S(2)}, u32[]{:S(2)}) collective-permute-start(bf16[16,4096]{1,0:T(8,128)(2,1)S(1)} %finish.1.refs_0_), channel_id=1, source_target_pairs={{0,96},{1,13},{2,98},{3,15},{4,100},{5,1},{6,102},{7,3},{8,104},{9... | collective-permute-start | bytes 393224 | tf_op jit(solution)/shard_map/ppermute | solution.py:32
  85.6 2.9 %collective-permute-done.15.refs_1_ = bf16[16,4096]{1,0:T(8,128)(2,1)S(1)} collective-permute-done((bf16[16,4096]{1,0:T(8,128)(2,1)S(1)}, bf16[16,4096]{1,0:T(8,128)(2,1)S(1)}, u32[]{:S(2)}, u32[]{:S(2)}) %collective-permute-start.15) | collective-permute-done | bytes 131104 | tf_op jit(solution)/shard_map/ppermute | solution.py:32
  88.5 6.2 %collective-permute-done.17.refs_0_ = bf16[16,4096]{1,0:T(8,128)(2,1)S(1)} collective-permute-done((bf16[16,4096]{1,0:T(8,128)(2,1)S(1)}, bf16[16,4096]{1,0:T(8,128)(2,1)S(1)}, u32[]{:S(2)}, u32[]{:S(2)}) %collective-permute-start.17) | collective-permute-done | bytes 131104 | tf_op jit(solution)/shard_map/ppermute | solution.py:32
  96.9 2.5 %collective-permute-start.21 = (bf16[32,4096]{1,0:T(8,128)(2,1)S(1)}, bf16[32,4096]{1,0:T(8,128)(2,1)S(1)}, u32[]{:S(2)}, u32[]{:S(2)}) collective-permute-start(bf16[32,4096]{1,0:T(8,128)(2,1)S(1)} %assemble.2.xa), channel_id=1, source_target_pairs={{0,12},{1,97},{2,14},{3,99},{4,0},{5,101},{6,2},{7,103},{8,4},{9,1... | collective-permute-start | bytes 786440 | tf_op jit(solution)/shard_map/ppermute | solution.py:32
  99.4 1.8 %collective-permute-done.22.xb = bf16[32,4096]{1,0:T(8,128)(2,1)S(1)} collective-permute-done((bf16[32,4096]{1,0:T(8,128)(2,1)S(1)}, bf16[32,4096]{1,0:T(8,128)(2,1)S(1)}, u32[]{:S(2)}, u32[]{:S(2)}) %collective-permute-start.22) | collective-permute-done | bytes 262176 | tf_op jit(solution)/shard_map/ppermute | solution.py:32
  101.1 2.5 %collective-permute-start.24 = (bf16[32,4096]{1,0:T(8,128)(2,1)S(1)}, bf16[32,4096]{1,0:T(8,128)(2,1)S(1)}, u32[]{:S(2)}, u32[]{:S(2)}) collective-permute-start(bf16[32,4096]{1,0:T(8,128)(2,1)S(1)} %collective-permute-done.22.xb), channel_id=1, source_target_pairs={{0,12},{1,97},{2,14},{3,99},{4,0},{5,101},{6,2},{7,103},{8,4},{9,1... | collective-permute-start | bytes 786440 | tf_op jit(solution)/shard_map/ppermute | solution.py:32
  105.4 1.5 %collective-permute-done.20.xb = bf16[32,4096]{1,0:T(8,128)(2,1)S(1)} collective-permute-done((bf16[32,4096]{1,0:T(8,128)(2,1)S(1)}, bf16[32,4096]{1,0:T(8,128)(2,1)S(1)}, u32[]{:S(2)}, u32[]{:S(2)}) %collective-permute-start.20) | collective-permute-done | bytes 262176 | tf_op jit(solution)/shard_map/ppermute | solution.py:32
  107.8 3.5 %collective-permute-done.23.xa = bf16[32,4096]{1,0:T(8,128)(2,1)S(1)} collective-permute-done((bf16[32,4096]{1,0:T(8,128)(2,1)S(1)}, bf16[32,4096]{1,0:T(8,128)(2,1)S(1)}, u32[]{:S(2)}, u32[]{:S(2)}) %collective-permute-start.23) | collective-permute-done | bytes 262176 | tf_op jit(solution)/shard_map/ppermute | solution.py:32
  112.8 1.5 %collective-permute-done.25 = f32[128,512]{1,0:T(8,128)S(1)} collective-permute-done((f32[128,512]{1,0:T(8,128)S(1)}, f32[128,512]{1,0:T(8,128)S(1)}, u32[]{:S(2)}, u32[]{:S(2)}) %collective-permute-start.25) | collective-permute-done | bytes 262176 | tf_op jit(solution)/shard_map/ppermute | solution.py:32
  114.4 2.4 %collective-permute-start.26 = (bf16[64,512]{1,0:T(8,128)(2,1)S(1)}, bf16[64,512]{1,0:T(8,128)(2,1)S(1)}, u32[]{:S(2)}, u32[]{:S(2)}) collective-permute-start(bf16[64,512]{1,0:T(8,128)(2,1)S(1)} %slice.40), channel_id=1, source_target_pairs={{0,2},{1,3},{2,0},{3,1},{4,6},{5,7},{6,4},{7,5},{8,10},{9,11},{10,... | collective-permute-start | bytes 196616 | tf_op jit(solution)/shard_map/ppermute | solution.py:32
  116.8 2.4 %collective-permute-done.26 = bf16[64,512]{1,0:T(8,128)(2,1)S(1)} collective-permute-done((bf16[64,512]{1,0:T(8,128)(2,1)S(1)}, bf16[64,512]{1,0:T(8,128)(2,1)S(1)}, u32[]{:S(2)}, u32[]{:S(2)}) %collective-permute-start.26) | collective-permute-done | bytes 65568 | tf_op jit(solution)/shard_map/ppermute | solution.py:32
  (53 shorter events, 17.4 us)
Async XLA Ops:
  0.0 6.5 %copy-start.1 = (bf16[8,32,128]{2,1,0:T(8,128)(2,1)S(1)}, bf16[8,32,128]{2,1,0:T(8,128)(2,1)}, u32[]{:S(2)}) copy-start(bf16[8,32,128]{2,1,0:T(8,128)(2,1)} %param.6) | copy-start | bytes 196612
  0.0 6.5 %collective-permute-start = (bf16[1,8,32,128]{3,2,1,0:T(8,128)(2,1)}, bf16[1,8,32,128]{3,2,1,0:T(8,128)(2,1)S(1)}, u32[]{:S(2)}, u32[]{:S(2)}) collective-permute-start(bf16[1,8,32,128]{3,2,1,0:T(8,128)(2,1)} %bitcast.10), channel_id=1, source_target_pairs={{0,16},{1,17},{2,18},{3,19},{4,20},{5,21},{6,22},{7,23},{8,24},{9,... | collective-permute-start | bytes 196616 | tf_op jit(solution)/shard_map/ppermute | solution.py:32
  6.6 7.1 %collective-permute-start.1 = (bf16[2,8,32,128]{3,2,1,0:T(8,128)(2,1)S(1)}, bf16[2,8,32,128]{3,2,1,0:T(8,128)(2,1)S(1)}, u32[]{:S(2)}, u32[]{:S(2)}) collective-permute-start(bf16[2,8,32,128]{3,2,1,0:T(8,128)(2,1)S(1)} %pad_maximum_fusion.1), channel_id=1, source_target_pairs={{0,32},{1,5},{2,34},{3,7},{4,36},{5,9},{6,38},{7,11},{8,40},{9,13}... | collective-permute-start | bytes 393224 | tf_op jit(solution)/shard_map/ppermute | solution.py:32
  8.5 7.2 %collective-permute-start.3 = (bf16[2,8,32,128]{3,2,1,0:T(8,128)(2,1)S(1)}, bf16[2,8,32,128]{3,2,1,0:T(8,128)(2,1)S(1)}, u32[]{:S(2)}, u32[]{:S(2)}) collective-permute-start(bf16[2,8,32,128]{3,2,1,0:T(8,128)(2,1)S(1)} %pad_maximum_fusion.1), channel_id=1, source_target_pairs={{0,96},{1,13},{2,98},{3,15},{4,100},{5,1},{6,102},{7,3},{8,104},{9... | collective-permute-start | bytes 393224 | tf_op jit(solution)/shard_map/ppermute | solution.py:32
  13.6 6.2 %collective-permute-start.2 = (bf16[2,8,32,128]{3,2,1,0:T(8,128)(2,1)S(1)}, bf16[2,8,32,128]{3,2,1,0:T(8,128)(2,1)S(1)}, u32[]{:S(2)}, u32[]{:S(2)}) collective-permute-start(bf16[2,8,32,128]{3,2,1,0:T(8,128)(2,1)S(1)} %collective-permute-done.1), channel_id=1, source_target_pairs={{0,32},{1,5},{2,34},{3,7},{4,36},{5,9},{6,38},{7,11},{8,40},{9,13}... | collective-permute-start | bytes 393224 | tf_op jit(solution)/shard_map/ppermute | solution.py:32
  19.9 11.5 %collective-permute-start.6 = (bf16[8,8,32,128]{3,2,1,0:T(8,128)(2,1)S(1)}, bf16[8,8,32,128]{3,2,1,0:T(8,128)(2,1)S(1)}, u32[]{:S(2)}, u32[]{:S(2)}) collective-permute-start(bf16[8,8,32,128]{3,2,1,0:T(8,128)(2,1)S(1)} %pad_maximum_fusion.q_ref), channel_id=1, source_target_pairs={{0,8},{1,65},{2,10},{3,67},{4,12},{5,69},{6,14},{7,71},{8,0},{9,73... | collective-permute-start | bytes 1572872 | tf_op jit(solution)/shard_map/ppermute | solution.py:32
  24.1 16.6 %collective-permute-start.4 = (bf16[8,8,32,128]{3,2,1,0:T(8,128)(2,1)S(1)}, bf16[8,8,32,128]{3,2,1,0:T(8,128)(2,1)S(1)}, u32[]{:S(2)}, u32[]{:S(2)}) collective-permute-start(bf16[8,8,32,128]{3,2,1,0:T(8,128)(2,1)S(1)} %pad_maximum_fusion.q_ref), channel_id=1, source_target_pairs={{0,4},{1,33},{2,6},{3,35},{4,8},{5,37},{6,10},{7,39},{8,12},{9,41}... | collective-permute-start | bytes 1572872 | tf_op jit(solution)/shard_map/ppermute | solution.py:32
  24.6 16.0 %collective-permute-start.5 = (bf16[8,8,32,128]{3,2,1,0:T(8,128)(2,1)S(1)}, bf16[8,8,32,128]{3,2,1,0:T(8,128)(2,1)S(1)}, u32[]{:S(2)}, u32[]{:S(2)}) collective-permute-start(bf16[8,8,32,128]{3,2,1,0:T(8,128)(2,1)S(1)} %pad_maximum_fusion.q_ref), channel_id=1, source_target_pairs={{0,12},{1,97},{2,14},{3,99},{4,0},{5,101},{6,2},{7,103},{8,4},{9,1... | collective-permute-start | bytes 1572872 | tf_op jit(solution)/shard_map/ppermute | solution.py:32
  36.9 14.3 %collective-permute-start.7 = (bf16[8,272,128]{2,1,0:T(8,128)(2,1)S(1)}, bf16[8,272,128]{2,1,0:T(8,128)(2,1)S(1)}, u32[]{:S(2)}, u32[]{:S(2)}) collective-permute-start(bf16[8,272,128]{2,1,0:T(8,128)(2,1)S(1)} %attend_plane.7), channel_id=1, source_target_pairs={{0,8},{1,65},{2,10},{3,67},{4,12},{5,69},{6,14},{7,71},{8,0},{9,73... | collective-permute-start | bytes 1671176 | tf_op jit(solution)/shard_map/ppermute | solution.py:32
  46.2 13.3 %collective-permute-start.8 = (bf16[8,272,128]{2,1,0:T(8,128)(2,1)S(1)}, bf16[8,272,128]{2,1,0:T(8,128)(2,1)S(1)}, u32[]{:S(2)}, u32[]{:S(2)}) collective-permute-start(bf16[8,272,128]{2,1,0:T(8,128)(2,1)S(1)} %attend_plane.8), channel_id=1, source_target_pairs={{0,12},{1,97},{2,14},{3,99},{4,0},{5,101},{6,2},{7,103},{8,4},{9,1... | collective-permute-start | bytes 1671176 | tf_op jit(solution)/shard_map/ppermute | solution.py:32
  50.2 9.3 %collective-permute-start.9 = (bf16[4,272,128]{2,1,0:T(8,128)(2,1)S(1)}, bf16[4,272,128]{2,1,0:T(8,128)(2,1)S(1)}, u32[]{:S(2)}, u32[]{:S(2)}) collective-permute-start(bf16[4,272,128]{2,1,0:T(8,128)(2,1)S(1)} %attend_plane.9), channel_id=1, source_target_pairs={{0,4},{1,33},{2,6},{3,35},{4,8},{5,37},{6,10},{7,39},{8,12},{9,41}... | collective-permute-start | bytes 835592 | tf_op jit(solution)/shard_map/ppermute | solution.py:32
  53.9 10.1 %collective-permute-start.10 = (bf16[4,272,128]{2,1,0:T(8,128)(2,1)S(1)}, bf16[4,272,128]{2,1,0:T(8,128)(2,1)S(1)}, u32[]{:S(2)}, u32[]{:S(2)}) collective-permute-start(bf16[4,272,128]{2,1,0:T(8,128)(2,1)S(1)} %attend_plane.10), channel_id=1, source_target_pairs={{0,4},{1,33},{2,6},{3,35},{4,8},{5,37},{6,10},{7,39},{8,12},{9,41}... | collective-permute-start | bytes 835592 | tf_op jit(solution)/shard_map/ppermute | solution.py:32
  60.2 6.9 %collective-permute-start.12 = (bf16[2,272,128]{2,1,0:T(8,128)(2,1)S(1)}, bf16[2,272,128]{2,1,0:T(8,128)(2,1)S(1)}, u32[]{:S(2)}, u32[]{:S(2)}) collective-permute-start(bf16[2,272,128]{2,1,0:T(8,128)(2,1)S(1)} %slice.23), channel_id=1, source_target_pairs={{0,64},{1,9},{2,66},{3,11},{4,68},{5,13},{6,70},{7,15},{8,72},{9,1... | collective-permute-start | bytes 417800 | tf_op jit(solution)/shard_map/ppermute | solution.py:32
  63.3 40.4 %copy-start = (bf16[4096,512]{1,0:T(8,128)(2,1)S(1)}, bf16[4096,512]{1,0:T(8,128)(2,1)}, u32[]{:S(2)}) copy-start(bf16[4096,512]{1,0:T(8,128)(2,1)} %w_ref.7) | copy-start | bytes 12582916
  64.7 5.1 %collective-permute-start.11 = (bf16[2,272,128]{2,1,0:T(8,128)(2,1)S(1)}, bf16[2,272,128]{2,1,0:T(8,128)(2,1)S(1)}, u32[]{:S(2)}, u32[]{:S(2)}) collective-permute-start(bf16[2,272,128]{2,1,0:T(8,128)(2,1)S(1)} %get-tuple-element.60), channel_id=1, source_target_pairs={{0,96},{1,13},{2,98},{3,15},{4,100},{5,1},{6,102},{7,3},{8,104},{9... | collective-permute-start | bytes 417800 | tf_op jit(solution)/shard_map/ppermute | solution.py:32
  65.8 6.3 %collective-permute-start.13 = (bf16[2,272,128]{2,1,0:T(8,128)(2,1)S(1)}, bf16[2,272,128]{2,1,0:T(8,128)(2,1)S(1)}, u32[]{:S(2)}, u32[]{:S(2)}) collective-permute-start(bf16[2,272,128]{2,1,0:T(8,128)(2,1)S(1)} %get-tuple-element.59), channel_id=1, source_target_pairs={{0,32},{1,5},{2,34},{3,7},{4,36},{5,9},{6,38},{7,11},{8,40},{9,13}... | collective-permute-start | bytes 417800 | tf_op jit(solution)/shard_map/ppermute | solution.py:32
  72.5 9.5 %collective-permute-start.14 = (bf16[2,272,128]{2,1,0:T(8,128)(2,1)S(1)}, bf16[2,272,128]{2,1,0:T(8,128)(2,1)S(1)}, u32[]{:S(2)}, u32[]{:S(2)}) collective-permute-start(bf16[2,272,128]{2,1,0:T(8,128)(2,1)S(1)} %combine.5.mine), channel_id=1, source_target_pairs={{0,16},{1,17},{2,18},{3,19},{4,20},{5,21},{6,22},{7,23},{8,24},{9,... | collective-permute-start | bytes 417800 | tf_op jit(solution)/shard_map/ppermute | solution.py:32
  82.2 6.2 %collective-permute-start.15 = (bf16[16,4096]{1,0:T(8,128)(2,1)S(1)}, bf16[16,4096]{1,0:T(8,128)(2,1)S(1)}, u32[]{:S(2)}, u32[]{:S(2)}) collective-permute-start(bf16[16,4096]{1,0:T(8,128)(2,1)S(1)} %finish.1.refs_0_), channel_id=1, source_target_pairs={{0,32},{1,5},{2,34},{3,7},{4,36},{5,9},{6,38},{7,11},{8,40},{9,13}... | collective-permute-start | bytes 393224 | tf_op jit(solution)/shard_map/ppermute | solution.py:32
  82.3 6.2 %collective-permute-start.18 = (bf16[16,4096]{1,0:T(8,128)(2,1)S(1)}, bf16[16,4096]{1,0:T(8,128)(2,1)S(1)}, u32[]{:S(2)}, u32[]{:S(2)}) collective-permute-start(bf16[16,4096]{1,0:T(8,128)(2,1)S(1)} %finish.1.refs_0_), channel_id=1, source_target_pairs={{0,96},{1,13},{2,98},{3,15},{4,100},{5,1},{6,102},{7,3},{8,104},{9... | collective-permute-start | bytes 393224 | tf_op jit(solution)/shard_map/ppermute | solution.py:32
  88.5 6.2 %collective-permute-start.17 = (bf16[16,4096]{1,0:T(8,128)(2,1)S(1)}, bf16[16,4096]{1,0:T(8,128)(2,1)S(1)}, u32[]{:S(2)}, u32[]{:S(2)}) collective-permute-start(bf16[16,4096]{1,0:T(8,128)(2,1)S(1)} %collective-permute-done.15.refs_1_), channel_id=1, source_target_pairs={{0,32},{1,5},{2,34},{3,7},{4,36},{5,9},{6,38},{7,11},{8,40},{9,13}... | collective-permute-start | bytes 393224 | tf_op jit(solution)/shard_map/ppermute | solution.py:32
  88.5 7.6 %collective-permute-start.16 = (bf16[16,4096]{1,0:T(8,128)(2,1)S(1)}, bf16[16,4096]{1,0:T(8,128)(2,1)S(1)}, u32[]{:S(2)}, u32[]{:S(2)}) collective-permute-start(bf16[16,4096]{1,0:T(8,128)(2,1)S(1)} %collective-permute-done.15.refs_1_), channel_id=1, source_target_pairs={{0,1},{1,0},{2,3},{3,2},{4,5},{5,4},{6,7},{7,6},{8,9},{9,8},{10,11... | collective-permute-start | bytes 393224 | tf_op jit(solution)/shard_map/ppermute | solution.py:32
  94.7 6.4 %collective-permute-start.22 = (bf16[32,4096]{1,0:T(8,128)(2,1)S(1)}, bf16[32,4096]{1,0:T(8,128)(2,1)S(1)}, u32[]{:S(2)}, u32[]{:S(2)}) collective-permute-start(bf16[32,4096]{1,0:T(8,128)(2,1)S(1)} %assemble.3.xb), channel_id=1, source_target_pairs={{0,12},{1,97},{2,14},{3,99},{4,0},{5,101},{6,2},{7,103},{8,4},{9,1... | collective-permute-start | bytes 786440 | tf_op jit(solution)/shard_map/ppermute | solution.py:32
  96.1 7.7 %collective-permute-start.19 = (bf16[32,4096]{1,0:T(8,128)(2,1)S(1)}, bf16[32,4096]{1,0:T(8,128)(2,1)S(1)}, u32[]{:S(2)}, u32[]{:S(2)}) collective-permute-start(bf16[32,4096]{1,0:T(8,128)(2,1)S(1)} %assemble.2.xa), channel_id=1, source_target_pairs={{0,4},{1,33},{2,6},{3,35},{4,8},{5,37},{6,10},{7,39},{8,12},{9,41}... | collective-permute-start | bytes 786440 | tf_op jit(solution)/shard_map/ppermute | solution.py:32
  96.9 7.7 %collective-permute-start.21 = (bf16[32,4096]{1,0:T(8,128)(2,1)S(1)}, bf16[32,4096]{1,0:T(8,128)(2,1)S(1)}, u32[]{:S(2)}, u32[]{:S(2)}) collective-permute-start(bf16[32,4096]{1,0:T(8,128)(2,1)S(1)} %assemble.2.xa), channel_id=1, source_target_pairs={{0,12},{1,97},{2,14},{3,99},{4,0},{5,101},{6,2},{7,103},{8,4},{9,1... | collective-permute-start | bytes 786440 | tf_op jit(solution)/shard_map/ppermute | solution.py:32
  99.4 7.6 %collective-permute-start.20 = (bf16[32,4096]{1,0:T(8,128)(2,1)S(1)}, bf16[32,4096]{1,0:T(8,128)(2,1)S(1)}, u32[]{:S(2)}, u32[]{:S(2)}) collective-permute-start(bf16[32,4096]{1,0:T(8,128)(2,1)S(1)} %assemble.3.xb), channel_id=1, source_target_pairs={{0,4},{1,33},{2,6},{3,35},{4,8},{5,37},{6,10},{7,39},{8,12},{9,41}... | collective-permute-start | bytes 786440 | tf_op jit(solution)/shard_map/ppermute | solution.py:32
  101.1 6.7 %collective-permute-start.24 = (bf16[32,4096]{1,0:T(8,128)(2,1)S(1)}, bf16[32,4096]{1,0:T(8,128)(2,1)S(1)}, u32[]{:S(2)}, u32[]{:S(2)}) collective-permute-start(bf16[32,4096]{1,0:T(8,128)(2,1)S(1)} %collective-permute-done.22.xb), channel_id=1, source_target_pairs={{0,12},{1,97},{2,14},{3,99},{4,0},{5,101},{6,2},{7,103},{8,4},{9,1... | collective-permute-start | bytes 786440 | tf_op jit(solution)/shard_map/ppermute | solution.py:32
  103.7 7.6 %collective-permute-start.23 = (bf16[32,4096]{1,0:T(8,128)(2,1)S(1)}, bf16[32,4096]{1,0:T(8,128)(2,1)S(1)}, u32[]{:S(2)}, u32[]{:S(2)}) collective-permute-start(bf16[32,4096]{1,0:T(8,128)(2,1)S(1)} %collective-permute-done.19.xa), channel_id=1, source_target_pairs={{0,4},{1,33},{2,6},{3,35},{4,8},{5,37},{6,10},{7,39},{8,12},{9,41}... | collective-permute-start | bytes 786440 | tf_op jit(solution)/shard_map/ppermute | solution.py:32
  112.7 1.6 %collective-permute-start.25 = (f32[128,512]{1,0:T(8,128)S(1)}, f32[128,512]{1,0:T(8,128)S(1)}, u32[]{:S(2)}, u32[]{:S(2)}) collective-permute-start(f32[128,512]{1,0:T(8,128)S(1)} %slice.32), channel_id=1, source_target_pairs={{0,1},{1,0},{2,3},{3,2},{4,5},{5,4},{6,7},{7,6},{8,9},{9,8},{10,11... | collective-permute-start | bytes 786440 | tf_op jit(solution)/shard_map/ppermute | solution.py:32
  114.4 4.8 %collective-permute-start.26 = (bf16[64,512]{1,0:T(8,128)(2,1)S(1)}, bf16[64,512]{1,0:T(8,128)(2,1)S(1)}, u32[]{:S(2)}, u32[]{:S(2)}) collective-permute-start(bf16[64,512]{1,0:T(8,128)(2,1)S(1)} %slice.40), channel_id=1, source_target_pairs={{0,2},{1,3},{2,0},{3,1},{4,6},{5,7},{6,4},{7,5},{8,10},{9,11},{10,... | collective-permute-start | bytes 196616 | tf_op jit(solution)/shard_map/ppermute | solution.py:32

commit v4 on v2

--- a/solution.py
+++ b/solution.py
@@ -69,7 +69,8 @@
     lane = lax.broadcasted_iota(jnp.int32, (1, 128), 1)
     slot = lax.broadcasted_iota(jnp.int32, (span, 128), 0)
     for db, kx in enumerate(masked):
-        z, yh, x = source(me, lane >> 4, db, (lane >> 3) & 1)
+        da = ((lane >> 5) & 1) | ((lane >> 3) & 2)
+        z, yh, x = source(me, da, db, (lane >> 3) & 1)
         seen = start + z * 64 + yh * 32 + x * 8 + (lane & 7) + 1 - shard * span
         seen = jnp.minimum(seen, length)
         mask = jnp.where((slot >= seen) & (lane < 64), NEG, 0.0).astype(jnp.bfloat16)
@@ -252,18 +253,18 @@
 def assemble_kernel(*refs, count):
     at = 0
     for x in refs[:count]:
-        refs[-1][at : at + x.shape[0], :] = x[...]
+        refs[-1][at : at + x.shape[0]] = x[...]
         at += x.shape[0]
 
 
 def assemble(pieces, *others):
     vmem = pl.BlockSpec(memory_space=pltpu.VMEM)
-    rows, width = sum(p.shape[0] for p in pieces), pieces[0].shape[1]
+    rows = sum(p.shape[0] for p in pieces)
     return pl.pallas_call(
         functools.partial(assemble_kernel, count=len(pieces)),
         in_specs=[vmem] * len(pieces) + [pl.BlockSpec(memory_space=pl.ANY)] * len(others),
         out_specs=vmem,
-        out_shape=jax.ShapeDtypeStruct((rows, width), pieces[0].dtype),
+        out_shape=jax.ShapeDtypeStruct((rows, *pieces[0].shape[1:]), pieces[0].dtype),
         compiler_params=pltpu.CompilerParams(vmem_limit_bytes=4 * MIB),
         name="assemble",
     )(*pieces, *others)
@@ -327,8 +328,8 @@
     q, k, v, info = together(q, k, v, info)
     vx, kx0, kx1, kx2, kx3 = prepare(info, k, v)
     q2, q1, q3 = (moved(q, a=d) for d in (2, 1, 3))
-    q = jnp.concatenate([q, q1, q2, q3], axis=0)
-    q, vx, kx0, kx1, kx2, kx3 = together(q, vx, kx0, kx1, kx2, kx3)
+    q2, vx, kx0, kx1, kx2, kx3 = together(q2, vx, kx0, kx1, kx2, kx3)
+    q = assemble([q, q2, q1, q3], moved(q2, core=1))
 
     q2, q1, q3 = (moved(q, b=d) for d in (2, 1, 3))
     kvs = tuple(range(nkv))
@@ -349,9 +350,9 @@
     low = combine(4, (own0, 0), (r1, 0), (r2, 0), (r3a, 0))
     q, low = together(q, low)
     own1 = attend(q, kx0, vx, kvs, 4, 4)
-    s1 = moved(low[2:], a=-1)
+    s2 = moved(low[2:], a=-2)
     high = combine(4, (own1, 0), (r1, 4), (r2, 4), (r3b, 0))
-    s2, s3 = moved(high[:2], a=-2), moved(high[2:], a=-3)
+    s1, s3 = moved(high[:2], a=-1), moved(high[2:], a=-3)
     c = combine(2, (low, 0), (s1, 0), (s2, 0), (s3, 0))
     attn = finish(c, moved(c, yh=1))
     x2, x1, x3 = (moved(attn, a=d) for d in (2, 1, 3))

time: 108 us -> 109 us (level)
  starting transfers between devices: 38.1 us -> 41.3 us
  waiting for transfers between devices: 35.2 us -> 32.8 us
    ppermute x27 -> x28, starting transfers between devices: 38.1 us -> 41.3 us  [moved(): return lax.ppermute(x, ('cp', 'tp'), pairs)]
    ppermute x27 -> x28, waiting for transfers between devices: 35.2 us -> 32.8 us  [moved(): return lax.ppermute(x, ('cp', 'tp'), pairs)]
  transfers between devices with their start and end apart: 27 -> 28, of which waited for: 15 -> 17; matrix products, arithmetic and copies ran while one was open for 2% -> 2% of each run, Pallas kernels for 26% -> 26%
where the time goes in v4:
time: 109 us
  starting transfers between devices  41.3 us (38%)
  waiting for transfers between devices  32.8 us (30%)
  Pallas kernels  30.3 us (28%)
  local copies, waits for them, and re-layouts  1.97 us (2%)
  between operations  1.6 us (1%)
    ppermute x28, starting transfers between devices, moved(): return lax.ppermute(x, ('cp', 'tp'), pairs)  41.3 us
    ppermute x28, waiting for transfers between devices, moved(): return lax.ppermute(x, ('cp', 'tp'), pairs)  32.8 us
    pallas_call x6, Pallas kernels, attend(): pl.pallas_call(functools.partial(attend_kernel, kvs=kvs, first=first, nb=...  22.1 us
    pallas_call x3, Pallas kernels, project(): pl.pallas_call(project_kernel, in_specs=[vmem] * 3, out_specs=vmem, out_s...  2.53 us
  transfers between devices with their start and end apart: 28, of which 17 were waited for; matrix products, arithmetic and copies ran while one was open for 2% of the time, Pallas kernels for 26%

profile of v4, /device:TPU:0, one launch (start us, length us, event | category | flops | bytes accessed | tf_op | source)
XLA Modules:
  0.0 108.7 jit_solution(15993665213908362702)
XLA Ops:
  0.0 3.3 %collective-permute-start = (bf16[1,8,32,128]{3,2,1,0:T(8,128)(2,1)}, bf16[1,8,32,128]{3,2,1,0:T(8,128)(2,1)S(1)}, u32[]{:S(2)}, u32[]{:S(2)}) collective-permute-start(bf16[1,8,32,128]{3,2,1,0:T(8,128)(2,1)} %bitcast.10), channel_id=1, source_target_pairs={{0,16},{1,17},{2,18},{3,19},{4,20},{5,21},{6,22},{7,23},{8,24},{9,... | collective-permute-start | bytes 196616 | tf_op jit(solution)/shard_map/ppermute | solution.py:32
  3.3 1.8 %copy_bitcast_fusion = (bf16[2,2048,128]{2,1,0:T(8,128)(2,1)S(1)}, bf16[2,2048,128]{2,1,0:T(8,128)(2,1)S(1)}) fusion(bf16[2048,2,128]{2,1,0:T(2,128)(2,1)} %param.8, bf16[2048,2,128]{2,1,0:T(2,128)(2,1)} %param.7), kind=kLoop, calls=%fused_computation | loop fusion | bytes 4194304 | tf_op jit(solution)/shard_map/transpose | solution.py:325
  6.6 4.0 %collective-permute-start.1 = (bf16[2,8,32,128]{3,2,1,0:T(8,128)(2,1)S(1)}, bf16[2,8,32,128]{3,2,1,0:T(8,128)(2,1)S(1)}, u32[]{:S(2)}, u32[]{:S(2)}) collective-permute-start(bf16[2,8,32,128]{3,2,1,0:T(8,128)(2,1)S(1)} %pad_maximum_fusion.refs_0_), channel_id=1, source_target_pairs={{0,64},{1,9},{2,66},{3,11},{4,68},{5,13},{6,70},{7,15},{8,72},{9,1... | collective-permute-start | bytes 393224 | tf_op jit(solution)/shard_map/ppermute | solution.py:32
  11.5 2.2 %collective-permute-start.3 = (bf16[2,8,32,128]{3,2,1,0:T(8,128)(2,1)S(1)}, bf16[2,8,32,128]{3,2,1,0:T(8,128)(2,1)S(1)}, u32[]{:S(2)}, u32[]{:S(2)}) collective-permute-start(bf16[2,8,32,128]{3,2,1,0:T(8,128)(2,1)S(1)} %pad_maximum_fusion.refs_0_), channel_id=1, source_target_pairs={{0,96},{1,13},{2,98},{3,15},{4,100},{5,1},{6,102},{7,3},{8,104},{9... | collective-permute-start | bytes 393224 | tf_op jit(solution)/shard_map/ppermute | solution.py:32
  13.8 2.2 %prepare.1 = (bf16[2,2048,256]{2,1,0:T(8,128)(2,1)S(1)}, bf16[2,2048,256]{2,1,0:T(8,128)(2,1)S(1)}, bf16[2,2048,256]{2,1,0:T(8,128)(2,1)S(1)}, bf16[2,2048,256]{...) custom-call(s32[7]{0:T(128)S(1)} %concatenate.7.info, bf16[2,2048,128]{2,1,0:T(8,128)(2,1)S(1)} %get-tuple-element.34.k_ref, ...), custom_call_target="tpu_custom_call" | custom-call | tf_op jit(solution)/shard_map/prepare/pallas_call | solution.py:88
  17.4 3.1 %collective-permute-start.7 = (bf16[8,8,32,128]{3,2,1,0:T(8,128)(2,1)S(1)}, bf16[8,8,32,128]{3,2,1,0:T(8,128)(2,1)S(1)}, u32[]{:S(2)}, u32[]{:S(2)}) collective-permute-start(bf16[8,8,32,128]{3,2,1,0:T(8,128)(2,1)S(1)} %assemble.3.q_ref), channel_id=1, source_target_pairs={{0,8},{1,65},{2,10},{3,67},{4,12},{5,69},{6,14},{7,71},{8,0},{9,73... | collective-permute-start | bytes 1572872 | tf_op jit(solution)/shard_map/ppermute | solution.py:32
  21.1 2.6 %collective-permute-start.6 = (bf16[8,8,32,128]{3,2,1,0:T(8,128)(2,1)S(1)}, bf16[8,8,32,128]{3,2,1,0:T(8,128)(2,1)S(1)}, u32[]{:S(2)}, u32[]{:S(2)}) collective-permute-start(bf16[8,8,32,128]{3,2,1,0:T(8,128)(2,1)S(1)} %assemble.3.q_ref), channel_id=1, source_target_pairs={{0,12},{1,97},{2,14},{3,99},{4,0},{5,101},{6,2},{7,103},{8,4},{9,1... | collective-permute-start | bytes 1572872 | tf_op jit(solution)/shard_map/ppermute | solution.py:32
  23.7 2.8 %attend_plane.6.refs_0_ = bf16[4,272,128]{2,1,0:T(8,128)(2,1)S(1)} custom-call(bf16[8,8,32,128]{3,2,1,0:T(8,128)(2,1)S(1)} %assemble.3.q_ref, bf16[2,2048,256]{2,1,0:T(8,128)(2,1)S(1)} %get-tuple-element.42.kx, bf16[2,2048,256]{2,1,0:T(8,128)(2,1)S(1)} %get-tuple-element.43.vx), custom_call_target="tpu_custom_call" | custom-call | flops 2147483648 | bytes 4194304 | tf_op jit(solution)/shard_map/attend_plane/pallas_call | solution.py:169
  26.5 1.8 %collective-permute-done.7.q_ref = bf16[8,8,32,128]{3,2,1,0:T(8,128)(2,1)S(1)} collective-permute-done((bf16[8,8,32,128]{3,2,1,0:T(8,128)(2,1)S(1)}, bf16[8,8,32,128]{3,2,1,0:T(8,128)(2,1)S(1)}, u32[]{:S(2)}, u32[]{:S(2)}) %collective-permute-start.7) | collective-permute-done | bytes 524320 | tf_op jit(solution)/shard_map/ppermute | solution.py:32
  28.3 5.5 %attend_plane.7 = bf16[8,272,128]{2,1,0:T(8,128)(2,1)S(1)} custom-call(bf16[8,8,32,128]{3,2,1,0:T(8,128)(2,1)S(1)} %collective-permute-done.7.q_ref, bf16[2,2048,256]{2,1,0:T(8,128)(2,1)S(1)} %get-tuple-element.45.kx, bf16[2,2048,256]{2,1,0:T(8,128)(2,1)S(1)} %get-tuple-element.43.vx), custom_call_target="tpu_custom_call" | custom-call | flops 4294967296 | bytes 4194304 | tf_op jit(solution)/shard_map/attend_plane/pallas_call | solution.py:169
  33.8 3.3 %collective-permute-start.8 = (bf16[8,272,128]{2,1,0:T(8,128)(2,1)S(1)}, bf16[8,272,128]{2,1,0:T(8,128)(2,1)S(1)}, u32[]{:S(2)}, u32[]{:S(2)}) collective-permute-start(bf16[8,272,128]{2,1,0:T(8,128)(2,1)S(1)} %attend_plane.7), channel_id=1, source_target_pairs={{0,8},{1,65},{2,10},{3,67},{4,12},{5,69},{6,14},{7,71},{8,0},{9,73... | collective-permute-start | bytes 1671176 | tf_op jit(solution)/shard_map/ppermute | solution.py:32
  37.1 5.5 %attend_plane.8 = bf16[8,272,128]{2,1,0:T(8,128)(2,1)S(1)} custom-call(bf16[8,8,32,128]{3,2,1,0:T(8,128)(2,1)S(1)} %collective-permute-done.5.q_ref, bf16[2,2048,256]{2,1,0:T(8,128)(2,1)S(1)} %get-tuple-element.48.kx, bf16[2,2048,256]{2,1,0:T(8,128)(2,1)S(1)} %get-tuple-element.43.vx), custom_call_target="tpu_custom_call" | custom-call | flops 4294967296 | bytes 4194304 | tf_op jit(solution)/shard_map/attend_plane/pallas_call | solution.py:169
  43.9 2.8 %attend_plane.9 = bf16[4,272,128]{2,1,0:T(8,128)(2,1)S(1)} custom-call(bf16[8,8,32,128]{3,2,1,0:T(8,128)(2,1)S(1)} %collective-permute-done.6.q_ref, bf16[2,2048,256]{2,1,0:T(8,128)(2,1)S(1)} %get-tuple-element.50.kx, bf16[2,2048,256]{2,1,0:T(8,128)(2,1)S(1)} %get-tuple-element.43.vx), custom_call_target="tpu_custom_call" | custom-call | flops 2147483648 | bytes 4194304 | tf_op jit(solution)/shard_map/attend_plane/pallas_call | solution.py:169
  47.6 2.8 %attend_plane.10 = bf16[4,272,128]{2,1,0:T(8,128)(2,1)S(1)} custom-call(bf16[8,8,32,128]{3,2,1,0:T(8,128)(2,1)S(1)} %collective-permute-done.6.q_ref, bf16[2,2048,256]{2,1,0:T(8,128)(2,1)S(1)} %get-tuple-element.50.kx, bf16[2,2048,256]{2,1,0:T(8,128)(2,1)S(1)} %get-tuple-element.43.vx), custom_call_target="tpu_custom_call" | custom-call | flops 2147483648 | bytes 4194304 | tf_op jit(solution)/shard_map/attend_plane/pallas_call | solution.py:169
  51.0 3.4 %collective-permute-done.10.refs_3_ = bf16[4,272,128]{2,1,0:T(8,128)(2,1)S(1)} collective-permute-done((bf16[4,272,128]{2,1,0:T(8,128)(2,1)S(1)}, bf16[4,272,128]{2,1,0:T(8,128)(2,1)S(1)}, u32[]{:S(2)}, u32[]{:S(2)}) %collective-permute-start.10) | collective-permute-done | bytes 278560 | tf_op jit(solution)/shard_map/ppermute | solution.py:32
  55.2 1.4 %collective-permute-start.13 = (bf16[2,272,128]{2,1,0:T(8,128)(2,1)S(1)}, bf16[2,272,128]{2,1,0:T(8,128)(2,1)S(1)}, u32[]{:S(2)}, u32[]{:S(2)}) collective-permute-start(bf16[2,272,128]{2,1,0:T(8,128)(2,1)S(1)} %slice.23), channel_id=1, source_target_pairs={{0,64},{1,9},{2,66},{3,11},{4,68},{5,13},{6,70},{7,15},{8,72},{9,1... | collective-permute-start | bytes 417800 | tf_op jit(solution)/shard_map/ppermute | solution.py:32
  56.6 2.8 %attend_plane.11.refs_0_ = bf16[4,272,128]{2,1,0:T(8,128)(2,1)S(1)} custom-call(bf16[8,8,32,128]{3,2,1,0:T(8,128)(2,1)S(1)} %assemble.3.q_ref, bf16[2,2048,256]{2,1,0:T(8,128)(2,1)S(1)} %get-tuple-element.42.kx, bf16[2,2048,256]{2,1,0:T(8,128)(2,1)S(1)} %get-tuple-element.43.vx), custom_call_target="tpu_custom_call" | custom-call | flops 2147483648 | bytes 4194304 | tf_op jit(solution)/shard_map/attend_plane/pallas_call | solution.py:169
  60.4 2.7 %collective-permute-start.12 = (bf16[2,272,128]{2,1,0:T(8,128)(2,1)S(1)}, bf16[2,272,128]{2,1,0:T(8,128)(2,1)S(1)}, u32[]{:S(2)}, u32[]{:S(2)}) collective-permute-start(bf16[2,272,128]{2,1,0:T(8,128)(2,1)S(1)} %get-tuple-element.60), channel_id=1, source_target_pairs={{0,96},{1,13},{2,98},{3,15},{4,100},{5,1},{6,102},{7,3},{8,104},{9... | collective-permute-start | bytes 417800 | tf_op jit(solution)/shard_map/ppermute | solution.py:32
  64.0 3.0 %collective-permute-done.12.refs_1_ = bf16[2,272,128]{2,1,0:T(8,128)(2,1)S(1)} collective-permute-done((bf16[2,272,128]{2,1,0:T(8,128)(2,1)S(1)}, bf16[2,272,128]{2,1,0:T(8,128)(2,1)S(1)}, u32[]{:S(2)}, u32[]{:S(2)}) %collective-permute-start.12) | collective-permute-done | bytes 139296 | tf_op jit(solution)/shard_map/ppermute | solution.py:32
  67.0 2.4 %collective-permute-done.14.refs_3_ = bf16[2,272,128]{2,1,0:T(8,128)(2,1)S(1)} collective-permute-done((bf16[2,272,128]{2,1,0:T(8,128)(2,1)S(1)}, bf16[2,272,128]{2,1,0:T(8,128)(2,1)S(1)}, u32[]{:S(2)}, u32[]{:S(2)}) %collective-permute-start.14) | collective-permute-done | bytes 139296 | tf_op jit(solution)/shard_map/ppermute | solution.py:32
  69.8 2.8 %collective-permute-start.15 = (bf16[2,272,128]{2,1,0:T(8,128)(2,1)S(1)}, bf16[2,272,128]{2,1,0:T(8,128)(2,1)S(1)}, u32[]{:S(2)}, u32[]{:S(2)}) collective-permute-start(bf16[2,272,128]{2,1,0:T(8,128)(2,1)S(1)} %combine.5.mine), channel_id=1, source_target_pairs={{0,16},{1,17},{2,18},{3,19},{4,20},{5,21},{6,22},{7,23},{8,24},{9,... | collective-permute-start | bytes 417800 | tf_op jit(solution)/shard_map/ppermute | solution.py:32
  72.6 3.8 %collective-permute-done.15.theirs = bf16[2,272,128]{2,1,0:T(8,128)(2,1)S(1)} collective-permute-done((bf16[2,272,128]{2,1,0:T(8,128)(2,1)S(1)}, bf16[2,272,128]{2,1,0:T(8,128)(2,1)S(1)}, u32[]{:S(2)}, u32[]{:S(2)}) %collective-permute-start.15) | collective-permute-done | bytes 139296 | tf_op jit(solution)/shard_map/ppermute | solution.py:32
  76.7 1.8 %collective-permute-start.17 = (bf16[16,4096]{1,0:T(8,128)(2,1)S(1)}, bf16[16,4096]{1,0:T(8,128)(2,1)S(1)}, u32[]{:S(2)}, u32[]{:S(2)}) collective-permute-start(bf16[16,4096]{1,0:T(8,128)(2,1)S(1)} %finish.1.refs_0_), channel_id=1, source_target_pairs={{0,64},{1,9},{2,66},{3,11},{4,68},{5,13},{6,70},{7,15},{8,72},{9,1... | collective-permute-start | bytes 393224 | tf_op jit(solution)/shard_map/ppermute | solution.py:32
  80.5 2.7 %collective-permute-done.17.refs_0_ = bf16[16,4096]{1,0:T(8,128)(2,1)S(1)} collective-permute-done((bf16[16,4096]{1,0:T(8,128)(2,1)S(1)}, bf16[16,4096]{1,0:T(8,128)(2,1)S(1)}, u32[]{:S(2)}, u32[]{:S(2)}) %collective-permute-start.17) | collective-permute-done | bytes 131104 | tf_op jit(solution)/shard_map/ppermute | solution.py:32
  83.6 1.8 %collective-permute-done.16.refs_1_ = bf16[16,4096]{1,0:T(8,128)(2,1)S(1)} collective-permute-done((bf16[16,4096]{1,0:T(8,128)(2,1)S(1)}, bf16[16,4096]{1,0:T(8,128)(2,1)S(1)}, u32[]{:S(2)}, u32[]{:S(2)}) %collective-permute-start.16) | collective-permute-done | bytes 131104 | tf_op jit(solution)/shard_map/ppermute | solution.py:32
  85.7 3.0 %collective-permute-start.22 = (bf16[32,4096]{1,0:T(8,128)(2,1)S(1)}, bf16[32,4096]{1,0:T(8,128)(2,1)S(1)}, u32[]{:S(2)}, u32[]{:S(2)}) collective-permute-start(bf16[32,4096]{1,0:T(8,128)(2,1)S(1)} %assemble.4.xa), channel_id=1, source_target_pairs={{0,12},{1,97},{2,14},{3,99},{4,0},{5,101},{6,2},{7,103},{8,4},{9,1... | collective-permute-start | bytes 786440 | tf_op jit(solution)/shard_map/ppermute | solution.py:32
  89.9 2.0 %collective-permute-start.25 = (bf16[32,4096]{1,0:T(8,128)(2,1)S(1)}, bf16[32,4096]{1,0:T(8,128)(2,1)S(1)}, u32[]{:S(2)}, u32[]{:S(2)}) collective-permute-start(bf16[32,4096]{1,0:T(8,128)(2,1)S(1)} %collective-permute-done.23.xb), channel_id=1, source_target_pairs={{0,12},{1,97},{2,14},{3,99},{4,0},{5,101},{6,2},{7,103},{8,4},{9,1... | collective-permute-start | bytes 786440 | tf_op jit(solution)/shard_map/ppermute | solution.py:32
  94.8 1.5 %collective-permute-done.21.xb = bf16[32,4096]{1,0:T(8,128)(2,1)S(1)} collective-permute-done((bf16[32,4096]{1,0:T(8,128)(2,1)S(1)}, bf16[32,4096]{1,0:T(8,128)(2,1)S(1)}, u32[]{:S(2)}, u32[]{:S(2)}) %collective-permute-start.21) | collective-permute-done | bytes 262176 | tf_op jit(solution)/shard_map/ppermute | solution.py:32
  97.2 3.5 %collective-permute-done.24.xa = bf16[32,4096]{1,0:T(8,128)(2,1)S(1)} collective-permute-done((bf16[32,4096]{1,0:T(8,128)(2,1)S(1)}, bf16[32,4096]{1,0:T(8,128)(2,1)S(1)}, u32[]{:S(2)}, u32[]{:S(2)}) %collective-permute-start.24) | collective-permute-done | bytes 262176 | tf_op jit(solution)/shard_map/ppermute | solution.py:32
  100.6 1.4 %place.1 = f32[256,512]{1,0:T(8,128)S(1)} custom-call(s32[7]{0:T(128)S(1)} %concatenate.7.info, f32[64,512]{1,0:T(8,128)S(1)} %project.3.y0, f32[64,512]{1,0:T(8,128)S(1)} %project.4.y1, f32[64,512]{1,0:T(8,128)S(1)} %project.5.y3, bf16[32,4096]{1,0:T(8,128)(2,1)S(1)} %collective-permute-done.24.xa, bf16[32,4096]{1,0:T(8,128)(2,1)S(1)} %collective-permute-done.25.xb, ...), custom_call_target="tpu_custom_call" | custom-call | tf_op jit(solution)/shard_map/place/pallas_call | solution.py:310
  102.1 1.5 %collective-permute-done.26 = f32[128,512]{1,0:T(8,128)S(1)} collective-permute-done((f32[128,512]{1,0:T(8,128)S(1)}, f32[128,512]{1,0:T(8,128)S(1)}, u32[]{:S(2)}, u32[]{:S(2)}) %collective-permute-start.26) | collective-permute-done | bytes 262176 | tf_op jit(solution)/shard_map/ppermute | solution.py:32
  104.9 3.2 %collective-permute-done.27 = bf16[64,512]{1,0:T(8,128)(2,1)S(1)} collective-permute-done((bf16[64,512]{1,0:T(8,128)(2,1)S(1)}, bf16[64,512]{1,0:T(8,128)(2,1)S(1)}, u32[]{:S(2)}, u32[]{:S(2)}) %collective-permute-start.27) | collective-permute-done | bytes 65568 | tf_op jit(solution)/shard_map/ppermute | solution.py:32
  (55 shorter events, 18.8 us)
Async XLA Ops:
  0.0 6.5 %copy-start.1 = (bf16[8,32,128]{2,1,0:T(8,128)(2,1)S(1)}, bf16[8,32,128]{2,1,0:T(8,128)(2,1)}, u32[]{:S(2)}) copy-start(bf16[8,32,128]{2,1,0:T(8,128)(2,1)} %param.6) | copy-start | bytes 196612
  0.0 6.5 %collective-permute-start = (bf16[1,8,32,128]{3,2,1,0:T(8,128)(2,1)}, bf16[1,8,32,128]{3,2,1,0:T(8,128)(2,1)S(1)}, u32[]{:S(2)}, u32[]{:S(2)}) collective-permute-start(bf16[1,8,32,128]{3,2,1,0:T(8,128)(2,1)} %bitcast.10), channel_id=1, source_target_pairs={{0,16},{1,17},{2,18},{3,19},{4,20},{5,21},{6,22},{7,23},{8,24},{9,... | collective-permute-start | bytes 196616 | tf_op jit(solution)/shard_map/ppermute | solution.py:32
  6.6 9.4 %collective-permute-start.1 = (bf16[2,8,32,128]{3,2,1,0:T(8,128)(2,1)S(1)}, bf16[2,8,32,128]{3,2,1,0:T(8,128)(2,1)S(1)}, u32[]{:S(2)}, u32[]{:S(2)}) collective-permute-start(bf16[2,8,32,128]{3,2,1,0:T(8,128)(2,1)S(1)} %pad_maximum_fusion.refs_0_), channel_id=1, source_target_pairs={{0,64},{1,9},{2,66},{3,11},{4,68},{5,13},{6,70},{7,15},{8,72},{9,1... | collective-permute-start | bytes 393224 | tf_op jit(solution)/shard_map/ppermute | solution.py:32
  10.5 6.2 %collective-permute-start.2 = (bf16[2,8,32,128]{3,2,1,0:T(8,128)(2,1)S(1)}, bf16[2,8,32,128]{3,2,1,0:T(8,128)(2,1)S(1)}, u32[]{:S(2)}, u32[]{:S(2)}) collective-permute-start(bf16[2,8,32,128]{3,2,1,0:T(8,128)(2,1)S(1)} %pad_maximum_fusion.refs_0_), channel_id=1, source_target_pairs={{0,32},{1,5},{2,34},{3,7},{4,36},{5,9},{6,38},{7,11},{8,40},{9,13}... | collective-permute-start | bytes 393224 | tf_op jit(solution)/shard_map/ppermute | solution.py:32
  11.5 5.2 %collective-permute-start.3 = (bf16[2,8,32,128]{3,2,1,0:T(8,128)(2,1)S(1)}, bf16[2,8,32,128]{3,2,1,0:T(8,128)(2,1)S(1)}, u32[]{:S(2)}, u32[]{:S(2)}) collective-permute-start(bf16[2,8,32,128]{3,2,1,0:T(8,128)(2,1)S(1)} %pad_maximum_fusion.refs_0_), channel_id=1, source_target_pairs={{0,96},{1,13},{2,98},{3,15},{4,100},{5,1},{6,102},{7,3},{8,104},{9... | collective-permute-start | bytes 393224 | tf_op jit(solution)/shard_map/ppermute | solution.py:32
  15.9 1.4 %collective-permute-start.4 = (bf16[2,8,32,128]{3,2,1,0:T(8,128)(2,1)S(1)}, bf16[2,8,32,128]{3,2,1,0:T(8,128)(2,1)S(1)}, u32[]{:S(2)}, u32[]{:S(2)}) collective-permute-start(bf16[2,8,32,128]{3,2,1,0:T(8,128)(2,1)S(1)} %collective-permute-done.1.refs_1_), channel_id=1, source_target_pairs={{0,1},{1,0},{2,3},{3,2},{4,5},{5,4},{6,7},{7,6},{8,9},{9,8},{10,11... | collective-permute-start | bytes 393224 | tf_op jit(solution)/shard_map/ppermute | solution.py:32
  17.4 10.9 %collective-permute-start.7 = (bf16[8,8,32,128]{3,2,1,0:T(8,128)(2,1)S(1)}, bf16[8,8,32,128]{3,2,1,0:T(8,128)(2,1)S(1)}, u32[]{:S(2)}, u32[]{:S(2)}) collective-permute-start(bf16[8,8,32,128]{3,2,1,0:T(8,128)(2,1)S(1)} %assemble.3.q_ref), channel_id=1, source_target_pairs={{0,8},{1,65},{2,10},{3,67},{4,12},{5,69},{6,14},{7,71},{8,0},{9,73... | collective-permute-start | bytes 1572872 | tf_op jit(solution)/shard_map/ppermute | solution.py:32
  20.5 16.6 %collective-permute-start.5 = (bf16[8,8,32,128]{3,2,1,0:T(8,128)(2,1)S(1)}, bf16[8,8,32,128]{3,2,1,0:T(8,128)(2,1)S(1)}, u32[]{:S(2)}, u32[]{:S(2)}) collective-permute-start(bf16[8,8,32,128]{3,2,1,0:T(8,128)(2,1)S(1)} %assemble.3.q_ref), channel_id=1, source_target_pairs={{0,4},{1,33},{2,6},{3,35},{4,8},{5,37},{6,10},{7,39},{8,12},{9,41}... | collective-permute-start | bytes 1572872 | tf_op jit(solution)/shard_map/ppermute | solution.py:32
  21.1 16.0 %collective-permute-start.6 = (bf16[8,8,32,128]{3,2,1,0:T(8,128)(2,1)S(1)}, bf16[8,8,32,128]{3,2,1,0:T(8,128)(2,1)S(1)}, u32[]{:S(2)}, u32[]{:S(2)}) collective-permute-start(bf16[8,8,32,128]{3,2,1,0:T(8,128)(2,1)S(1)} %assemble.3.q_ref), channel_id=1, source_target_pairs={{0,12},{1,97},{2,14},{3,99},{4,0},{5,101},{6,2},{7,103},{8,4},{9,1... | collective-permute-start | bytes 1572872 | tf_op jit(solution)/shard_map/ppermute | solution.py:32
  33.8 13.8 %collective-permute-start.8 = (bf16[8,272,128]{2,1,0:T(8,128)(2,1)S(1)}, bf16[8,272,128]{2,1,0:T(8,128)(2,1)S(1)}, u32[]{:S(2)}, u32[]{:S(2)}) collective-permute-start(bf16[8,272,128]{2,1,0:T(8,128)(2,1)S(1)} %attend_plane.7), channel_id=1, source_target_pairs={{0,8},{1,65},{2,10},{3,67},{4,12},{5,69},{6,14},{7,71},{8,0},{9,73... | collective-permute-start | bytes 1671176 | tf_op jit(solution)/shard_map/ppermute | solution.py:32
  42.7 11.8 %collective-permute-start.9 = (bf16[8,272,128]{2,1,0:T(8,128)(2,1)S(1)}, bf16[8,272,128]{2,1,0:T(8,128)(2,1)S(1)}, u32[]{:S(2)}, u32[]{:S(2)}) collective-permute-start(bf16[8,272,128]{2,1,0:T(8,128)(2,1)S(1)} %attend_plane.8), channel_id=1, source_target_pairs={{0,12},{1,97},{2,14},{3,99},{4,0},{5,101},{6,2},{7,103},{8,4},{9,1... | collective-permute-start | bytes 1671176 | tf_op jit(solution)/shard_map/ppermute | solution.py:32
  46.6 7.8 %collective-permute-start.10 = (bf16[4,272,128]{2,1,0:T(8,128)(2,1)S(1)}, bf16[4,272,128]{2,1,0:T(8,128)(2,1)S(1)}, u32[]{:S(2)}, u32[]{:S(2)}) collective-permute-start(bf16[4,272,128]{2,1,0:T(8,128)(2,1)S(1)} %attend_plane.9), channel_id=1, source_target_pairs={{0,4},{1,33},{2,6},{3,35},{4,8},{5,37},{6,10},{7,39},{8,12},{9,41}... | collective-permute-start | bytes 835592 | tf_op jit(solution)/shard_map/ppermute | solution.py:32
  50.4 9.3 %collective-permute-start.11 = (bf16[4,272,128]{2,1,0:T(8,128)(2,1)S(1)}, bf16[4,272,128]{2,1,0:T(8,128)(2,1)S(1)}, u32[]{:S(2)}, u32[]{:S(2)}) collective-permute-start(bf16[4,272,128]{2,1,0:T(8,128)(2,1)S(1)} %attend_plane.10), channel_id=1, source_target_pairs={{0,4},{1,33},{2,6},{3,35},{4,8},{5,37},{6,10},{7,39},{8,12},{9,41}... | collective-permute-start | bytes 835592 | tf_op jit(solution)/shard_map/ppermute | solution.py:32
  55.2 8.9 %collective-permute-start.13 = (bf16[2,272,128]{2,1,0:T(8,128)(2,1)S(1)}, bf16[2,272,128]{2,1,0:T(8,128)(2,1)S(1)}, u32[]{:S(2)}, u32[]{:S(2)}) collective-permute-start(bf16[2,272,128]{2,1,0:T(8,128)(2,1)S(1)} %slice.23), channel_id=1, source_target_pairs={{0,64},{1,9},{2,66},{3,11},{4,68},{5,13},{6,70},{7,15},{8,72},{9,1... | collective-permute-start | bytes 417800 | tf_op jit(solution)/shard_map/ppermute | solution.py:32
  59.3 33.7 %copy-start = (bf16[4096,512]{1,0:T(8,128)(2,1)S(1)}, bf16[4096,512]{1,0:T(8,128)(2,1)}, u32[]{:S(2)}) copy-start(bf16[4096,512]{1,0:T(8,128)(2,1)} %w_ref.7) | copy-start | bytes 12582916
  60.4 6.6 %collective-permute-start.12 = (bf16[2,272,128]{2,1,0:T(8,128)(2,1)S(1)}, bf16[2,272,128]{2,1,0:T(8,128)(2,1)S(1)}, u32[]{:S(2)}, u32[]{:S(2)}) collective-permute-start(bf16[2,272,128]{2,1,0:T(8,128)(2,1)S(1)} %get-tuple-element.60), channel_id=1, source_target_pairs={{0,96},{1,13},{2,98},{3,15},{4,100},{5,1},{6,102},{7,3},{8,104},{9... | collective-permute-start | bytes 417800 | tf_op jit(solution)/shard_map/ppermute | solution.py:32
  63.1 6.3 %collective-permute-start.14 = (bf16[2,272,128]{2,1,0:T(8,128)(2,1)S(1)}, bf16[2,272,128]{2,1,0:T(8,128)(2,1)S(1)}, u32[]{:S(2)}, u32[]{:S(2)}) collective-permute-start(bf16[2,272,128]{2,1,0:T(8,128)(2,1)S(1)} %get-tuple-element.59), channel_id=1, source_target_pairs={{0,32},{1,5},{2,34},{3,7},{4,36},{5,9},{6,38},{7,11},{8,40},{9,13}... | collective-permute-start | bytes 417800 | tf_op jit(solution)/shard_map/ppermute | solution.py:32
  69.8 6.6 %collective-permute-start.15 = (bf16[2,272,128]{2,1,0:T(8,128)(2,1)S(1)}, bf16[2,272,128]{2,1,0:T(8,128)(2,1)S(1)}, u32[]{:S(2)}, u32[]{:S(2)}) collective-permute-start(bf16[2,272,128]{2,1,0:T(8,128)(2,1)S(1)} %combine.5.mine), channel_id=1, source_target_pairs={{0,16},{1,17},{2,18},{3,19},{4,20},{5,21},{6,22},{7,23},{8,24},{9,... | collective-permute-start | bytes 417800 | tf_op jit(solution)/shard_map/ppermute | solution.py:32
  76.7 6.6 %collective-permute-start.17 = (bf16[16,4096]{1,0:T(8,128)(2,1)S(1)}, bf16[16,4096]{1,0:T(8,128)(2,1)S(1)}, u32[]{:S(2)}, u32[]{:S(2)}) collective-permute-start(bf16[16,4096]{1,0:T(8,128)(2,1)S(1)} %finish.1.refs_0_), channel_id=1, source_target_pairs={{0,64},{1,9},{2,66},{3,11},{4,68},{5,13},{6,70},{7,15},{8,72},{9,1... | collective-permute-start | bytes 393224 | tf_op jit(solution)/shard_map/ppermute | solution.py:32
  78.5 5.0 %collective-permute-start.19 = (bf16[16,4096]{1,0:T(8,128)(2,1)S(1)}, bf16[16,4096]{1,0:T(8,128)(2,1)S(1)}, u32[]{:S(2)}, u32[]{:S(2)}) collective-permute-start(bf16[16,4096]{1,0:T(8,128)(2,1)S(1)} %finish.1.refs_0_), channel_id=1, source_target_pairs={{0,96},{1,13},{2,98},{3,15},{4,100},{5,1},{6,102},{7,3},{8,104},{9... | collective-permute-start | bytes 393224 | tf_op jit(solution)/shard_map/ppermute | solution.py:32
  79.2 6.2 %collective-permute-start.16 = (bf16[16,4096]{1,0:T(8,128)(2,1)S(1)}, bf16[16,4096]{1,0:T(8,128)(2,1)S(1)}, u32[]{:S(2)}, u32[]{:S(2)}) collective-permute-start(bf16[16,4096]{1,0:T(8,128)(2,1)S(1)} %finish.1.refs_0_), channel_id=1, source_target_pairs={{0,32},{1,5},{2,34},{3,7},{4,36},{5,9},{6,38},{7,11},{8,40},{9,13}... | collective-permute-start | bytes 393224 | tf_op jit(solution)/shard_map/ppermute | solution.py:32
  83.3 2.1 %collective-permute-start.18 = (bf16[16,4096]{1,0:T(8,128)(2,1)S(1)}, bf16[16,4096]{1,0:T(8,128)(2,1)S(1)}, u32[]{:S(2)}, u32[]{:S(2)}) collective-permute-start(bf16[16,4096]{1,0:T(8,128)(2,1)S(1)} %collective-permute-done.17.refs_0_), channel_id=1, source_target_pairs={{0,1},{1,0},{2,3},{3,2},{4,5},{5,4},{6,7},{7,6},{8,9},{9,8},{10,11... | collective-permute-start | bytes 393224 | tf_op jit(solution)/shard_map/ppermute | solution.py:32
  83.5 6.4 %collective-permute-start.23 = (bf16[32,4096]{1,0:T(8,128)(2,1)S(1)}, bf16[32,4096]{1,0:T(8,128)(2,1)S(1)}, u32[]{:S(2)}, u32[]{:S(2)}) collective-permute-start(bf16[32,4096]{1,0:T(8,128)(2,1)S(1)} %assemble.5.xb), channel_id=1, source_target_pairs={{0,12},{1,97},{2,14},{3,99},{4,0},{5,101},{6,2},{7,103},{8,4},{9,1... | collective-permute-start | bytes 786440 | tf_op jit(solution)/shard_map/ppermute | solution.py:32
  85.4 7.7 %collective-permute-start.20 = (bf16[32,4096]{1,0:T(8,128)(2,1)S(1)}, bf16[32,4096]{1,0:T(8,128)(2,1)S(1)}, u32[]{:S(2)}, u32[]{:S(2)}) collective-permute-start(bf16[32,4096]{1,0:T(8,128)(2,1)S(1)} %assemble.4.xa), channel_id=1, source_target_pairs={{0,4},{1,33},{2,6},{3,35},{4,8},{5,37},{6,10},{7,39},{8,12},{9,41}... | collective-permute-start | bytes 786440 | tf_op jit(solution)/shard_map/ppermute | solution.py:32
  85.7 8.2 %collective-permute-start.22 = (bf16[32,4096]{1,0:T(8,128)(2,1)S(1)}, bf16[32,4096]{1,0:T(8,128)(2,1)S(1)}, u32[]{:S(2)}, u32[]{:S(2)}) collective-permute-start(bf16[32,4096]{1,0:T(8,128)(2,1)S(1)} %assemble.4.xa), channel_id=1, source_target_pairs={{0,12},{1,97},{2,14},{3,99},{4,0},{5,101},{6,2},{7,103},{8,4},{9,1... | collective-permute-start | bytes 786440 | tf_op jit(solution)/shard_map/ppermute | solution.py:32
  88.7 7.6 %collective-permute-start.21 = (bf16[32,4096]{1,0:T(8,128)(2,1)S(1)}, bf16[32,4096]{1,0:T(8,128)(2,1)S(1)}, u32[]{:S(2)}, u32[]{:S(2)}) collective-permute-start(bf16[32,4096]{1,0:T(8,128)(2,1)S(1)} %assemble.5.xb), channel_id=1, source_target_pairs={{0,4},{1,33},{2,6},{3,35},{4,8},{5,37},{6,10},{7,39},{8,12},{9,41}... | collective-permute-start | bytes 786440 | tf_op jit(solution)/shard_map/ppermute | solution.py:32
  89.9 7.2 %collective-permute-start.25 = (bf16[32,4096]{1,0:T(8,128)(2,1)S(1)}, bf16[32,4096]{1,0:T(8,128)(2,1)S(1)}, u32[]{:S(2)}, u32[]{:S(2)}) collective-permute-start(bf16[32,4096]{1,0:T(8,128)(2,1)S(1)} %collective-permute-done.23.xb), channel_id=1, source_target_pairs={{0,12},{1,97},{2,14},{3,99},{4,0},{5,101},{6,2},{7,103},{8,4},{9,1... | collective-permute-start | bytes 786440 | tf_op jit(solution)/shard_map/ppermute | solution.py:32
  93.1 7.6 %collective-permute-start.24 = (bf16[32,4096]{1,0:T(8,128)(2,1)S(1)}, bf16[32,4096]{1,0:T(8,128)(2,1)S(1)}, u32[]{:S(2)}, u32[]{:S(2)}) collective-permute-start(bf16[32,4096]{1,0:T(8,128)(2,1)S(1)} %collective-permute-done.20.xa), channel_id=1, source_target_pairs={{0,4},{1,33},{2,6},{3,35},{4,8},{5,37},{6,10},{7,39},{8,12},{9,41}... | collective-permute-start | bytes 786440 | tf_op jit(solution)/shard_map/ppermute | solution.py:32
  102.1 1.6 %collective-permute-start.26 = (f32[128,512]{1,0:T(8,128)S(1)}, f32[128,512]{1,0:T(8,128)S(1)}, u32[]{:S(2)}, u32[]{:S(2)}) collective-permute-start(f32[128,512]{1,0:T(8,128)S(1)} %slice.32), channel_id=1, source_target_pairs={{0,1},{1,0},{2,3},{3,2},{4,5},{5,4},{6,7},{7,6},{8,9},{9,8},{10,11... | collective-permute-start | bytes 786440 | tf_op jit(solution)/shard_map/ppermute | solution.py:32
  103.7 4.3 %collective-permute-start.27 = (bf16[64,512]{1,0:T(8,128)(2,1)S(1)}, bf16[64,512]{1,0:T(8,128)(2,1)S(1)}, u32[]{:S(2)}, u32[]{:S(2)}) collective-permute-start(bf16[64,512]{1,0:T(8,128)(2,1)S(1)} %slice.40), channel_id=1, source_target_pairs={{0,2},{1,3},{2,0},{3,1},{4,6},{5,7},{6,4},{7,5},{8,10},{9,11},{10,... | collective-permute-start | bytes 196616 | tf_op jit(solution)/shard_map/ppermute | solution.py:32
